TPU v7x, 32 devices: a whole 2x2x4 slice. The times are simulated.
32 devices in a mesh: edge: 8 (over z, y), rep: 4 (over x, core).
Axes of the slice: x: 2, y: 2, z: 4, core: 2. Of those that a mesh axis runs over, the one named last changes fastest.
Arguments:
- atom_features: bfloat16 [4, 8192, 256], P('rep', 'edge'), may hold values from -6 to 6
- distances: float32 [4, 131072], P('rep', 'edge'), may hold values from 0.5 to 6
- source_index: int32 [4, 131072], P('rep', 'edge'), may hold values from 0 to 1023
- slot_index: int32 [4, 8192, 16], P('rep', 'edge'), may hold values from 0 to 16383, as said below
- live_mask: int32 [4, 8192, 16], P('rep', 'edge'), may hold values from 0 to 1, as said below
- output_cot: bfloat16 [4, 8192, 256], P('rep', 'edge'), may hold values from -6 to 6
- energy_cot: float32 [4, 8192], P('rep', 'edge'), may hold values from -6 to 6
- attention_weight: float32 [256, 768], P(None, 'edge'), may hold values from -0.375 to 0.375
- attention_first: float32 [256, 768], P(None, 'edge'), may hold values from -320 to 320
- attention_second: float32 [256, 768], P(None, 'edge'), may hold values from 2949.12 to 11796.48
- output_weight: float32 [256, 256], P(None, 'edge'), may hold values from -1.5 to 1.5
- output_first: float32 [256, 256], P(None, 'edge'), may hold values from -512 to 512
- output_second: float32 [256, 256], P(None, 'edge'), may hold values from 8192 to 32768
- gateup_weight: float32 [256, 2048], P(None, 'edge'), may hold values from -0.375 to 0.375
- gateup_first: float32 [256, 2048], P(None, 'edge'), may hold values from -448 to 448
- gateup_second: float32 [256, 2048], P(None, 'edge'), may hold values from 5242.88 to 20971.52
- down_weight: float32 [1024, 256], P(None, 'edge'), may hold values from -0.1875 to 0.1875
- down_first: float32 [1024, 256], P(None, 'edge'), may hold values from -896 to 896
- down_second: float32 [1024, 256], P(None, 'edge'), may hold values from 20971.52 to 83886.08
- basis_weight: float32 [600, 512], P(None, 'edge'), may hold values from -3 to 3
- basis_first: float32 [600, 512], P(None, 'edge'), may hold values from -224 to 224
- basis_second: float32 [600, 512], P(None, 'edge'), may hold values from 1310.72 to 5242.88
- readout_weight: float32 [256], P('edge'), may hold values from -0.375 to 0.375
- readout_first: float32 [256], P('edge'), may hold values from -1536 to 1536
- readout_second: float32 [256], P('edge'), may hold values from 73728 to 294912
- norm_gains: float32 [2, 256], P(None, 'edge'), may hold values from 0.5 to 1.5
- gains_first: float32 [2, 256], P(None, 'edge'), may hold values from -1024 to 1024
- gains_second: float32 [2, 256], P(None, 'edge'), may hold values from 32768 to 131072
Outputs:
- block_out: bfloat16 [4, 8192, 256], P('rep', 'edge')
- energy: float32 [4, 8192], P('rep', 'edge')
- input_grad: float32 [4, 8192, 256], P('rep', 'edge')
- attention_first_new: float32 [256, 768], P(None, 'edge')
- attention_second_new: float32 [256, 768], P(None, 'edge')
- attention_weight_new: float32 [256, 768], P(None, 'edge')
- output_first_new: float32 [256, 256], P(None, 'edge')
- output_second_new: float32 [256, 256], P(None, 'edge')
- output_weight_new: float32 [256, 256], P(None, 'edge')
- gateup_first_new: float32 [256, 2048], P(None, 'edge')
- gateup_second_new: float32 [256, 2048], P(None, 'edge')
- gateup_weight_new: float32 [256, 2048], P(None, 'edge')
- down_first_new: float32 [1024, 256], P(None, 'edge')
- down_second_new: float32 [1024, 256], P(None, 'edge')
- down_weight_new: float32 [1024, 256], P(None, 'edge')
- basis_first_new: float32 [600, 512], P(None, 'edge')
- basis_second_new: float32 [600, 512], P(None, 'edge')
- basis_weight_new: float32 [600, 512], P(None, 'edge')
- readout_first_new: float32 [256], P('edge')
- readout_second_new: float32 [256], P('edge')
- readout_weight_new: float32 [256], P('edge')
- gains_first_new: float32 [2, 256], P(None, 'edge')
- gains_second_new: float32 [2, 256], P(None, 'edge')
- norm_gains_new: float32 [2, 256], P(None, 'edge')
- attention_low: bfloat16 [256, 768], P(None, 'edge')
- output_low: bfloat16 [256, 256], P(None, 'edge')
- gateup_low: bfloat16 [256, 2048], P(None, 'edge')
- down_low: bfloat16 [1024, 256], P(None, 'edge')
- basis_low: bfloat16 [600, 512], P(None, 'edge')
Inputs may be any that keep to these rules, and one draw needn't show every extreme that they name: `slot_index`: for each graph batch and each owner's 1024 atoms, the 16384 entries form a permutation of 0 to 16383, so every edge row is named by exactly one slot. `live_mask`: each atom's live slots come first, and its first slot is live.
All inputs are finite; a program needn't handle non-finite values.
Results may differ from a plain program's by a relative error of at most 0.017.
Values may be sent and summed in bfloat16 or wider, within the bound.
No kernel may reach another device: no remote copies, remote signals or barrier semaphores. Data moves between devices by JAX's collectives and lax.ppermute only.
A program may use at most 320 MiB of HBM per device.

v0:
```python
import jax
import jax.numpy as jnp
from jax import lax
from jax.sharding import PartitionSpec as P

H = 256
HEADS = 8
FF = 1024
NB = 600
STEP = 5
HEAD_DIM = 32


EPS = 1e-06
CUTOFF = 6.0
BETA_ONE = 0.5
BETA_TWO = 0.5
ADAM_EPS = 1e-08
DECAY = 0.01


def radial_basis(edge_len):
    centres = jnp.arange(NB).astype(jnp.float32) * (CUTOFF / (NB - 1))
    spread = 2.0 * CUTOFF / (NB - 1)
    return jnp.exp(-jnp.square((edge_len[:, None] - centres) / spread))


def adamw_step(weight, first_mom, second, gradient, step_rate):
    first_new = BETA_ONE * first_mom + (1.0 - BETA_ONE) * gradient
    second_new = BETA_TWO * second + (1.0 - BETA_TWO) * gradient * gradient
    fix_one = 1.0 - BETA_ONE**STEP
    fix_two = 1.0 - BETA_TWO**STEP
    direction = first_new / fix_one / (jnp.sqrt(second_new / fix_two) + ADAM_EPS) + DECAY * weight
    return (first_new, second_new, weight - step_rate * direction)


def norm_back(inputs, inverse, gain_row, d_normed):
    scaled = d_normed * gain_row
    gain_grad = jnp.sum(d_normed * inputs * inverse, axis=0)
    d_inputs = inverse * scaled - inputs * inverse**3 * jnp.mean(
        scaled * inputs, axis=-1, keepdims=True
    )
    return (gain_grad, d_inputs)


def local(
    atom_features,
    distances,
    source_index,
    slot_index,
    live_mask,
    output_cot,
    energy_cot,
    attention_weight,
    attention_first,
    attention_second,
    output_weight,
    output_first,
    output_second,
    gateup_weight,
    gateup_first,
    gateup_second,
    down_weight,
    down_first,
    down_second,
    basis_weight,
    basis_first,
    basis_second,
    readout_weight,
    readout_first,
    readout_second,
    norm_gains,
    gains_first,
    gains_second,
):
    proj_attention, proj_output, proj_gateup, proj_down, proj_basis, read_full, gain_full = (
        lax.all_gather(attention_weight.astype(jnp.bfloat16), "edge", axis=1, tiled=True),
        lax.all_gather(output_weight.astype(jnp.bfloat16), "edge", axis=1, tiled=True),
        lax.all_gather(gateup_weight.astype(jnp.bfloat16), "edge", axis=1, tiled=True),
        lax.all_gather(down_weight.astype(jnp.bfloat16), "edge", axis=1, tiled=True),
        lax.all_gather(basis_weight.astype(jnp.bfloat16), "edge", axis=1, tiled=True),
        lax.all_gather(readout_weight[None].astype(jnp.bfloat16), "edge", axis=1, tiled=True),
        lax.all_gather(norm_gains.astype(jnp.bfloat16), "edge", axis=1, tiled=True),
    )
    features = atom_features[0].astype(jnp.float32)
    edge_len = distances[0]
    sources = source_index[0]
    slot_ids = slot_index[0].reshape(-1)
    is_live = live_mask[0] > 0
    atom_count = features.shape[0]
    model_width = features.shape[1]
    neighbours = live_mask.shape[2]
    ff_width = proj_down.shape[0]
    gain_one = gain_full[0].astype(jnp.float32)
    gain_two = gain_full[1].astype(jnp.float32)
    reader = read_full[0].astype(jnp.float32)
    proj_query = proj_attention[:, :model_width]
    proj_kv = proj_attention[:, model_width:]
    scaling = HEAD_DIM ** (-0.5)
    inv_one = lax.rsqrt(jnp.mean(features * features, axis=-1, keepdims=True) + EPS)
    normed_one = (features * inv_one * gain_one).astype(jnp.bfloat16)
    query_vals = jnp.dot(normed_one, proj_query, preferred_element_type=jnp.float32)
    queries = query_vals.astype(jnp.bfloat16).reshape(atom_count, HEADS, HEAD_DIM)
    edge_rows = normed_one[sources]
    kept_radial = radial_basis(edge_len).astype(jnp.bfloat16)
    edge_kv = jnp.dot(edge_rows, proj_kv, preferred_element_type=jnp.float32) + jnp.dot(
        kept_radial, proj_basis, preferred_element_type=jnp.float32
    )
    received = lax.all_to_all(
        edge_kv.astype(jnp.bfloat16), "edge", split_axis=0, concat_axis=0, tiled=True
    )
    paired = received[slot_ids].reshape(atom_count, neighbours, 2 * model_width)
    key_rows = paired[..., :model_width].reshape(atom_count, neighbours, HEADS, HEAD_DIM)
    values = paired[..., model_width:].reshape(atom_count, neighbours, HEADS, HEAD_DIM)
    scores = (
        jnp.einsum("ahd,akhd->akh", queries, key_rows, preferred_element_type=jnp.float32) * scaling
    )
    masked = jnp.where(is_live[..., None], scores, -1e30)
    row_top = jnp.max(masked, axis=1, keepdims=True)
    exp_terms = jnp.exp(masked - row_top)
    softmax = exp_terms / jnp.sum(exp_terms, axis=1, keepdims=True)
    soft_low = softmax.astype(jnp.bfloat16)
    mixture = jnp.einsum("akh,akhd->ahd", soft_low, values, preferred_element_type=jnp.float32)
    mixture_low = mixture.astype(jnp.bfloat16).reshape(atom_count, model_width)
    after_attn = features + jnp.dot(mixture_low, proj_output, preferred_element_type=jnp.float32)
    inv_two = lax.rsqrt(jnp.mean(after_attn * after_attn, axis=-1, keepdims=True) + EPS)
    normed_two = (after_attn * inv_two * gain_two).astype(jnp.bfloat16)
    gate_up = jnp.dot(normed_two, proj_gateup, preferred_element_type=jnp.float32)
    gate = gate_up[:, :ff_width]
    up_part = gate_up[:, ff_width:]
    gate_sig = jax.nn.sigmoid(gate)
    swished = gate * gate_sig
    hidden_low = (swished * up_part).astype(jnp.bfloat16)
    result = after_attn + jnp.dot(hidden_low, proj_down, preferred_element_type=jnp.float32)
    energy = jnp.sum(result * reader, axis=-1)
    energy_row = energy_cot[0]
    d_result = output_cot[0].astype(jnp.float32) + energy_row[:, None] * reader
    grad_read = jnp.sum(energy_row[:, None] * result, axis=0)
    d_ffn = d_result.astype(jnp.bfloat16)
    grad_down = jnp.dot(hidden_low.T, d_ffn, preferred_element_type=jnp.float32)
    d_hidden = jnp.dot(d_ffn, proj_down.T, preferred_element_type=jnp.float32)
    d_gate = d_hidden * up_part * gate_sig * (1.0 + gate * (1.0 - gate_sig))
    d_up = d_hidden * swished
    d_gate_up = jnp.concatenate([d_gate, d_up], axis=1).astype(jnp.bfloat16)
    grad_gateup = jnp.dot(normed_two.T, d_gate_up, preferred_element_type=jnp.float32)
    d_normed_two = jnp.dot(d_gate_up, proj_gateup.T, preferred_element_type=jnp.float32)
    grad_gain_two, d_norm_two = norm_back(after_attn, inv_two, gain_two, d_normed_two)
    d_after = d_result + d_norm_two
    d_attn = d_after.astype(jnp.bfloat16)
    grad_output = jnp.dot(mixture_low.T, d_attn, preferred_element_type=jnp.float32)
    d_mixture = jnp.dot(d_attn, proj_output.T, preferred_element_type=jnp.float32)
    d_mixture = d_mixture.astype(jnp.bfloat16).reshape(atom_count, HEADS, HEAD_DIM)
    d_soft = jnp.einsum("ahd,akhd->akh", d_mixture, values, preferred_element_type=jnp.float32)
    d_values = jnp.einsum("akh,ahd->akhd", soft_low, d_mixture, preferred_element_type=jnp.float32)
    d_scores = softmax * (d_soft - jnp.sum(softmax * d_soft, axis=1, keepdims=True))
    d_scores = d_scores.astype(jnp.bfloat16)
    d_queries = (
        jnp.einsum("akh,akhd->ahd", d_scores, key_rows, preferred_element_type=jnp.float32)
        * scaling
    )
    d_queries = d_queries.astype(jnp.bfloat16).reshape(atom_count, model_width)
    d_keys = (
        jnp.einsum("akh,ahd->akhd", d_scores, queries, preferred_element_type=jnp.float32) * scaling
    )
    d_paired = jnp.concatenate(
        [
            d_keys.reshape(atom_count, neighbours, model_width),
            d_values.reshape(atom_count, neighbours, model_width),
        ],
        axis=-1,
    )
    d_paired = d_paired.reshape(atom_count * neighbours, 2 * model_width)
    d_received = (
        jnp.zeros((received.shape[0], 2 * model_width), jnp.float32).at[slot_ids].add(d_paired)
    )
    d_received = d_received.astype(jnp.bfloat16)
    d_edges = lax.all_to_all(d_received, "edge", split_axis=0, concat_axis=0, tiled=True)
    grad_basis = jnp.dot(kept_radial.T, d_edges, preferred_element_type=jnp.float32)
    grad_kv = jnp.dot(edge_rows.T, d_edges, preferred_element_type=jnp.float32)
    d_rows = jnp.dot(d_edges, proj_kv.T, preferred_element_type=jnp.float32).astype(jnp.bfloat16)
    d_from_edges = jax.ops.segment_sum(d_rows.astype(jnp.float32), sources, num_segments=atom_count)
    d_normed_one = (
        jnp.dot(d_queries, proj_query.T, preferred_element_type=jnp.float32) + d_from_edges
    )
    grad_attention = jnp.concatenate(
        [jnp.dot(normed_one.T, d_queries, preferred_element_type=jnp.float32), grad_kv], axis=1
    )
    grad_gain_one, d_norm_one = norm_back(features, inv_one, gain_one, d_normed_one)
    input_grad = (d_after + d_norm_one)[None]
    grad_gains = jnp.stack([grad_gain_one, grad_gain_two])
    totals = lax.psum(
        (
            grad_attention,
            grad_output,
            grad_gateup,
            grad_down,
            grad_basis,
            grad_read[None],
            grad_gains,
        ),
        "rep",
    )
    shards = (
        lax.psum_scatter(totals[0], "edge", scatter_dimension=1, tiled=True),
        lax.psum_scatter(totals[1], "edge", scatter_dimension=1, tiled=True),
        lax.psum_scatter(totals[2], "edge", scatter_dimension=1, tiled=True),
        lax.psum_scatter(totals[3], "edge", scatter_dimension=1, tiled=True),
        lax.psum_scatter(totals[4], "edge", scatter_dimension=1, tiled=True),
        lax.psum_scatter(totals[5], "edge", scatter_dimension=1, tiled=True),
        lax.psum_scatter(totals[6], "edge", scatter_dimension=1, tiled=True),
    )
    step_rates = (
        H ** (-0.5),
        (H // 16) ** (-0.5),
        H ** (-0.5),
        FF ** (-0.5),
        0.5,
        H ** (-0.5),
        0.2,
    )
    masters = (
        attention_weight,
        output_weight,
        gateup_weight,
        down_weight,
        basis_weight,
        readout_weight,
        norm_gains,
    )
    firsts = (
        attention_first,
        output_first,
        gateup_first,
        down_first,
        basis_first,
        readout_first,
        gains_first,
    )
    seconds = (
        attention_second,
        output_second,
        gateup_second,
        down_second,
        basis_second,
        readout_second,
        gains_second,
    )
    gradients = (shards[0], shards[1], shards[2], shards[3], shards[4], shards[5][0], shards[6])
    updated = [
        adamw_step(
            masters[number], firsts[number], seconds[number], gradients[number], step_rates[number]
        )
        for number in range(7)
    ]
    return (
        result.astype(jnp.bfloat16)[None],
        energy[None],
        input_grad,
        updated[0][0],
        updated[0][1],
        updated[0][2],
        updated[1][0],
        updated[1][1],
        updated[1][2],
        updated[2][0],
        updated[2][1],
        updated[2][2],
        updated[3][0],
        updated[3][1],
        updated[3][2],
        updated[4][0],
        updated[4][1],
        updated[4][2],
        updated[5][0],
        updated[5][1],
        updated[5][2],
        updated[6][0],
        updated[6][1],
        updated[6][2],
        updated[0][2].astype(jnp.bfloat16),
        updated[1][2].astype(jnp.bfloat16),
        updated[2][2].astype(jnp.bfloat16),
        updated[3][2].astype(jnp.bfloat16),
        updated[4][2].astype(jnp.bfloat16),
    )


def solution(mesh):
    return jax.shard_map(
        local,
        mesh=mesh,
        in_specs=(
            P("rep", "edge", None),
            P("rep", "edge"),
            P("rep", "edge"),
            P("rep", "edge", None),
            P("rep", "edge", None),
            P("rep", "edge", None),
            P("rep", "edge"),
            P(None, "edge"),
            P(None, "edge"),
            P(None, "edge"),
            P(None, "edge"),
            P(None, "edge"),
            P(None, "edge"),
            P(None, "edge"),
            P(None, "edge"),
            P(None, "edge"),
            P(None, "edge"),
            P(None, "edge"),
            P(None, "edge"),
            P(None, "edge"),
            P(None, "edge"),
            P(None, "edge"),
            P("edge"),
            P("edge"),
            P("edge"),
            P(None, "edge"),
            P(None, "edge"),
            P(None, "edge"),
        ),
        out_specs=(
            P("rep", "edge", None),
            P("rep", "edge"),
            P("rep", "edge", None),
            P(None, "edge"),
            P(None, "edge"),
            P(None, "edge"),
            P(None, "edge"),
            P(None, "edge"),
            P(None, "edge"),
            P(None, "edge"),
            P(None, "edge"),
            P(None, "edge"),
            P(None, "edge"),
            P(None, "edge"),
            P(None, "edge"),
            P(None, "edge"),
            P(None, "edge"),
            P(None, "edge"),
            P("edge"),
            P("edge"),
            P("edge"),
            P(None, "edge"),
            P(None, "edge"),
            P(None, "edge"),
            P(None, "edge"),
            P(None, "edge"),
            P(None, "edge"),
            P(None, "edge"),
            P(None, "edge"),
        ),
        check_vma=False,
    )
```

profile of v0, /device:TPU:0, one launch (start us, length us, event | category | flops | bytes accessed | tf_op | source)
XLA Modules:
  0.0 2021.0 jit_solution(11173113462124886549)
XLA Ops:
  7.9 22.1 %all-gather.1 = bf16[8,32,2]{1,2,0:T(2,128)(2,1)S(1)} all-gather(bf16[1,32,2]{1,2,0:T(2,128)(2,1)S(1)} %convert_bitcast_fusion.4), channel_id=1, replica_groups=mesh['edge'=8,'rep'=4] {'edge'}, dimensions={0}, use_global_device_ids=true | all-gather | bytes 1152 | tf_op jit(solution)/shard_map/all_gather | solution.py:83
  33.5 31.1 %all_gather.22 = bf16[256,768]{0,1:T(8,128)(2,1)S(1)} all-gather(bf16[256,96]{0,1:T(8,128)(2,1)S(1)} %convert_element_type.128), channel_id=1, replica_groups=mesh['edge'=8,'rep'=4] {'edge'}, dimensions={1}, use_global_device_ids=true | all-gather | bytes 442368 | tf_op jit(solution)/shard_map/all_gather | solution.py:77
  67.2 31.7 %all_gather.23 = bf16[600,512]{0,1:T(8,128)(2,1)S(1)} all-gather(bf16[600,64]{0,1:T(8,128)(2,1)S(1)} %convert_element_type.131), channel_id=1, replica_groups=mesh['edge'=8,'rep'=4] {'edge'}, dimensions={1}, use_global_device_ids=true | all-gather | bytes 691200 | tf_op jit(solution)/shard_map/all_gather | solution.py:81
  98.8 64.9 %gather_fusion = bf16[16384,256]{1,0:T(8,128)(2,1)} fusion(bf16[1024,256]{1,0:T(8,128)(2,1)S(1)} %copy.170, s32[16384]{0:T(1024)S(1)} %broadcast_clamp_fusion.1), kind=kCustom, calls=%fused_computation | custom fusion | bytes 16842752 | tf_op jit(solution)/shard_map/gather | solution.py:104
  163.7 16.8 fusion.52
  180.5 22.3 %add_convert_fusion = bf16[16384,512]{1,0:T(8,128)(2,1)} fusion(f32[16384,512]{1,0:T(8,128)} %fusion.52, bf16[600,512]{0,1:T(8,128)(2,1)S(1)} %all_gather.23, f32[600]{0:T(1024)S(1)} %convert_multiply_fusion.1, f32[16384]{0:T(1024)S(1)} %bitcast.199), kind=kOutput, calls=%fused_computation.14 | convolution fusion | flops 10132258816 | bytes 51013984 | tf_op jit(solution)/shard_map/dot_general | solution.py:106
  211.0 280.5 %all-reduce = bf16[256]{0:T(256)(128)(2,1)S(1)} all-reduce(bf16[256]{0:T(256)(128)(2,1)S(1)} %dynamic-update-slice), channel_id=2, replica_groups=mesh['edge'=8,'rep'=4] {'edge'}, use_global_device_ids=true, to_apply=%add | all-reduce | flops 256 | bytes 1024
  495.7 115.2 %all_gather.24 = bf16[256,256]{0,1:T(8,128)(2,1)S(1)} all-gather(bf16[256,32]{0,1:T(8,128)(2,1)S(1)} %convert_element_type.136), channel_id=1, replica_groups=mesh['edge'=8,'rep'=4] {'edge'}, dimensions={1}, use_global_device_ids=true | all-gather | bytes 147456 | tf_op jit(solution)/shard_map/all_gather | solution.py:78
  610.8 31.6 %all_gather.26 = bf16[1024,256]{0,1:T(8,128)(2,1)S(1)} all-gather(bf16[1024,32]{0,1:T(8,128)(2,1)S(1)} %convert_element_type.140), channel_id=1, replica_groups=mesh['edge'=8,'rep'=4] {'edge'}, dimensions={1}, use_global_device_ids=true | all-gather | bytes 589824 | tf_op jit(solution)/shard_map/all_gather | solution.py:80
  642.5 74.5 %gather_fusion.1 = bf16[16384,512]{1,0:T(8,128)(2,1)} fusion(bf16[16384,512]{1,0:T(8,128)(2,1)} %bitcast.16, s32[16384]{0:T(1024)S(1)} %broadcast_clamp_fusion), kind=kCustom, calls=%fused_computation.1 | custom fusion | bytes 33619968 | tf_op jit(solution)/shard_map/gather | solution.py:112
  717.0 11.3 fusion.86
  728.4 12.2 copy.226
  753.5 12.2 copy.227
  823.9 15.1 fusion.11
  847.2 21.4 %multiply_bitcast_fusion.1 = f32[1024,16,8,32]{3,2,1,0:T(8,128)} fusion(f32[1024,8,16]{1,2,0:T(8,128)S(1)} %get-tuple-element.220, f32[1024,8,32]{2,1,0:T(8,128)S(1)} %copy-done.3), kind=kLoop, calls=%fused_computation.8 | loop fusion | flops 8388608 | bytes 18350080 | tf_op jit(solution)/shard_map/mul | solution.py:163
  868.5 45.2 %concatenate.16 = f32[16384,256]{1,0:T(8,128)} reshape(f32[1024,16,8,32]{3,2,1,0:T(8,128)} %multiply_bitcast_fusion.1) | data formatting | bytes 33554432 | tf_op jit(solution)/shard_map/concatenate | solution.py:165
  913.8 25.7 %multiply_bitcast_fusion = f32[1024,16,8,32]{3,2,1,0:T(8,128)} fusion(f32[1024,8,16]{1,2,0:T(8,128)} %get-tuple-element.217, f32[1024,8,32]{2,1,0:T(8,128)} %copy.180), kind=kLoop, calls=%fused_computation.7 | loop fusion | flops 4194304 | bytes 18350080 | tf_op jit(solution)/shard_map/akh,ahd->akhd/transpose | solution.py:154
  939.5 45.3 %concatenate.17 = f32[16384,256]{1,0:T(8,128)} reshape(f32[1024,16,8,32]{3,2,1,0:T(8,128)} %multiply_bitcast_fusion) | data formatting | bytes 33554432 | tf_op jit(solution)/shard_map/concatenate | solution.py:165
  984.8 112.4 %scatter_custom_fusion = f32[16384,512]{1,0:T(8,128)} fusion(s32[16384]{0:T(1024)} %bitcast.182, f32[16384,256]{1,0:T(8,128)} %concatenate.17, f32[]{:T(128)} %constant.30.clone.1, f32[16384,256]{1,0:T(8,128)} %concatenate.16, f32[]{:T(128)} %constant.21.clone.1), kind=kCustom, calls=%fused_computation.10 | custom fusion | flops 16777216 | bytes 67109888 | tf_op jit(solution)/shard_map/scatter-add | solution.py:174
  1097.2 17.3 convert_element_type.151
  1134.0 335.2 %all-to-all-done.1 = bf16[8,2048,512]{2,1,0:T(8,128)(2,1)} async-done(((bf16[8,2048,512]{2,1,0:T(8,128)(2,1)}), bf16[8,2048,512]{2,1,0:T(8,128)(2,1)}, u32[]{:S(2)}, u32[]{:S(2)}) %all-to-all-start.1) | async-done | bytes 16777248 | tf_op jit(solution)/shard_map/all_to_all | solution.py:177
  1469.2 16.1 fusion.7
  1485.3 88.7 %scatter_fusion = f32[1024,256]{1,0:T(8,128)S(1)} fusion(f32[1024,256]{1,0:T(8,128)S(1)} %fusion.60, s32[16384]{0:T(1024)S(1)} %bitcast.180, f32[16384,256]{1,0:T(8,128)} %fusion.7), kind=kCustom, calls=%fused_computation.3 | custom fusion | flops 4194304 | bytes 50397184 | tf_op jit(solution)/shard_map/scatter-add | solution.py:181
  1600.3 18.2 fusion.8
  1625.9 12.0 reduce-scatter.26.cloned.1.call-done
  1638.7 63.3 %reduce-scatter.14.cloned.1.call-done = f32[256,32]{0,1:T(8,128)} async-done(((f32[256,256]{0,1:T(8,128)}), f32[256,32]{0,1:T(8,128)}) %reduce-scatter.14.cloned.1.call-update) | async-done | bytes 32784 | tf_op jit(solution)/shard_map/reduce_scatter | solution.py:205
  1701.9 11.0 all-reduce.1
  1714.2 53.5 %reduce-scatter.18.cloned.1.call-done = f32[1024,32]{0,1:T(8,128)} async-done(((f32[1024,256]{0,1:T(8,128)}), f32[1024,32]{0,1:T(8,128)}) %reduce-scatter.18.cloned.1.call-update) | async-done | bytes 131088 | tf_op jit(solution)/shard_map/reduce_scatter | solution.py:207
  1767.7 71.2 %reduce-scatter.16.cloned.1.call-done = f32[256,256]{1,0:T(8,128)} async-done(((f32[256,2048]{1,0:T(8,128)}), f32[256,256]{1,0:T(8,128)}) %reduce-scatter.16.cloned.1.call-update) | async-done | bytes 262160 | tf_op jit(solution)/shard_map/reduce_scatter | solution.py:206
  1838.9 65.2 %reduce-scatter.22.cloned.1.call-done = f32[96,256]{1,0:T(8,128)} async-done(((f32[768,256]{1,0:T(8,128)}), f32[96,256]{1,0:T(8,128)}) %reduce-scatter.22.cloned.1.call-update) | async-done | bytes 98320
  1904.1 66.8 %reduce-scatter.20.cloned.1.call-done = f32[600,64]{0,1:T(8,128)} async-done(((f32[600,512]{0,1:T(8,128)}), f32[600,64]{0,1:T(8,128)}) %reduce-scatter.20.cloned.1.call-update) | async-done | bytes 153616 | tf_op jit(solution)/shard_map/reduce_scatter | solution.py:208
  1973.6 33.1 %all-reduce.5.cloned.1.call-done = (f32[256,96]{0,1:T(8,128)}, f32[256,256]{1,0:T(8,128)}, f32[1024,32]{0,1:T(8,128)}, f32[600,64]{0,1:T(8,128)}) async-done(((f32[256,96]{0,1:T(8,128)}, f32[256,256]{1,0:T(8,128)}, f32[1024,32]{0,1:T(8,128)}, f32[600,64]{0,1:T(8,128)}), (f32[256,96]{0,1:T(8,128)}, f32[256,256]{1,0:T(8,128)}, f32[1024,32]{0,1:T(8,128)}, f32[600,64]{0,1:T(8,128)})) %all-reduce.5.cloned.1.call-update) | async-done | bytes 645136 | tf_op jit(solution)/shard_map/psum | solution.py:191
  (214 shorter events, 162.6 us)
Async XLA Ops:
  7.2 173.3 %copy-start.39 = (f32[600]{0:T(1024)}, f32[600]{0:T(1024)S(1)}, u32[]{:S(2)}) copy-start(f32[600]{0:T(1024)S(1)} %convert_multiply_fusion.1) | copy-start | bytes 7204
  30.7 133.0 %copy-start.34 = (f32[1,256]{1,0:T(1,128)}, f32[1,256]{1,0:T(1,128)S(1)}, u32[]{:S(2)}) copy-start(f32[1,256]{1,0:T(1,128)S(1)} %get-tuple-element.229) | copy-start | bytes 3076
  64.6 428.0 %copy-start.11 = (bf16[256,768]{0,1:T(8,128)(2,1)}, bf16[256,768]{0,1:T(8,128)(2,1)S(1)}, u32[]{:S(2)}) copy-start(bf16[256,768]{0,1:T(8,128)(2,1)S(1)} %all_gather.22) | copy-start | bytes 1179652
  66.7 97.0 %copy-start.30 = (f32[1024]{0:T(1024)}, f32[1024]{0:T(1024)S(1)}, u32[]{:S(2)}) copy-start(f32[1024]{0:T(1024)S(1)} %get-tuple-element.225) | copy-start | bytes 12292
  202.8 288.8 %copy-start.27 = (f32[256,32]{0,1:T(8,128)S(1)}, f32[256,32]{0,1:T(8,128)}, u32[]{:S(2)}) copy-start(f32[256,32]{0,1:T(8,128)} %param.38) | copy-start | bytes 98308
  202.8 288.8 %copy-start.19 = (f32[1024,32]{0,1:T(8,128)S(1)}, f32[1024,32]{0,1:T(8,128)}, u32[]{:S(2)}) copy-start(f32[1024,32]{0,1:T(8,128)} %param.44) | copy-start | bytes 393220
  202.8 288.8 %copy-start.33 = (s32[1,1024,16]{1,2,0:T(8,128)S(1)}, s32[1,1024,16]{1,2,0:T(8,128)}, u32[]{:S(2)}) copy-start(s32[1,1024,16]{1,2,0:T(8,128)} %param.32) | copy-start | bytes 196612
  202.8 289.1 %copy-start.21 = (bf16[1,1024,256]{2,1,0:T(8,128)(2,1)S(1)}, bf16[1,1024,256]{2,1,0:T(8,128)(2,1)}, u32[]{:S(2)}) copy-start(bf16[1,1024,256]{2,1,0:T(8,128)(2,1)} %param.33) | copy-start | bytes 1572868
  202.8 289.3 %copy-start.32 = (s32[1,1024,16]{1,2,0:T(8,128)S(1)}, s32[1,1024,16]{1,2,0:T(8,128)}, u32[]{:S(2)}) copy-start(s32[1,1024,16]{1,2,0:T(8,128)} %param.31) | copy-start | bytes 196612
  202.8 439.7 %all-to-all-start = ((bf16[8,2048,512]{2,1,0:T(8,128)(2,1)}), bf16[8,2048,512]{2,1,0:T(8,128)(2,1)}, u32[]{:S(2)}, u32[]{:S(2)}) async-start(bf16[8,2048,512]{2,1,0:T(8,128)(2,1)} %bitcast.172), calls=%async_computation | async-start | bytes 33554432 | tf_op jit(solution)/shard_map/all_to_all | solution.py:109
  208.7 589.9 %all-gather.4.cloned.1.call-start = ((), (), s32[]{:S(2)}) async-start(), calls=%async_computation.9 | async-start | bytes 1179648 | tf_op jit(solution)/shard_map/all_gather | solution.py:79
  491.6 315.2 %copy-start.48 = (f32[256]{0:T(256)}, f32[256]{0:T(256)S(1)}, u32[]{:S(2)}) copy-start(f32[256]{0:T(256)S(1)} %mul.521) | copy-start | bytes 3076
  492.1 314.7 %copy-start.22 = (bf16[1,1024,256]{1,2,0:T(8,128)(2,1)}, bf16[1,1024,256]{1,2,0:T(8,128)(2,1)S(1)}, u32[]{:S(2)}) copy-start(bf16[1,1024,256]{1,2,0:T(8,128)(2,1)S(1)} %copy.175) | copy-start | bytes 1572868
  1114.5 354.7 %all-to-all-start.1 = ((bf16[8,2048,512]{2,1,0:T(8,128)(2,1)}), bf16[8,2048,512]{2,1,0:T(8,128)(2,1)}, u32[]{:S(2)}, u32[]{:S(2)}) async-start(bf16[8,2048,512]{2,1,0:T(8,128)(2,1)} %bitcast.170), calls=%async_computation.1 | async-start | bytes 33554432 | tf_op jit(solution)/shard_map/all_to_all | solution.py:177
  1120.4 500.4 %reduce-scatter.24.cloned.1.call-start = ((), (), s32[]{:S(2)}) async-start(), calls=%async_computation.15 | async-start | bytes 147456
  1121.3 516.6 %reduce-scatter.26.cloned.1.call-start = ((), (), s32[]{:S(2)}) async-start(), calls=%async_computation.16 | async-start | bytes 147456
  1485.3 91.8 %copy-start.42 = (f32[256]{0:T(256)S(1)}, f32[256]{0:T(256)}, u32[]{:S(2)}) copy-start(f32[256]{0:T(256)} %get-tuple-element.174) | copy-start | bytes 3076
  1485.3 92.7 %copy-start.5 = (f32[1024,256]{0,1:T(8,128)S(1)}, f32[1024,256]{0,1:T(8,128)}, u32[]{:S(2)}) copy-start(f32[1024,256]{0,1:T(8,128)} %copy-done.4) | copy-start | bytes 3145732
  1485.3 92.7 %copy-start.10 = (bf16[1024,8,32]{0,2,1:T(8,128)(2,1)S(1)}, bf16[1024,8,32]{0,2,1:T(8,128)(2,1)}, u32[]{:S(2)}) copy-start(bf16[1024,8,32]{0,2,1:T(8,128)(2,1)} %copy-done.9) | copy-start | bytes 1572868
  1485.3 94.0 %copy-start.47 = (f32[1,1024]{1,0:T(1,128)S(1)}, f32[1,1024]{1,0:T(1,128)}, u32[]{:S(2)}) copy-start(f32[1,1024]{1,0:T(1,128)} %param.34) | copy-start | bytes 12292
  1485.3 94.0 %copy-start.49 = (f32[256]{0:T(256)S(1)}, f32[256]{0:T(256)}, u32[]{:S(2)}) copy-start(f32[256]{0:T(256)} %copy-done.48) | copy-start | bytes 3076
  1577.9 124.0 %reduce-scatter.14.cloned.1.call-start = ((), (), s32[]{:S(2)}) async-start(), calls=%async_computation.10 | async-start | bytes 294912 | tf_op jit(solution)/shard_map/reduce_scatter | solution.py:205
  1579.1 188.7 %reduce-scatter.18.cloned.1.call-start = ((), (), s32[]{:S(2)}) async-start(), calls=%async_computation.12 | async-start | bytes 1179648 | tf_op jit(solution)/shard_map/reduce_scatter | solution.py:207
  1582.8 256.1 %reduce-scatter.16.cloned.1.call-start = ((), (), s32[]{:S(2)}) async-start(), calls=%async_computation.11 | async-start | bytes 2359296 | tf_op jit(solution)/shard_map/reduce_scatter | solution.py:206
  1587.8 316.3 %reduce-scatter.22.cloned.1.call-start = ((), (), s32[]{:S(2)}) async-start(), calls=%async_computation.14 | async-start | bytes 884736
  1600.3 370.7 %reduce-scatter.20.cloned.1.call-start = ((), (), s32[]{:S(2)}) async-start(), calls=%async_computation.13 | async-start | bytes 1474560 | tf_op jit(solution)/shard_map/reduce_scatter | solution.py:208
  1618.5 388.1 %copy-start.23 = (f32[256,96]{0,1:T(8,128)S(1)}, f32[256,96]{0,1:T(8,128)}, u32[]{:S(2)}) copy-start(f32[256,96]{0,1:T(8,128)} %param.35) | copy-start | bytes 294916
  1618.5 389.9 %copy-start.20 = (f32[1024,32]{0,1:T(8,128)S(1)}, f32[1024,32]{0,1:T(8,128)}, u32[]{:S(2)}) copy-start(f32[1024,32]{0,1:T(8,128)} %param.44) | copy-start | bytes 393220
  1618.5 391.7 %copy-start.18 = (f32[600,64]{0,1:T(8,128)S(1)}, f32[600,64]{0,1:T(8,128)}, u32[]{:S(2)}) copy-start(f32[600,64]{0,1:T(8,128)} %param.47) | copy-start | bytes 460804
  1618.5 393.7 %copy-start.16 = (f32[256,256]{1,0:T(8,128)S(1)}, f32[256,256]{1,0:T(8,128)}, u32[]{:S(2)}) copy-start(f32[256,256]{1,0:T(8,128)} %param.41) | copy-start | bytes 786436
  1618.5 393.7 %copy-start.25 = (f32[256,256]{1,0:T(8,128)S(1)}, f32[256,256]{1,0:T(8,128)}, u32[]{:S(2)}) copy-start(f32[256,256]{1,0:T(8,128)} %param.43) | copy-start | bytes 786436
  1618.6 388.1 %all-reduce.5.cloned.1.call-start = ((), (), s32[]{:S(2)}) async-start(), calls=%async_computation.17 | async-start | bytes 1310720 | tf_op jit(solution)/shard_map/psum | solution.py:191
  (35 other events, 596.9 us)
Sparse Core Ops, SparseCore 0:
  212.2 95.4 all-gather.3
  1125.1 286.0 reduce-scatter.23
  1578.0 59.8 reduce-scatter.25
  1641.6 60.2 reduce-scatter.13
  1705.2 62.4 reduce-scatter.17
  1771.5 67.3 reduce-scatter.15
  1842.6 61.5 reduce-scatter.21
  1907.5 63.3 reduce-scatter.19
  1973.5 33.1 all-reduce.4
where the time goes:
time: 2030 us; the launch traced here: 2020 us
  waiting for transfers between devices  700 us (34%)
  blocking collectives  523 us (26%)
  other arithmetic  352 us (17%)
  local copies, waits for them, and re-layouts  312 us (15%)
  matrix products  106 us (5%)
    all_to_all x1, waiting for transfers between devices, local(): lax.all_to_all(d_received, 'edge', split_axis=0, concat_axis=0, tiled=True)  335 us
    unnamed x1, blocking collectives  281 us
    all_gather x1, blocking collectives, local(): lax.all_gather(output_weight.astype(jnp.bfloat16), 'edge', axis=1, tiled=...  115 us
    scatter-add x1, other arithmetic, local(): jnp.zeros((received.shape[0], 2 * model_width), jnp.float32).at[slot_ids]  112 us
    concatenate x2, local copies, waits for them, and re-layouts, local(): jnp.concatenate([d_keys.reshape(atom_count, neighbours, model_width), d_v...  90.5 us
    scatter-add x1, other arithmetic, local(): jax.ops.segment_sum(d_rows.astype(jnp.float32), sources, num_segments=ato...  88.7 us
    unnamed x12, waiting for transfers between devices  77.3 us
    gather x1, local copies, waits for them, and re-layouts, local(): paired = received[slot_ids].reshape(atom_count, neighbours, 2 * model_width)  74.5 us
  transfers between devices with their start and end apart: 11, of which 8 were waited for; matrix products, arithmetic and copies ran while one was open for 17% of the time, Pallas kernels for 0%

commit v1 on v0

v1 whole, which is shorter than its diff:
```python
import functools
import math

import jax
import jax.numpy as jnp
import numpy as np
from jax import lax
from jax.experimental import pallas as pl
from jax.experimental.pallas import tpu as pltpu
from jax.sharding import PartitionSpec as P

H = 256
HEADS = 8
FF = 1024
NB = 600
STEP = 5
HEAD_DIM = 32

EPS = 1e-06
CUTOFF = 6.0
BETA_ONE = 0.5
BETA_TWO = 0.5
ADAM_EPS = 1e-08
DECAY = 0.01

LANES = 128
NB_PAD = 640
NB_ROWS = 768
WIDE = H + NB_PAD
CHUNK = 1024
BLOCK = 128
GROUP = 1024
UNROLL = 16
VMEM_BYTES = 60 * 1024 * 1024

F32 = jnp.float32
BF16 = jnp.bfloat16


def dot_nn(left, right):
    return jnp.dot(left, right, preferred_element_type=F32)


def dot_nt(left, right):
    return lax.dot_general(left, right, (((1,), (1,)), ((), ())), preferred_element_type=F32)


def dot_tn(left, right):
    return lax.dot_general(left, right, (((0,), (0,)), ((), ())), preferred_element_type=F32)


def inverse_rms(rows):
    return lax.rsqrt(jnp.mean(rows * rows, axis=-1, keepdims=True) + EPS)


def edges_forward(order_ref, mine_ref, other_ref, small_ref, dist_ref, src_ref, *rest):
    kept_ref, normed_ref = rest[-2:]
    atoms = mine_ref.shape[0]

    def norm(ref):
        features = ref[...].astype(F32)
        normed_ref[...] = (features * inverse_rms(features) * small_ref[0:1, :]).astype(BF16)

    first = pl.program_id(1) == 0
    pl.when(jnp.logical_and(first, pl.program_id(0) == 0))(lambda: norm(mine_ref))
    pl.when(jnp.logical_and(first, pl.program_id(0) == 1))(lambda: norm(other_ref))
    atom_lane = lax.broadcasted_iota(jnp.int32, (1, atoms), 1).astype(F32)
    centres = lax.broadcasted_iota(jnp.int32, (1, NB_PAD), 1).astype(F32) * (CUTOFF / (NB - 1))
    per_spread = math.sqrt(math.log2(math.e)) / (2.0 * CUTOFF / (NB - 1))
    picks, bases = [], []
    for column in range(dist_ref.shape[3]):
        source = src_ref[0, 0, :, column : column + 1]
        picks.append(jnp.where(source == atom_lane, 1.0, 0.0).astype(BF16))
        offset = (dist_ref[0, 0, :, column : column + 1] - centres) * per_spread
        bases.append(jnp.exp2(-(offset * offset)).astype(BF16))
    kept_ref[:, :H] = dot_nn(jnp.concatenate(picks, axis=0), normed_ref[...]).astype(BF16)
    kept_ref[:, H:] = jnp.concatenate(bases, axis=0)


def atoms_kernel(
    ins, blocks, outs, owners,
    idx_ref, core_ref, kept_ref, x_ref, cot_ref, ecot_ref, count_ref, small_ref,
    wide_ref, query_ref, output_ref, gateup_ref, down_ref,
    block_ref, energy_ref, after_ref, dnorm_ref, drows_ref, mine_ref, theirs_ref,
    rows, stage, products, spread_out, sum_up,
    gwide_ref, ggateup_ref, gdown_ref, goutput_ref, gquery_ref, gsmall_ref,
):
    step = pl.program_id(0)
    scaling = HEAD_DIM ** (-0.5)
    slots = stage.shape[0] // (4 * BLOCK)
    pairs = slots * HEADS

    @pl.when(step == 0)
    def _():
        for ref in (gwide_ref, ggateup_ref, gdown_ref, goutput_ref, gquery_ref, gsmall_ref):
            ref[...] = jnp.zeros_like(ref)
        lane = lax.broadcasted_iota(jnp.int32, (pairs, slots * H), 1) // HEAD_DIM
        pair = lax.broadcasted_iota(jnp.int32, (pairs, slots * H), 0)
        spread_out[...] = jnp.where(lane == pair, 1.0, 0.0).astype(BF16)
        lane = lax.broadcasted_iota(jnp.int32, (slots * H, pairs), 0) // HEAD_DIM
        pair = lax.broadcasted_iota(jnp.int32, (slots * H, pairs), 1)
        sum_up[...] = jnp.where(lane == pair, 1.0, 0.0).astype(BF16)

    @pl.when(step < ins)
    def _():
        base = pl.multiple_of(step * (CHUNK * 4), CHUNK * 4)
        edge_kv = dot_nt(kept_ref[...], wide_ref[...]).astype(BF16).astype(F32)
        for part in range(4):
            rows[pl.ds(base + part, CHUNK, stride=4), :] = edge_kv[
                :, part * LANES : (part + 1) * LANES
            ]

    @pl.when(jnp.logical_and(step >= ins, step < ins + blocks))
    def _():
        block = step - ins
        total = slots * BLOCK
        base = block * total

        def fetch(turn, carry):
            for inner in range(UNROLL):
                row = turn * UNROLL + inner
                at = pl.multiple_of(idx_ref[base + row], 4)
                stage[pl.ds(pl.multiple_of(row * 4, 4), 4), :] = rows[pl.ds(at, 4), :]
            return carry

        lax.fori_loop(0, total // UNROLL, fetch, 0)

        def staged(slot, part):
            first = slot * (4 * BLOCK) + 2 * part
            return jnp.concatenate(
                [stage[pl.ds(first + half, BLOCK, stride=4), :] for half in (0, 1)], axis=1
            )

        def put(slot, part, value):
            first = slot * (4 * BLOCK) + 2 * part
            for half in (0, 1):
                stage[pl.ds(first + half, BLOCK, stride=4), :] = value[
                    :, half * LANES : (half + 1) * LANES
                ]

        def over_slots(values, combine):
            shift = HEADS
            while shift < pairs:
                values = combine(values, pltpu.roll(values, shift, 1))
                shift *= 2
            return values

        def over_features(left, part):
            for slot in range(slots):
                products[:, slot * H : (slot + 1) * H] = (left * staged(slot, part)).astype(BF16)
            return dot_nn(products[...], sum_up[...])

        gain_one = small_ref[0:1, :]
        gain_two = small_ref[1:2, :]
        reader = small_ref[2:3, :]
        features = x_ref[...].astype(F32)
        inv_one = inverse_rms(features)
        normed_one = (features * inv_one * gain_one).astype(BF16)
        queries = dot_nt(normed_one, query_ref[...]).astype(BF16).astype(F32)

        scores = over_features(queries, 0) * scaling
        slot_of = lax.broadcasted_iota(jnp.int32, (1, pairs), 1) // HEADS
        scores = jnp.where(slot_of.astype(F32) < count_ref[...], scores, -1e30)
        terms = jnp.exp(scores - over_slots(scores, jnp.maximum))
        soft = terms / over_slots(terms, jnp.add)
        soft_low = soft.astype(BF16)

        def spread(values, slot):
            return dot_nn(values, spread_out[:, slot * H : (slot + 1) * H])

        mixture = jnp.zeros((BLOCK, H), F32)
        for slot in range(slots):
            mixture += spread(soft_low, slot) * staged(slot, 1)
        mixture = mixture.astype(BF16)

        after = features + dot_nt(mixture, output_ref[...])
        inv_two = inverse_rms(after)
        normed_two = (after * inv_two * gain_two).astype(BF16)
        gate_up = dot_nt(normed_two, gateup_ref[...])
        ff = gate_up.shape[1] // 2
        gate, up_part = gate_up[:, :ff], gate_up[:, ff:]
        gate_sig = 1.0 / (1.0 + jnp.exp(-gate))
        swished = gate * gate_sig
        hidden = (swished * up_part).astype(BF16)
        result = after + dot_nt(hidden, down_ref[...])
        block_ref[...] = result.astype(BF16)
        energy_ref[...] = jnp.broadcast_to(
            jnp.sum(result * reader, axis=-1, keepdims=True), energy_ref.shape
        )
        energy_row = ecot_ref[...]
        d_result = cot_ref[...].astype(F32) + energy_row * reader
        grad_read = jnp.sum(energy_row * result, axis=0, keepdims=True)
        d_ffn = d_result.astype(BF16)
        gdown_ref[...] += dot_tn(d_ffn, hidden)
        d_hidden = dot_nn(d_ffn, down_ref[...])
        d_gate = d_hidden * up_part * gate_sig * (1.0 + gate * (1.0 - gate_sig))
        d_gate_up = jnp.concatenate(
            [d_gate.astype(BF16), (d_hidden * swished).astype(BF16)], axis=1
        )
        ggateup_ref[...] += dot_tn(d_gate_up, normed_two)
        d_normed_two = dot_nn(d_gate_up, gateup_ref[...])
        scaled = d_normed_two * gain_two
        grad_gain_two = jnp.sum(d_normed_two * after * inv_two, axis=0, keepdims=True)
        d_after = (
            d_result
            + inv_two * scaled
            - after * (inv_two * inv_two * inv_two)
            * jnp.mean(scaled * after, axis=-1, keepdims=True)
        )
        after_ref[...] = d_after
        d_attn = d_after.astype(BF16)
        goutput_ref[...] += dot_tn(d_attn, mixture)
        d_mixture = dot_nn(d_attn, output_ref[...]).astype(BF16).astype(F32)

        d_soft = over_features(d_mixture, 1)
        d_scores = soft * (d_soft - over_slots(soft * d_soft, jnp.add))
        d_scores = d_scores.astype(BF16)
        scaled_queries = queries * scaling
        d_queries = jnp.zeros((BLOCK, H), F32)
        for slot in range(slots):
            wide_scores = spread(d_scores, slot)
            d_queries += wide_scores * staged(slot, 0)
            put(slot, 0, wide_scores * scaled_queries)
            put(slot, 1, spread(soft_low, slot) * d_mixture)
        d_queries = (d_queries * scaling).astype(BF16)
        gquery_ref[...] += dot_tn(d_queries, normed_one)
        d_normed = dot_nn(d_queries, query_ref[...])
        dnorm_ref[...] = d_normed
        grad_gain_one = jnp.sum(d_normed * features * inv_one, axis=0, keepdims=True)
        gsmall_ref[0:1, :] += grad_gain_one
        gsmall_ref[1:2, :] += grad_gain_two
        gsmall_ref[2:3, :] += grad_read

        def spill(turn, carry):
            for inner in range(UNROLL):
                row = turn * UNROLL + inner
                at = pl.multiple_of(idx_ref[base + row], 4)
                rows[pl.ds(at, 4), :] = stage[pl.ds(pl.multiple_of(row * 4, 4), 4), :]
            return carry

        lax.fori_loop(0, total // UNROLL, spill, 0)

    @pl.when(step >= ins + blocks)
    def _():
        base = pl.multiple_of((step - ins - blocks) * (CHUNK * 4), CHUNK * 4)
        d_edges = jnp.concatenate(
            [rows[pl.ds(base + part, CHUNK, stride=4), :].astype(BF16) for part in range(4)], axis=1
        )
        gwide_ref[...] += dot_tn(d_edges, kept_ref[...])
        drows_ref[...] = dot_nn(d_edges, wide_ref[:, :H]).astype(BF16)

    @pl.when(step == ins + blocks + outs - 1)
    def _():
        shares = gwide_ref[:, :H] * wide_ref[:, :H].astype(F32)
        gsmall_ref[0:1, :] += jnp.sum(shares, axis=0, keepdims=True) / small_ref[0:1, :]
        size = mine_ref.shape[0]
        height = size // owners
        for owner in range(owners):
            for half in (0, 1):
                at = half * size + owner * height
                for ref, first, count, columns in packed_pieces(
                    owner, owners, gquery_ref, gwide_ref, ggateup_ref, gdown_ref, goutput_ref
                ):
                    for low in range(columns.start + half * LANES, columns.stop, H):
                        if low < ref.shape[1]:
                            rows[at : at + count, :] = ref[
                                first : first + count, low : low + LANES
                            ]
                        at += count
                rows[at : at + 8, :] = gsmall_ref[:, half * LANES : (half + 1) * LANES]
        core = core_ref[0]
        for ref, half in ((mine_ref, core), (theirs_ref, 1 - core)):
            ref[...] = rows[pl.ds(pl.multiple_of(half * size, 8), size), :].astype(BF16)


def packed_pieces(owner, owners, query, wide, gateup, down, output):
    count = 3 * H // owners
    first, last = owner * count, (owner + 1) * count
    if first < H:
        yield query, first, min(last, H) - first, range(H)
    if last > H:
        yield wide, max(first, H) - H, last - max(first, H), range(H)
    share = 2 * H // owners
    yield wide, owner * share, share, range(H, H + NB_ROWS)
    for ref in (gateup, down, output):
        share = ref.shape[0] // owners
        yield ref, owner * share, share, range(ref.shape[1])


def edges_backward(order_ref, rows_ref, src_ref, mine_ref, other_ref):
    d_rows = rows_ref[...]
    source = src_ref[0]
    step = 256

    def sums(ref):
        for start in range(0, ref.shape[0], step):
            atom = lax.broadcasted_iota(jnp.int32, (step, 1), 0).astype(F32) + float(start)
            pick = jnp.where(atom == source, 1.0, 0.0).astype(BF16)
            ref[start : start + step, :] = dot_nn(pick, d_rows).astype(ref.dtype)

    pl.when(pl.program_id(0) == 0)(lambda: sums(mine_ref))
    pl.when(pl.program_id(0) == 1)(lambda: sums(other_ref))


def adamw_step(weight, first_mom, second, gradient, step_rate):
    first_new = BETA_ONE * first_mom + (1.0 - BETA_ONE) * gradient
    second_new = BETA_TWO * second + (1.0 - BETA_TWO) * gradient * gradient
    fix_one = 1.0 - BETA_ONE**STEP
    fix_two = 1.0 - BETA_TWO**STEP
    direction = first_new / fix_one / (jnp.sqrt(second_new / fix_two) + ADAM_EPS) + DECAY * weight
    return (first_new, second_new, weight - step_rate * direction)


def whole_spec(shape):
    return pl.BlockSpec(shape, lambda *_: (0,) * len(shape), pipeline_mode=pl.Buffered(1))


def run_edges_forward(turn, order, mine, other, small, dist_cols, src_cols, before):
    atoms = mine.shape[0]
    owners, groups, _, columns = dist_cols.shape
    size = columns * LANES
    edges = owners * groups * size

    def picked(i, g, order_ref):
        return (order_ref[2 * turn + i], g, 0, 0)

    def written(i, g, order_ref):
        return ((2 * turn + i) * groups + g, 0)

    return pl.pallas_call(
        edges_forward,
        grid_spec=pltpu.PrefetchScalarGridSpec(
            num_scalar_prefetch=1,
            grid=(2, groups),
            in_specs=[
                whole_spec(mine.shape),
                whole_spec(other.shape),
                whole_spec(small.shape),
                pl.BlockSpec((1, 1, LANES, columns), picked),
                pl.BlockSpec((1, 1, LANES, columns), picked),
            ]
            + [pl.BlockSpec(memory_space=pl.ANY)] * len(before),
            out_specs=pl.BlockSpec((size, WIDE), written),
            scratch_shapes=[pltpu.VMEM((atoms, H), BF16)],
        ),
        out_shape=jax.ShapeDtypeStruct((edges, WIDE), BF16),
        input_output_aliases={6: 0} if before else {},
        compiler_params=pltpu.CompilerParams(vmem_limit_bytes=VMEM_BYTES),
        cost_estimate=pl.CostEstimate(
            flops=4 * groups * size * atoms * H,
            bytes_accessed=2 * groups * size * 2 * WIDE + 2 * atoms * H * 2,
            transcendentals=2 * groups * size * NB_PAD,
        ),
    )(order, mine, other, small, dist_cols, src_cols, *before)


def run_atoms(
    owners, idx, core, kept, features, cot, ecot, count, small, wide, query, output, gateup, down
):
    edges, atoms = kept.shape[0], features.shape[0]
    ins, blocks = edges // CHUNK, atoms // BLOCK
    outs = ins
    slots = edges // atoms
    ff = down.shape[1]
    height = (3 * H + 3 * 2 * H + gateup.shape[0] + ff // H * H + H) // owners + 8

    def atom_block(i):
        return (jnp.clip(i - ins, 0, blocks - 1), 0)

    def edge_block(i):
        return (jnp.where(i < ins, i, jnp.maximum(i - ins - blocks, 0)), 0)

    return pl.pallas_call(
        functools.partial(atoms_kernel, ins, blocks, outs, owners),
        grid=(ins + blocks + outs,),
        in_specs=[
            pl.BlockSpec(memory_space=pltpu.SMEM),
            pl.BlockSpec(memory_space=pltpu.SMEM),
            pl.BlockSpec((CHUNK, WIDE), edge_block),
            pl.BlockSpec((BLOCK, H), atom_block),
            pl.BlockSpec((BLOCK, H), atom_block),
            pl.BlockSpec((BLOCK, 1), atom_block),
            pl.BlockSpec((BLOCK, 1), atom_block),
            whole_spec(small.shape),
            whole_spec(wide.shape),
            whole_spec(query.shape),
            whole_spec(output.shape),
            whole_spec(gateup.shape),
            whole_spec(down.shape),
        ],
        out_specs=[
            pl.BlockSpec((BLOCK, H), atom_block),
            pl.BlockSpec((BLOCK, LANES), atom_block),
            pl.BlockSpec((BLOCK, H), atom_block),
            pl.BlockSpec((BLOCK, H), atom_block),
            pl.BlockSpec((CHUNK, H), lambda i: (jnp.maximum(i - ins - blocks, 0), 0)),
            whole_spec((owners * height, LANES)),
            whole_spec((owners * height, LANES)),
        ],
        out_shape=[
            jax.ShapeDtypeStruct((atoms, H), BF16),
            jax.ShapeDtypeStruct((atoms, LANES), F32),
            jax.ShapeDtypeStruct((atoms, H), F32),
            jax.ShapeDtypeStruct((atoms, H), F32),
            jax.ShapeDtypeStruct((edges, H), BF16),
            jax.ShapeDtypeStruct((owners * height, LANES), BF16),
            jax.ShapeDtypeStruct((owners * height, LANES), BF16),
        ],
        scratch_shapes=[
            pltpu.VMEM((edges * 4 + 8, LANES), F32),
            pltpu.VMEM((slots * BLOCK * 4 + 8, LANES), F32),
            pltpu.VMEM((BLOCK, slots * H), BF16),
            pltpu.VMEM((slots * HEADS, slots * H), BF16),
            pltpu.VMEM((slots * H, slots * HEADS), BF16),
            pltpu.VMEM(wide.shape, F32),
            pltpu.VMEM(gateup.shape, F32),
            pltpu.VMEM(down.shape, F32),
            pltpu.VMEM(output.shape, F32),
            pltpu.VMEM(query.shape, F32),
            pltpu.VMEM((8, H), F32),
        ],
        compiler_params=pltpu.CompilerParams(vmem_limit_bytes=VMEM_BYTES),
        cost_estimate=pl.CostEstimate(
            flops=2 * edges * H * (WIDE * 4 + H * 8) + 2 * atoms * H * ff * 9,
            bytes_accessed=edges * WIDE * 4 + edges * H * 2 + ff * H * 3 * 6,
            transcendentals=edges * HEADS,
        ),
    )(idx, core, kept, features, cot, ecot, count, small, wide, query, output, gateup, down)


def run_edges_backward(turn, order, d_rows, src_rows, atoms):
    owners, sent = src_rows.shape[0], src_rows.shape[2]
    return pl.pallas_call(
        edges_backward,
        grid_spec=pltpu.PrefetchScalarGridSpec(
            num_scalar_prefetch=1,
            grid=(2,),
            in_specs=[
                pl.BlockSpec((sent, H), lambda i, order_ref: (2 * turn + i, 0)),
                pl.BlockSpec((1, 1, sent), lambda i, order_ref: (order_ref[2 * turn + i], 0, 0)),
            ],
            out_specs=[whole_spec((atoms, H)), whole_spec((atoms, H))],
        ),
        out_shape=[jax.ShapeDtypeStruct((atoms, H), BF16)] * 2,
        compiler_params=pltpu.CompilerParams(vmem_limit_bytes=VMEM_BYTES),
        cost_estimate=pl.CostEstimate(
            flops=4 * sent * atoms * H,
            bytes_accessed=2 * sent * 2 * H + 4 * atoms * H,
            transcendentals=0,
        ),
    )(order, d_rows, src_rows)


def halves(axis_size):
    return range((axis_size - 1).bit_length())


def across(array, bit):
    size = lax.axis_size("rep")
    return lax.ppermute(array, "rep", [(r, r ^ (1 << bit)) for r in range(size)])


def gather_rows(rows):
    owners, reps = lax.axis_size("edge"), lax.axis_size("rep")
    me = lax.axis_index("rep")
    share = rows.shape[0] // reps
    part = lax.dynamic_slice_in_dim(rows, me * share, share, 0)
    held = lax.all_to_all(
        jnp.broadcast_to(part[None], (owners, share, H)), "edge", 0, 0, tiled=True
    )
    for bit in reversed(halves(reps)):
        fetched = across(held, bit)
        upper = (me >> bit) & 1 == 1
        held = jnp.stack([jnp.where(upper, fetched, held), jnp.where(upper, held, fetched)])
    bits = len(halves(reps))
    held = held.transpose((bits,) + tuple(reversed(range(bits))) + (bits + 1, bits + 2))
    return held.reshape(owners, reps * share, H)


def reduce_rows(mine, theirs):
    owners, reps = lax.axis_size("edge"), lax.axis_size("rep")
    me = lax.axis_index("rep")
    totals = mine.astype(F32) + across(theirs, 0).astype(F32)
    totals = totals.reshape(owners, -1, LANES)
    for bit in halves(reps)[1:]:
        half = totals.shape[1] // 2
        upper = (me >> bit) & 1
        sent = lax.dynamic_slice_in_dim(totals, (1 - upper) * half, half, 1)
        kept = lax.dynamic_slice_in_dim(totals, upper * half, half, 1)
        totals = kept + across(sent.astype(BF16), bit).astype(F32)
    pieces = lax.all_to_all(totals.astype(BF16), "edge", 0, 0, tiled=True)
    held = jnp.sum(pieces.astype(F32), axis=0)
    for bit in reversed(halves(reps)):
        fetched = across(held, bit)
        upper = (me >> bit) & 1 == 1
        held = jnp.concatenate(
            [jnp.where(upper, fetched, held), jnp.where(upper, held, fetched)],
            axis=0 if bit > 0 else 1,
        )
    return held


def ring_of(owners):
    pairs = owners // 2
    return [*range(0, pairs, 2), *reversed(range(1, pairs, 2))]


def ring_step(array):
    owners = lax.axis_size("edge")
    ring = ring_of(owners)
    moves = [
        (2 * here + side, 2 * ring[(at + 1) % len(ring)] + side)
        for at, here in enumerate(ring)
        for side in (0, 1)
    ]
    return lax.ppermute(array, "edge", moves)


def pair_swap(array):
    owners = lax.axis_size("edge")
    return lax.ppermute(array, "edge", [(e, e ^ 1) for e in range(owners)])


def arrival_order(owners):
    ring = ring_of(owners)
    table = np.zeros((owners, owners), np.int32)
    for at, here in enumerate(ring):
        for side in (0, 1):
            for turn in range(len(ring)):
                source = 2 * ring[at - turn]
                table[2 * here + side, 2 * turn : 2 * turn + 2] = (source + side, source + 1 - side)
    return table


def pad_rows(array, multiple):
    short = -array.shape[0] % multiple
    return jnp.pad(array, ((0, short), (0, 0)))


def unstack(pieces, rows, width):
    return pieces.reshape(width // H, rows, H).transpose(1, 0, 2).reshape(rows, width)


def local(
    atom_features,
    distances,
    source_index,
    slot_index,
    live_mask,
    output_cot,
    energy_cot,
    attention_weight,
    attention_first,
    attention_second,
    output_weight,
    output_first,
    output_second,
    gateup_weight,
    gateup_first,
    gateup_second,
    down_weight,
    down_first,
    down_second,
    basis_weight,
    basis_first,
    basis_second,
    readout_weight,
    readout_first,
    readout_second,
    norm_gains,
    gains_first,
    gains_second,
):
    features = atom_features[0]
    atoms = features.shape[0]
    slots = slot_index.shape[2]
    edges = atoms * slots
    owners = H // output_weight.shape[1]
    sent = edges // owners
    wa, wo, wg, wd, wb, wr = (
        attention_weight.shape[1],
        output_weight.shape[1],
        gateup_weight.shape[1],
        down_weight.shape[1],
        basis_weight.shape[1],
        readout_weight.shape[0],
    )

    dist = distances[0]
    high = lax.reduce_precision(dist, 8, 7)
    middle = lax.reduce_precision(dist - high, 8, 7)
    lower = dist - high - middle
    source = source_index[0]
    pieces = (high, middle, lower, source >> 5, source & 31)
    meta = jnp.stack([piece.astype(BF16) for piece in pieces])
    meta = meta.reshape(5, owners, sent // H, H).transpose(1, 0, 2, 3)
    meta_rows = 5 * sent // H
    thin = jnp.concatenate([norm_gains, readout_weight[None]], axis=0).astype(BF16).reshape(1, 1, -1)
    thin = jnp.broadcast_to(
        jnp.pad(thin, ((0, 0), (0, 7), (0, H - thin.shape[2]))), (owners, 8, H)
    )
    meta = jnp.concatenate([meta.reshape(owners, meta_rows, H), thin], axis=1)
    meta = lax.all_to_all(meta, "edge", 0, 0, tiled=True)
    small = meta[:, meta_rows, : 3 * wr].reshape(owners, 3, wr)
    small = small.transpose(1, 0, 2).reshape(3, H)
    small = jnp.pad(small.astype(F32), ((0, 5), (0, 0)))
    pieces = meta[:, :meta_rows].reshape(owners, 5, sent).astype(F32)
    dist = pieces[:, 0] + pieces[:, 1] + pieces[:, 2]
    source = pieces[:, 3] * 32.0 + pieces[:, 4]

    basis_rows = jnp.pad(basis_weight.T.astype(BF16), ((0, 0), (0, NB_ROWS - NB)))
    weight_rows = pad_rows(
        jnp.concatenate(
            [
                attention_weight.T.astype(BF16),
                basis_rows.reshape(3 * wb, H),
                gateup_weight.T.astype(BF16),
                down_weight.T.astype(BF16).reshape(wd * (FF // H), H),
                output_weight.T.astype(BF16),
            ],
            axis=0,
        ),
        8 * lax.axis_size("rep"),
    )
    weight_rows, meta = lax.optimization_barrier((weight_rows, meta))
    weight_rows = gather_rows(weight_rows)
    at = 0
    fulls = []
    for width, rows in ((H, wa), (NB_ROWS, wb), (H, wg), (FF, wd), (H, wo)):
        count = rows * width // H
        fulls.append(weight_rows[:, at : at + count].reshape(owners * rows, width))
        at += count
    attention_rows, basis_rows, gateup_rows, down_rows, output_rows = fulls
    query_rows, kv_rows = attention_rows[:H], attention_rows[H:]
    wide = jnp.concatenate([kv_rows, basis_rows[:, :NB_PAD]], axis=1)

    size = min(GROUP, sent)
    dist_cols, src_cols = (
        values.reshape(owners, sent // size, size // LANES, LANES).transpose(0, 1, 3, 2)
        for values in (dist, source)
    )
    src_rows = source[:, None]

    table = arrival_order(owners)
    me = lax.axis_index("edge")
    order = jnp.asarray(table)[me]
    place = jnp.asarray(np.argsort(table, axis=1).astype(np.int32))[me]
    turns = owners // 2
    mine, before = features, ()
    for turn in range(turns):
        if turn > 0:
            mine = ring_step(mine)
        before = (
            run_edges_forward(
                turn, order, mine, pair_swap(mine), small, dist_cols, src_cols, before
            ),
        )
    (kept,) = before

    slot_ids = slot_index[0]
    slot_owner = slot_ids // sent
    arrived = sum(jnp.where(slot_owner == s, place[s], 0) for s in range(owners))
    arrived = arrived * sent + slot_ids % sent
    idx = arrived.reshape(atoms // BLOCK, BLOCK, slots).transpose(0, 2, 1).reshape(-1) * 4
    count = jnp.sum(live_mask[0], axis=1, keepdims=True).astype(F32)
    core = (lax.axis_index("rep") & 1).astype(jnp.int32)[None]
    block_out, energy, d_after, d_normed_own, d_rows, grads_mine, grads_theirs = run_atoms(
        owners,
        idx,
        core,
        kept,
        features,
        output_cot[0],
        energy_cot[0][:, None],
        count,
        small,
        wide,
        query_rows,
        output_rows,
        gateup_rows,
        down_rows,
    )
    shard = reduce_rows(grads_mine, grads_theirs)

    running = None
    for turn in [*range(1, turns), 0]:
        part, part_other = run_edges_backward(turn, order, d_rows, src_rows, atoms)
        total = part.astype(F32) + pair_swap(part_other).astype(F32)
        if running is not None:
            total = total + ring_step(running).astype(F32)
        running = total.astype(BF16)
    d_from_edges = total

    features = features.astype(F32)
    inv_one = inverse_rms(features)
    d_normed_one = d_normed_own + d_from_edges
    scaled = d_normed_one * small[0:1]
    input_grad = (
        d_after
        + inv_one * scaled
        - features * inv_one**3 * jnp.mean(scaled * features, axis=-1, keepdims=True)
    )

    cuts = np.cumsum([wa, 3 * wb, wg, wd * (FF // H), wo])
    thin_shard = lax.dynamic_slice_in_dim(shard[cuts[4] : cuts[4] + 3], me * wr, wr, 1)
    gradients = (
        shard[: cuts[0]].T,
        shard[cuts[3] : cuts[4]].T,
        shard[cuts[1] : cuts[2]].T,
        unstack(shard[cuts[2] : cuts[3]], wd, FF).T,
        unstack(shard[cuts[0] : cuts[1]], wb, NB_ROWS)[:, :NB].T,
        thin_shard[2],
        thin_shard[:2],
    )
    step_rates = (
        H ** (-0.5),
        (H // 16) ** (-0.5),
        H ** (-0.5),
        FF ** (-0.5),
        0.5,
        H ** (-0.5),
        0.2,
    )
    masters = (
        attention_weight,
        output_weight,
        gateup_weight,
        down_weight,
        basis_weight,
        readout_weight,
        norm_gains,
    )
    firsts = (
        attention_first,
        output_first,
        gateup_first,
        down_first,
        basis_first,
        readout_first,
        gains_first,
    )
    seconds = (
        attention_second,
        output_second,
        gateup_second,
        down_second,
        basis_second,
        readout_second,
        gains_second,
    )
    updated = [
        adamw_step(
            masters[number], firsts[number], seconds[number], gradients[number], step_rates[number]
        )
        for number in range(7)
    ]
    flat = [array for triple in updated for array in triple]
    lows = [updated[number][2].astype(BF16) for number in range(5)]
    return (block_out[None], energy[:, 0][None], input_grad[None], *flat, *lows)


def solution(mesh):
    matrix = P(None, "edge")
    rows = P("rep", "edge", None)
    pairs = P("rep", "edge")
    weights = (matrix,) * 15 + (P("edge"),) * 3 + (matrix,) * 3
    return jax.shard_map(
        local,
        mesh=mesh,
        in_specs=(rows, pairs, pairs, rows, rows, rows, pairs) + weights,
        out_specs=(rows, pairs, rows) + weights + (matrix,) * 5,
        check_vma=False,
    )
```

time: 2030 us -> 360 us (0.18)
  waiting for transfers between devices: 700 us -> 37.2 us
  blocking collectives: 523 us -> 21.5 us
  other arithmetic: 352 us -> 33 us
  local copies, waits for them, and re-layouts: 312 us -> 29.3 us
  Pallas kernels: 0 us -> 197 us
  matrix products: 106 us -> 0 us
  starting transfers between devices: 12.3 us -> 38.2 us
    all_to_all x2, waiting for transfers between devices: 335 us -> 6.92 us  [the longest x1 6.91 us: local(): meta = lax.all_to_all(meta, 'edge', 0, 0, tiled=True)]
    unnamed x1 -> x0, blocking collectives: 281 us -> none
    reduce_scatter x4 -> x0, waiting for transfers between devices: 255 us -> none  [the longest x1 71.2 us: local(): lax.psum_scatter(totals[2], 'edge', scatter_dimension=1, tiled=True)]
    all_gather x5 -> x0, blocking collectives: 232 us -> none  [the longest x1 115 us: local(): lax.all_gather(output_weight.astype(jnp.bfloat16), 'edge', axis=1, tiled=...]
    scatter-add x2 -> x0, other arithmetic: 201 us -> none  [the longest x1 112 us: local(): jnp.zeros((received.shape[0], 2 * model_width), jnp.float32).at[slot_ids]]
    pallas_call x0 -> x9, Pallas kernels: none -> 197 us  [the longest x1 140 us: run_atoms(): pl.pallas_call(functools.partial(atoms_kernel, ins, blocks, outs, owners)...]
    gather x2 -> x0, local copies, waits for them, and re-layouts: 139 us -> none  [the longest x1 74.5 us: local(): paired = received[slot_ids].reshape(atom_count, neighbours, 2 * model_width)]
    dot_general x17 -> x0, matrix products: 106 us -> none  [the longest x1 22.3 us: local(): jnp.dot(kept_radial, proj_basis, preferred_element_type=jnp.float32)]
  transfers between devices with their start and end apart: 11 -> 22, of which waited for: 8 -> 7; matrix products, arithmetic and copies ran while one was open for 17% -> 11% of each run, Pallas kernels for 0% -> 16%
where the time goes in v1:
time: 360 us; the launch traced here: 357 us
  Pallas kernels  197 us (55%)
  starting transfers between devices  38.2 us (11%)
  waiting for transfers between devices  37.2 us (10%)
  other arithmetic  33 us (9%)
  local copies, waits for them, and re-layouts  29.3 us (8%)
  blocking collectives  21.5 us (6%)
    pallas_call x1, Pallas kernels, run_atoms(): pl.pallas_call(functools.partial(atoms_kernel, ins, blocks, outs, owners)...  140 us
    pallas_call x4, Pallas kernels, run_edges_forward(): pl.pallas_call(edges_forward, grid_spec=pltpu.PrefetchScalarGridSpec(num_...  33.8 us
    ppermute x6, waiting for transfers between devices, ring_step(): return lax.ppermute(array, 'edge', moves)  26.8 us
    pallas_call x4, Pallas kernels, run_edges_backward(): pl.pallas_call(edges_backward, grid_spec=pltpu.PrefetchScalarGridSpec(num...  22.5 us
    all_to_all x1, blocking collectives, gather_rows(): lax.all_to_all(jnp.broadcast_to(part[None], (owners, share, H)), 'edge',...  21.5 us
    ppermute x6, starting transfers between devices, ring_step(): return lax.ppermute(array, 'edge', moves)  15.6 us
    unnamed x95, local copies, waits for them, and re-layouts  11.9 us
    ppermute x8, starting transfers between devices, pair_swap(): return lax.ppermute(array, 'edge', [(e, e ^ 1) for e in range(owners)])  8.96 us
  transfers between devices with their start and end apart: 22, of which 7 were waited for; matrix products, arithmetic and copies ran while one was open for 11% of the time, Pallas kernels for 16%

profile of v1, /device:TPU:0, one launch (start us, length us, event | category | flops | bytes accessed | tf_op | source)
XLA Modules:
  0.0 357.4 jit_solution(7992012423347313617)
XLA Ops:
  5.7 7.3 %all-to-all-start = ((bf16[8,48,256]{2,1,0:T(8,128)(2,1)}), bf16[8,48,256]{2,1,0:T(8,128)(2,1)S(1)}, u32[]{:S(2)}, u32[]{:S(2)}) async-start(bf16[8,48,256]{2,1,0:T(8,128)(2,1)} %pad_maximum_fusion.4), calls=%async_computation | async-start | bytes 393216 | tf_op jit(solution)/shard_map/all_to_all | solution.py:603
  14.0 6.9 %all-to-all-done = bf16[8,48,256]{2,1,0:T(8,128)(2,1)S(1)} async-done(((bf16[8,48,256]{2,1,0:T(8,128)(2,1)}), bf16[8,48,256]{2,1,0:T(8,128)(2,1)S(1)}, u32[]{:S(2)}, u32[]{:S(2)}) %all-to-all-start) | async-done | bytes 196640 | tf_op jit(solution)/shard_map/all_to_all | solution.py:603
  21.7 21.5 %all_to_all.15 = bf16[8,176,256]{2,1,0:T(8,128)(2,1)S(1)} all-to-all(bf16[8,176,256]{2,1,0:T(8,128)(2,1)S(1)} %broadcast_in_dim.76), channel_id=1, replica_groups=mesh['edge'=8,'rep'=4] {'edge'}, dimensions={0} | all-to-all | bytes 1441792 | tf_op jit(solution)/shard_map/all_to_all | solution.py:468
  47.4 5.3 %fusion.19 = s32[8,16,128]{2,0,1:T(8,128)S(1)} fusion(s32[2,8,8,128]{3,2,1,0:T(8,128)S(1)} %copy.212, s32[]{:T(128)} %bitcast.7, s32[]{:T(128)} %bitcast.6, s32[]{:T(128)} %bitcast.5, s32[]{:T(128)} %bitcast.4, s32[]{:T(128)} %bitcast.3, s32[]{:T(128)} %bitcast.2, s32[]{:T(128)} %bitcast.1, s32[]{:T(128)} %bitcast), kind=kLoop, calls=%fused_computation.77 | loop fusion | flops 737280 | bytes 131104 | tf_op jit(solution)/shard_map/mul | solution.py:664
  56.6 2.5 collective-permute-start.1
  61.0 1.9 collective-permute-start.5
  62.9 6.1 %collective-permute-done.1.mine_ref = bf16[1024,256]{1,0:T(8,128)(2,1)} collective-permute-done((bf16[1024,256]{1,0:T(8,128)(2,1)}, bf16[1024,256]{1,0:T(8,128)(2,1)}, u32[]{:S(2)}, u32[]{:S(2)}) %collective-permute-start.1) | collective-permute-done | bytes 524320 | tf_op jit(solution)/shard_map/ppermute | solution.py:516
  69.0 3.2 collective-permute-start.2
  76.2 4.7 %collective-permute-done.2.mine_ref = bf16[1024,256]{1,0:T(8,128)(2,1)} collective-permute-done((bf16[1024,256]{1,0:T(8,128)(2,1)}, bf16[1024,256]{1,0:T(8,128)(2,1)}, u32[]{:S(2)}, u32[]{:S(2)}) %collective-permute-start.2) | collective-permute-done | bytes 524320 | tf_op jit(solution)/shard_map/ppermute | solution.py:516
  81.7 8.4 %shard_map.509.rest_0_ = bf16[16384,896]{1,0:T(8,128)(2,1)} custom-call(s32[8]{0:T(128)} %fusion.28.order_ref, bf16[1024,256]{1,0:T(8,128)(2,1)} %bitcast.144, bf16[1024,256]{1,0:T(8,128)(2,1)} %collective-permute-done.6.other_ref, f32[8,256]{1,0:T(8,128)} %pad.13.small_ref, f32[8,2,128,8]{3,2,1,0:T(8,128)} %bitcast.129, f32[8,2,128,8]{3,2,1,0:T(8,128)} %bitcast.133), custom_call_target="tpu_custom_call" | custom-call | flops 2147483648 | bytes 8388608 | tf_op jit(solution)/shard_map/pallas_call | solution.py:330
  90.1 8.4 %shard_map.510.rest_0_ = bf16[16384,896]{1,0:T(8,128)(2,1)} custom-call(s32[8]{0:T(128)} %fusion.28.order_ref, bf16[1024,256]{1,0:T(8,128)(2,1)} %collective-permute-done.mine_ref, bf16[1024,256]{1,0:T(8,128)(2,1)} %collective-permute-done.5.other_ref, f32[8,256]{1,0:T(8,128)} %pad.13.small_ref, ...), custom_call_target="tpu_custom_call", output_to_operand_aliasing={{}: (6, {})} | custom-call | flops 2147483648 | bytes 8388608 | tf_op jit(solution)/shard_map/pallas_call | solution.py:330
  98.5 8.4 %shard_map.511.rest_0_ = bf16[16384,896]{1,0:T(8,128)(2,1)} custom-call(s32[8]{0:T(128)} %fusion.28.order_ref, bf16[1024,256]{1,0:T(8,128)(2,1)} %collective-permute-done.1.mine_ref, bf16[1024,256]{1,0:T(8,128)(2,1)} %collective-permute-done.4.other_ref, f32[8,256]{1,0:T(8,128)} %pad.13.small_ref, ...), custom_call_target="tpu_custom_call", output_to_operand_aliasing={{}: (6, {})} | custom-call | flops 2147483648 | bytes 8388608 | tf_op jit(solution)/shard_map/pallas_call | solution.py:330
  107.8 8.5 %shard_map.512.kept_ref = bf16[16384,896]{1,0:T(8,128)(2,1)} custom-call(s32[8]{0:T(128)} %fusion.28.order_ref, bf16[1024,256]{1,0:T(8,128)(2,1)} %collective-permute-done.2.mine_ref, bf16[1024,256]{1,0:T(8,128)(2,1)} %copy-done.16, f32[8,256]{1,0:T(8,128)} %pad.13.small_ref, f32[8,2,128,8]{3,2,1,0:T(8,128)} %bitcast.132, ...), custom_call_target="tpu_custom_call", output_to_operand_aliasing={{}: (6, {})} | custom-call | flops 2147483648 | bytes 8388608 | tf_op jit(solution)/shard_map/pallas_call | solution.py:330
  123.2 140.5 %shard_map.513 = (bf16[1024,256]{1,0:T(8,128)(2,1)}, f32[1024,128]{1,0:T(8,128)}, f32[1024,256]{1,0:T(8,128)}, f32[1024,256]{1,0:T(8,128)}, bf16[16384,256]{1,0:...) custom-call(s32[16384]{0:T(1024)} %bitcast.162, s32[1]{0:T(128)} %bitcast.10.core_ref, ...), custom_call_target="tpu_custom_call" | custom-call | flops 52076478464 | bytes 71827456 | tf_op jit(solution)/shard_map/pallas_call | solution.py:373
  263.7 5.6 %shard_map.517 = (bf16[1024,256]{1,0:T(8,128)(2,1)}, bf16[1024,256]{1,0:T(8,128)(2,1)}) custom-call(s32[8]{0:T(128)} %fusion.28.order_ref, bf16[16384,256]{1,0:T(8,128)(2,1)} %get-tuple-element.50.rows_ref, f32[8,1,2048]{2,1,0:T(1,128)} %copy-done.3), custom_call_target="tpu_custom_call" | custom-call | flops 2147483648 | bytes 3145728 | tf_op jit(solution)/shard_map/pallas_call | solution.py:433
  271.7 2.1 convert_add_fusion
  274.7 5.8 %shard_map.516 = (bf16[1024,256]{1,0:T(8,128)(2,1)}, bf16[1024,256]{1,0:T(8,128)(2,1)}) custom-call(s32[8]{0:T(128)} %fusion.28.order_ref, bf16[16384,256]{1,0:T(8,128)(2,1)} %get-tuple-element.50.rows_ref, f32[8,1,2048]{2,1,0:T(1,128)} %copy-done.3), custom_call_target="tpu_custom_call" | custom-call | flops 2147483648 | bytes 3145728 | tf_op jit(solution)/shard_map/pallas_call | solution.py:433
  281.3 3.0 collective-permute-done.12
  284.4 2.2 add_convert_fusion.2
  286.5 2.6 collective-permute-start.13
  289.1 5.6 %shard_map.515 = (bf16[1024,256]{1,0:T(8,128)(2,1)}, bf16[1024,256]{1,0:T(8,128)(2,1)}) custom-call(s32[8]{0:T(128)} %fusion.28.order_ref, bf16[16384,256]{1,0:T(8,128)(2,1)} %get-tuple-element.50.rows_ref, f32[8,1,2048]{2,1,0:T(1,128)} %copy-done.3), custom_call_target="tpu_custom_call" | custom-call | flops 2147483648 | bytes 3145728 | tf_op jit(solution)/shard_map/pallas_call | solution.py:433
  294.7 2.1 collective-permute-start.10
  299.3 3.5 all-to-all-start.2
  304.2 2.9 collective-permute-start.14
  307.1 5.6 %shard_map.514 = (bf16[1024,256]{1,0:T(8,128)(2,1)}, bf16[1024,256]{1,0:T(8,128)(2,1)}) custom-call(s32[8]{0:T(128)} %fusion.28.order_ref, bf16[16384,256]{1,0:T(8,128)(2,1)} %get-tuple-element.50.rows_ref, f32[8,1,2048]{2,1,0:T(1,128)} %copy-done.3), custom_call_target="tpu_custom_call" | custom-call | flops 2147483648 | bytes 3145728 | tf_op jit(solution)/shard_map/pallas_call | solution.py:433
  314.1 11.2 %collective-permute-done.14 = bf16[1024,256]{1,0:T(8,128)(2,1)S(1)} collective-permute-done((bf16[1024,256]{1,0:T(8,128)(2,1)S(1)}, bf16[1024,256]{1,0:T(8,128)(2,1)S(1)}, u32[]{:S(2)}, u32[]{:S(2)}) %collective-permute-start.14) | collective-permute-done | bytes 524320 | tf_op jit(solution)/shard_map/ppermute | solution.py:516
  325.3 2.0 add_convert_fusion
  327.3 3.4 collective-permute-start.15
  330.7 1.8 copy.202
  336.2 1.8 slice_reduce_fusion
  338.7 4.9 %collective-permute-done.15 = bf16[1024,256]{1,0:T(8,128)(2,1)} collective-permute-done((bf16[1024,256]{1,0:T(8,128)(2,1)}, bf16[1024,256]{1,0:T(8,128)(2,1)}, u32[]{:S(2)}, u32[]{:S(2)}) %collective-permute-start.15) | collective-permute-done | bytes 524320 | tf_op jit(solution)/shard_map/ppermute | solution.py:516
  346.4 2.5 fusion.4
  (214 shorter events, 53.9 us)
Async XLA Ops:
  0.7 12.4 %copy-start.26 = (f32[256,32]{0,1:T(8,128)S(1)}, f32[256,32]{0,1:T(8,128)}, u32[]{:S(2)}) copy-start(f32[256,32]{0,1:T(8,128)} %param.40) | copy-start | bytes 98308
  5.7 15.2 %all-to-all-start = ((bf16[8,48,256]{2,1,0:T(8,128)(2,1)}), bf16[8,48,256]{2,1,0:T(8,128)(2,1)S(1)}, u32[]{:S(2)}, u32[]{:S(2)}) async-start(bf16[8,48,256]{2,1,0:T(8,128)(2,1)} %pad_maximum_fusion.4), calls=%async_computation | async-start | bytes 393216 | tf_op jit(solution)/shard_map/all_to_all | solution.py:603
  14.0 30.7 %copy-start = (bf16[1,1024,256]{2,1,0:T(8,128)(2,1)S(1)}, bf16[1,1024,256]{2,1,0:T(8,128)(2,1)}, u32[]{:S(2)}) copy-start(bf16[1,1024,256]{2,1,0:T(8,128)(2,1)} %param.30) | copy-start | bytes 1572868
  14.0 32.0 %copy-start.30 = (s32[1,1024,16]{1,2,0:T(8,128)S(1)}, s32[1,1024,16]{1,2,0:T(8,128)}, u32[]{:S(2)}) copy-start(s32[1,1024,16]{1,2,0:T(8,128)} %param.33) | copy-start | bytes 196612
  21.1 32.2 %copy-start.34 = (f32[1,1024]{1,0:T(1,128)S(1)}, f32[1,1024]{1,0:T(1,128)}, u32[]{:S(2)}) copy-start(f32[1,1024]{1,0:T(1,128)} %param.36) | copy-start | bytes 12292
  21.6 32.7 %copy-start.31 = (s32[1,1024,16]{1,2,0:T(8,128)S(1)}, s32[1,1024,16]{1,2,0:T(8,128)}, u32[]{:S(2)}) copy-start(s32[1,1024,16]{1,2,0:T(8,128)} %param.34) | copy-start | bytes 196612
  43.2 16.3 %collective-permute-start.7 = (bf16[8,176,256]{2,1,0:T(8,128)(2,1)S(1)}, bf16[8,176,256]{2,1,0:T(8,128)(2,1)S(1)}, u32[]{:S(2)}, u32[]{:S(2)}) collective-permute-start(bf16[8,176,256]{2,1,0:T(8,128)(2,1)S(1)} %all_to_all.15), channel_id=1, source_target_pairs={{0,2},{1,3},{2,0},{3,1},{4,6},{5,7},{6,4},{7,5},{8,10},{9,11},{10,... | collective-permute-start | bytes 2162696 | tf_op jit(solution)/shard_map/ppermute | solution.py:460
  44.7 11.9 %collective-permute-start = (bf16[1024,256]{1,0:T(8,128)(2,1)S(1)}, bf16[1024,256]{1,0:T(8,128)(2,1)}, u32[]{:S(2)}, u32[]{:S(2)}) collective-permute-start(bf16[1024,256]{1,0:T(8,128)(2,1)S(1)} %bitcast.146), channel_id=1, source_target_pairs={{0,16},{4,20},{16,24},{20,28},{24,8},{28,12},{8,0},{12,4},{1,17},{... | collective-permute-start | bytes 1572872 | tf_op jit(solution)/shard_map/ppermute | solution.py:516
  45.7 36.0 %collective-permute-start.6 = (bf16[1024,256]{1,0:T(8,128)(2,1)S(1)}, bf16[1024,256]{1,0:T(8,128)(2,1)}, u32[]{:S(2)}, u32[]{:S(2)}) collective-permute-start(bf16[1024,256]{1,0:T(8,128)(2,1)S(1)} %bitcast.147), channel_id=1, source_target_pairs={{0,4},{4,0},{8,12},{12,8},{16,20},{20,16},{24,28},{28,24},{1,5},{5... | collective-permute-start | bytes 1572872 | tf_op jit(solution)/shard_map/ppermute | solution.py:521
  56.6 12.3 %collective-permute-start.1 = (bf16[1024,256]{1,0:T(8,128)(2,1)}, bf16[1024,256]{1,0:T(8,128)(2,1)}, u32[]{:S(2)}, u32[]{:S(2)}) collective-permute-start(bf16[1024,256]{1,0:T(8,128)(2,1)} %collective-permute-done.mine_ref), channel_id=1, source_target_pairs={{0,16},{4,20},{16,24},{20,28},{24,8},{28,12},{8,0},{12,4},{1,17},{... | collective-permute-start | bytes 1572872 | tf_op jit(solution)/shard_map/ppermute | solution.py:516
  60.9 55.4 %collective-permute-start.8 = (bf16[2,8,176,256]{3,2,0,1:T(8,128)(2,1)}, bf16[2,8,176,256]{3,2,0,1:T(8,128)(2,1)}, u32[]{:S(2)}, u32[]{:S(2)}) collective-permute-start(bf16[2,8,176,256]{3,2,0,1:T(8,128)(2,1)} %pad_maximum_fusion.1), channel_id=1, source_target_pairs={{0,1},{1,0},{2,3},{3,2},{4,5},{5,4},{6,7},{7,6},{8,9},{9,8},{10,11... | collective-permute-start | bytes 4325384 | tf_op jit(solution)/shard_map/ppermute | solution.py:460
  61.0 29.1 %collective-permute-start.5 = (bf16[1024,256]{1,0:T(8,128)(2,1)}, bf16[1024,256]{1,0:T(8,128)(2,1)}, u32[]{:S(2)}, u32[]{:S(2)}) collective-permute-start(bf16[1024,256]{1,0:T(8,128)(2,1)} %collective-permute-done.mine_ref), channel_id=1, source_target_pairs={{0,4},{4,0},{8,12},{12,8},{16,20},{20,16},{24,28},{28,24},{1,5},{5... | collective-permute-start | bytes 1572872 | tf_op jit(solution)/shard_map/ppermute | solution.py:521
  69.0 11.9 %collective-permute-start.2 = (bf16[1024,256]{1,0:T(8,128)(2,1)}, bf16[1024,256]{1,0:T(8,128)(2,1)}, u32[]{:S(2)}, u32[]{:S(2)}) collective-permute-start(bf16[1024,256]{1,0:T(8,128)(2,1)} %collective-permute-done.1.mine_ref), channel_id=1, source_target_pairs={{0,16},{4,20},{16,24},{20,28},{24,8},{28,12},{8,0},{12,4},{1,17},{... | collective-permute-start | bytes 1572872 | tf_op jit(solution)/shard_map/ppermute | solution.py:516
  72.2 26.4 %collective-permute-start.4 = (bf16[1024,256]{1,0:T(8,128)(2,1)}, bf16[1024,256]{1,0:T(8,128)(2,1)}, u32[]{:S(2)}, u32[]{:S(2)}) collective-permute-start(bf16[1024,256]{1,0:T(8,128)(2,1)} %collective-permute-done.1.mine_ref), channel_id=1, source_target_pairs={{0,4},{4,0},{8,12},{12,8},{16,20},{20,16},{24,28},{28,24},{1,5},{5... | collective-permute-start | bytes 1572872 | tf_op jit(solution)/shard_map/ppermute | solution.py:521
  72.8 17.3 %copy-start.3 = (f32[8,1,2048]{2,1,0:T(1,128)}, f32[8,1,2048]{2,1,0:T(1,128)S(1)}, u32[]{:S(2)}) copy-start(f32[8,1,2048]{2,1,0:T(1,128)S(1)} %get-tuple-element.273.src_ref) | copy-start | bytes 196612
  80.9 26.1 %collective-permute-start.3 = (bf16[1024,256]{1,0:T(8,128)(2,1)}, bf16[1024,256]{1,0:T(8,128)(2,1)S(1)}, u32[]{:S(2)}, u32[]{:S(2)}) collective-permute-start(bf16[1024,256]{1,0:T(8,128)(2,1)} %collective-permute-done.2.mine_ref), channel_id=1, source_target_pairs={{0,4},{4,0},{8,12},{12,8},{16,20},{20,16},{24,28},{28,24},{1,5},{5... | collective-permute-start | bytes 1572872 | tf_op jit(solution)/shard_map/ppermute | solution.py:521
  263.7 6.9 %collective-permute-start.16 = (bf16[5696,128]{1,0:T(8,128)(2,1)}, bf16[5696,128]{1,0:T(8,128)(2,1)S(1)}, u32[]{:S(2)}, u32[]{:S(2)}) collective-permute-start(bf16[5696,128]{1,0:T(8,128)(2,1)} %get-tuple-element.60), channel_id=1, source_target_pairs={{0,1},{1,0},{2,3},{3,2},{4,5},{5,4},{6,7},{7,6},{8,9},{9,8},{10,11... | collective-permute-start | bytes 4374536 | tf_op jit(solution)/shard_map/ppermute | solution.py:460
  269.3 15.0 %collective-permute-start.12 = (bf16[1024,256]{1,0:T(8,128)(2,1)}, bf16[1024,256]{1,0:T(8,128)(2,1)}, u32[]{:S(2)}, u32[]{:S(2)}) collective-permute-start(bf16[1024,256]{1,0:T(8,128)(2,1)} %get-tuple-element.58), channel_id=1, source_target_pairs={{0,4},{4,0},{8,12},{12,8},{16,20},{20,16},{24,28},{28,24},{1,5},{5... | collective-permute-start | bytes 1572872 | tf_op jit(solution)/shard_map/ppermute | solution.py:521
  274.1 22.7 %collective-permute-start.17 = (bf16[8,356,128]{2,0,1:T(8,128)(2,1)S(1)}, bf16[8,356,128]{2,0,1:T(8,128)(2,1)}, u32[]{:S(2)}, u32[]{:S(2)}) collective-permute-start(bf16[8,356,128]{2,0,1:T(8,128)(2,1)S(1)} %copy.219), channel_id=1, source_target_pairs={{0,2},{1,3},{2,0},{3,1},{4,6},{5,7},{6,4},{7,5},{8,10},{9,11},{10,... | collective-permute-start | bytes 2187272 | tf_op jit(solution)/shard_map/ppermute | solution.py:460
  280.6 22.2 %collective-permute-start.11 = (bf16[1024,256]{1,0:T(8,128)(2,1)}, bf16[1024,256]{1,0:T(8,128)(2,1)}, u32[]{:S(2)}, u32[]{:S(2)}) collective-permute-start(bf16[1024,256]{1,0:T(8,128)(2,1)} %get-tuple-element.56), channel_id=1, source_target_pairs={{0,4},{4,0},{8,12},{12,8},{16,20},{20,16},{24,28},{28,24},{1,5},{5... | collective-permute-start | bytes 1572872 | tf_op jit(solution)/shard_map/ppermute | solution.py:521
  286.5 16.3 %collective-permute-start.13 = (bf16[1024,256]{1,0:T(8,128)(2,1)}, bf16[1024,256]{1,0:T(8,128)(2,1)}, u32[]{:S(2)}, u32[]{:S(2)}) collective-permute-start(bf16[1024,256]{1,0:T(8,128)(2,1)} %add_convert_fusion.2), channel_id=1, source_target_pairs={{0,16},{4,20},{16,24},{20,28},{24,8},{28,12},{8,0},{12,4},{1,17},{... | collective-permute-start | bytes 1572872 | tf_op jit(solution)/shard_map/ppermute | solution.py:516
  294.7 19.5 %collective-permute-start.10 = (bf16[1024,256]{1,0:T(8,128)(2,1)}, bf16[1024,256]{1,0:T(8,128)(2,1)}, u32[]{:S(2)}, u32[]{:S(2)}) collective-permute-start(bf16[1024,256]{1,0:T(8,128)(2,1)} %get-tuple-element.54), channel_id=1, source_target_pairs={{0,4},{4,0},{8,12},{12,8},{16,20},{20,16},{24,28},{28,24},{1,5},{5... | collective-permute-start | bytes 1572872 | tf_op jit(solution)/shard_map/ppermute | solution.py:521
  299.3 38.8 %all-to-all-start.2 = ((bf16[8,356,128]{2,1,0:T(8,128)(2,1)}), bf16[8,356,128]{2,1,0:T(8,128)(2,1)S(1)}, u32[]{:S(2)}, u32[]{:S(2)}) async-start(bf16[8,356,128]{2,1,0:T(8,128)(2,1)} %copy.198), calls=%async_computation.2 | async-start | bytes 1474560 | tf_op jit(solution)/shard_map/all_to_all | solution.py:491
  304.2 21.1 %copy-start.18 = (bf16[1024,256]{1,0:T(8,128)(2,1)S(1)}, bf16[1024,256]{1,0:T(8,128)(2,1)}, u32[]{:S(2)}) copy-start(bf16[1024,256]{1,0:T(8,128)(2,1)} %get-tuple-element.53) | copy-start | bytes 1572868
  304.2 21.1 %collective-permute-start.14 = (bf16[1024,256]{1,0:T(8,128)(2,1)S(1)}, bf16[1024,256]{1,0:T(8,128)(2,1)S(1)}, u32[]{:S(2)}, u32[]{:S(2)}) collective-permute-start(bf16[1024,256]{1,0:T(8,128)(2,1)S(1)} %add_convert_fusion.1), channel_id=1, source_target_pairs={{0,16},{4,20},{16,24},{20,28},{24,8},{28,12},{8,0},{12,4},{1,17},{... | collective-permute-start | bytes 1572872 | tf_op jit(solution)/shard_map/ppermute | solution.py:516
  312.7 26.0 %collective-permute-start.9 = (bf16[1024,256]{1,0:T(8,128)(2,1)}, bf16[1024,256]{1,0:T(8,128)(2,1)S(1)}, u32[]{:S(2)}, u32[]{:S(2)}) collective-permute-start(bf16[1024,256]{1,0:T(8,128)(2,1)} %get-tuple-element.52), channel_id=1, source_target_pairs={{0,4},{4,0},{8,12},{12,8},{16,20},{20,16},{24,28},{28,24},{1,5},{5... | collective-permute-start | bytes 1572872 | tf_op jit(solution)/shard_map/ppermute | solution.py:521
  327.3 16.3 %copy-start.1 = (bf16[1,1024,256]{2,1,0:T(8,128)(2,1)S(1)}, bf16[1,1024,256]{2,1,0:T(8,128)(2,1)}, u32[]{:S(2)}) copy-start(bf16[1,1024,256]{2,1,0:T(8,128)(2,1)} %param.30) | copy-start | bytes 1572868
  327.3 16.3 %copy-start.2 = (f32[1024,256]{1,0:T(8,128)S(1)}, f32[1024,256]{1,0:T(8,128)}, u32[]{:S(2)}) copy-start(f32[1024,256]{1,0:T(8,128)} %get-tuple-element.49) | copy-start | bytes 3145732
  327.3 16.3 %copy-start.4 = (bf16[1024,256]{1,0:T(8,128)(2,1)S(1)}, bf16[1024,256]{1,0:T(8,128)(2,1)}, u32[]{:S(2)}) copy-start(bf16[1024,256]{1,0:T(8,128)(2,1)} %get-tuple-element.51) | copy-start | bytes 1572868
  327.3 16.3 %collective-permute-start.15 = (bf16[1024,256]{1,0:T(8,128)(2,1)}, bf16[1024,256]{1,0:T(8,128)(2,1)}, u32[]{:S(2)}, u32[]{:S(2)}) collective-permute-start(bf16[1024,256]{1,0:T(8,128)(2,1)} %add_convert_fusion), channel_id=1, source_target_pairs={{0,16},{4,20},{16,24},{20,28},{24,8},{28,12},{8,0},{12,4},{1,17},{... | collective-permute-start | bytes 1572872 | tf_op jit(solution)/shard_map/ppermute | solution.py:516
  338.1 7.0 %collective-permute-start.18 = (f32[356,128]{1,0:T(8,128)S(1)}, f32[356,128]{1,0:T(8,128)S(1)}, u32[]{:S(2)}, u32[]{:S(2)}) collective-permute-start(f32[356,128]{1,0:T(8,128)S(1)} %convert_reduce_fusion), channel_id=1, source_target_pairs={{0,2},{1,3},{2,0},{3,1},{4,6},{5,7},{6,4},{7,5},{8,10},{9,11},{10,... | collective-permute-start | bytes 546824 | tf_op jit(solution)/shard_map/ppermute | solution.py:460
  345.2 3.6 %collective-permute-start.19 = (f32[712,128]{1,0:T(8,128)S(1)}, f32[712,128]{1,0:T(8,128)S(1)}, u32[]{:S(2)}, u32[]{:S(2)}) collective-permute-start(f32[712,128]{1,0:T(8,128)S(1)} %pad_maximum_fusion.3), channel_id=1, source_target_pairs={{0,1},{1,0},{2,3},{3,2},{4,5},{5,4},{6,7},{7,6},{8,9},{9,8},{10,11... | collective-permute-start | bytes 1093640 | tf_op jit(solution)/shard_map/ppermute | solution.py:460
  (31 other events, 101.0 us)

commit v2 on v1

--- a/solution.py
+++ b/solution.py
@@ -53,17 +53,17 @@
     return lax.rsqrt(jnp.mean(rows * rows, axis=-1, keepdims=True) + EPS)
 
 
-def edges_forward(order_ref, mine_ref, other_ref, small_ref, dist_ref, src_ref, *rest):
-    kept_ref, normed_ref = rest[-2:]
-    atoms = mine_ref.shape[0]
+def edges_forward(count, order_ref, small_ref, dist_ref, src_ref, *rest):
+    feature_refs, (kept_ref, normed_ref) = rest[:count], rest[-2:]
+    atoms = normed_ref.shape[0]
 
     def norm(ref):
         features = ref[...].astype(F32)
         normed_ref[...] = (features * inverse_rms(features) * small_ref[0:1, :]).astype(BF16)
 
     first = pl.program_id(1) == 0
-    pl.when(jnp.logical_and(first, pl.program_id(0) == 0))(lambda: norm(mine_ref))
-    pl.when(jnp.logical_and(first, pl.program_id(0) == 1))(lambda: norm(other_ref))
+    for number, ref in enumerate(feature_refs):
+        pl.when(jnp.logical_and(first, pl.program_id(0) == number))(functools.partial(norm, ref))
     atom_lane = lax.broadcasted_iota(jnp.int32, (1, atoms), 1).astype(F32)
     centres = lax.broadcasted_iota(jnp.int32, (1, NB_PAD), 1).astype(F32) * (CUTOFF / (NB - 1))
     per_spread = math.sqrt(math.log2(math.e)) / (2.0 * CUTOFF / (NB - 1))
@@ -287,7 +287,8 @@
         yield ref, owner * share, share, range(ref.shape[1])
 
 
-def edges_backward(order_ref, rows_ref, src_ref, mine_ref, other_ref):
+def edges_backward(order_ref, rows_ref, src_ref, *rest):
+    mine_ref, other_ref = rest[-2:]
     d_rows = rows_ref[...]
     source = src_ref[0]
     step = 256
@@ -311,47 +312,120 @@
     return (first_new, second_new, weight - step_rate * direction)
 
 
+def adamw_kernel(where_ref, held_ref, fetched_ref, *refs):
+    ins, outs, lows = refs[:21], refs[21:42], refs[42:47]
+    left, right = refs[47:]
+    core = where_ref[0]
+    for here in (0, 1):
+
+        @pl.when(core == here)
+        def _():
+            for ref, half in ((held_ref, here), (fetched_ref, 1 - here)):
+                (left, right)[half][...] = ref[...]
+
+    def packed(at, rows, pieces=1):
+        halves = [
+            half[at + part * rows : at + (part + 1) * rows, :]
+            for part in range(pieces)
+            for half in (left, right)
+        ]
+        return jnp.concatenate(halves, axis=1)
+
+    wa, wo, wd, wb = (ins[3 * number].shape[0] for number in (0, 1, 3, 4))
+    wg = ins[6].shape[1]
+    at = 0
+    attention = packed(at, wa)
+    at += wa
+    basis = packed(at, wb, NB_ROWS // H)[:, :NB]
+    at += wb * (NB_ROWS // H)
+    gateup = packed(at, wg)
+    if wg < LANES:
+        gateup = jnp.concatenate([gateup, jnp.zeros((LANES - wg, H), F32)], axis=0)
+    gateup = gateup.T[:, :wg]
+    at += wg
+    down = packed(at, wd, FF // H)
+    at += wd * (FF // H)
+    output = packed(at, wo)
+    at += wo
+    thin = packed(at, 8)
+    width = ins[15].shape[1]
+    column = lax.broadcasted_iota(jnp.int32, (H, width), 0)
+    mine = lax.broadcasted_iota(jnp.int32, (H, width), 1) + where_ref[1] * width
+    thin = jnp.dot(
+        thin,
+        jnp.where(column == mine, 1.0, 0.0),
+        precision=lax.Precision.HIGHEST,
+        preferred_element_type=F32,
+    )
+    gradients = (attention, output, gateup, down, basis, thin[2:3], thin[:2])
+    rates = (H ** (-0.5), (H // 16) ** (-0.5), H ** (-0.5), FF ** (-0.5), 0.5, H ** (-0.5), 0.2)
+    for number, (gradient, rate) in enumerate(zip(gradients, rates, strict=True)):
+        weight, first, second = (ref[...] for ref in ins[3 * number : 3 * number + 3])
+        results = adamw_step(weight, first, second, gradient, rate)
+        for ref, value in zip(outs[3 * number : 3 * number + 3], results, strict=True):
+            ref[...] = value
+        if number < 5:
+            lows[number][...] = results[2].astype(BF16)
+
+
+def run_adamw(where, held, fetched, states):
+    arrays = [array for triple in states for array in triple]
+    spec = pl.BlockSpec(memory_space=pltpu.VMEM)
+    shapes = [
+        jax.ShapeDtypeStruct(array.shape, F32) for triple in states for array in (*triple[1:], triple[0])
+    ]
+    shapes += [jax.ShapeDtypeStruct(triple[0].shape, BF16) for triple in states[:5]]
+    return list(
+        pl.pallas_call(
+            adamw_kernel,
+            in_specs=[pl.BlockSpec(memory_space=pltpu.SMEM)] + [spec] * (2 + len(arrays)),
+            out_specs=[spec] * len(shapes),
+            out_shape=shapes,
+            scratch_shapes=[pltpu.VMEM(held.shape, F32)] * 2,
+            compiler_params=pltpu.CompilerParams(vmem_limit_bytes=VMEM_BYTES),
+        )(where, held, fetched, *arrays)
+    )
+
+
 def whole_spec(shape):
     return pl.BlockSpec(shape, lambda *_: (0,) * len(shape), pipeline_mode=pl.Buffered(1))
 
 
-def run_edges_forward(turn, order, mine, other, small, dist_cols, src_cols, before):
-    atoms = mine.shape[0]
+def run_edges_forward(place, order, sources, small, dist_cols, src_cols, before):
+    atoms = sources[0].shape[0]
+    count = len(sources)
     owners, groups, _, columns = dist_cols.shape
     size = columns * LANES
-    edges = owners * groups * size
 
     def picked(i, g, order_ref):
-        return (order_ref[2 * turn + i], g, 0, 0)
-
-    def written(i, g, order_ref):
-        return ((2 * turn + i) * groups + g, 0)
+        return (order_ref[place + i], g, 0, 0)
 
     return pl.pallas_call(
-        edges_forward,
+        functools.partial(edges_forward, count),
         grid_spec=pltpu.PrefetchScalarGridSpec(
             num_scalar_prefetch=1,
-            grid=(2, groups),
+            grid=(count, groups),
             in_specs=[
-                whole_spec(mine.shape),
-                whole_spec(other.shape),
                 whole_spec(small.shape),
                 pl.BlockSpec((1, 1, LANES, columns), picked),
                 pl.BlockSpec((1, 1, LANES, columns), picked),
             ]
+            + [whole_spec(source.shape) for source in sources]
             + [pl.BlockSpec(memory_space=pl.ANY)] * len(before),
-            out_specs=pl.BlockSpec((size, WIDE), written),
+            out_specs=pl.BlockSpec(
+                (size, WIDE), lambda i, g, order_ref: ((place + i) * groups + g, 0)
+            ),
             scratch_shapes=[pltpu.VMEM((atoms, H), BF16)],
         ),
-        out_shape=jax.ShapeDtypeStruct((edges, WIDE), BF16),
-        input_output_aliases={6: 0} if before else {},
+        out_shape=jax.ShapeDtypeStruct((owners * groups * size, WIDE), BF16),
+        input_output_aliases={4 + count: 0} if before else {},
         compiler_params=pltpu.CompilerParams(vmem_limit_bytes=VMEM_BYTES),
         cost_estimate=pl.CostEstimate(
-            flops=4 * groups * size * atoms * H,
-            bytes_accessed=2 * groups * size * 2 * WIDE + 2 * atoms * H * 2,
-            transcendentals=2 * groups * size * NB_PAD,
+            flops=2 * count * groups * size * atoms * H,
+            bytes_accessed=count * (groups * size * 2 * WIDE + atoms * H * 2),
+            transcendentals=count * groups * size * NB_PAD,
         ),
-    )(order, mine, other, small, dist_cols, src_cols, *before)
+    )(order, small, dist_cols, src_cols, *sources, *before)
 
 
 def run_atoms(
@@ -428,7 +502,7 @@
     )(idx, core, kept, features, cot, ecot, count, small, wide, query, output, gateup, down)
 
 
-def run_edges_backward(turn, order, d_rows, src_rows, atoms):
+def run_edges_backward(turn, order, d_rows, src_rows, atoms, after):
     owners, sent = src_rows.shape[0], src_rows.shape[2]
     return pl.pallas_call(
         edges_backward,
@@ -438,7 +512,8 @@
             in_specs=[
                 pl.BlockSpec((sent, H), lambda i, order_ref: (2 * turn + i, 0)),
                 pl.BlockSpec((1, 1, sent), lambda i, order_ref: (order_ref[2 * turn + i], 0, 0)),
-            ],
+            ]
+            + [pl.BlockSpec(memory_space=pl.ANY)] * len(after),
             out_specs=[whole_spec((atoms, H)), whole_spec((atoms, H))],
         ),
         out_shape=[jax.ShapeDtypeStruct((atoms, H), BF16)] * 2,
@@ -448,7 +523,7 @@
             bytes_accessed=2 * sent * 2 * H + 4 * atoms * H,
             transcendentals=0,
         ),
-    )(order, d_rows, src_rows)
+    )(order, d_rows, src_rows, *after)
 
 
 def halves(axis_size):
@@ -460,44 +535,27 @@
     return lax.ppermute(array, "rep", [(r, r ^ (1 << bit)) for r in range(size)])
 
 
-def gather_rows(rows):
-    owners, reps = lax.axis_size("edge"), lax.axis_size("rep")
+def behind(array, other):
+    return lax.optimization_barrier((array, other))[0]
+
+
+def halve(totals, bit):
+    half = totals.shape[1] // 2
+    upper = (lax.axis_index("rep") >> bit) & 1
+    sent = lax.dynamic_slice_in_dim(totals, (1 - upper) * half, half, 1)
+    return lax.dynamic_slice_in_dim(totals, upper * half, half, 1), sent.astype(BF16)
+
+
+def gather_back(held):
+    reps = lax.axis_size("rep")
     me = lax.axis_index("rep")
-    share = rows.shape[0] // reps
-    part = lax.dynamic_slice_in_dim(rows, me * share, share, 0)
-    held = lax.all_to_all(
-        jnp.broadcast_to(part[None], (owners, share, H)), "edge", 0, 0, tiled=True
-    )
-    for bit in reversed(halves(reps)):
-        fetched = across(held, bit)
-        upper = (me >> bit) & 1 == 1
-        held = jnp.stack([jnp.where(upper, fetched, held), jnp.where(upper, held, fetched)])
-    bits = len(halves(reps))
-    held = held.transpose((bits,) + tuple(reversed(range(bits))) + (bits + 1, bits + 2))
-    return held.reshape(owners, reps * share, H)
-
-
-def reduce_rows(mine, theirs):
-    owners, reps = lax.axis_size("edge"), lax.axis_size("rep")
-    me = lax.axis_index("rep")
-    totals = mine.astype(F32) + across(theirs, 0).astype(F32)
-    totals = totals.reshape(owners, -1, LANES)
-    for bit in halves(reps)[1:]:
-        half = totals.shape[1] // 2
-        upper = (me >> bit) & 1
-        sent = lax.dynamic_slice_in_dim(totals, (1 - upper) * half, half, 1)
-        kept = lax.dynamic_slice_in_dim(totals, upper * half, half, 1)
-        totals = kept + across(sent.astype(BF16), bit).astype(F32)
-    pieces = lax.all_to_all(totals.astype(BF16), "edge", 0, 0, tiled=True)
-    held = jnp.sum(pieces.astype(F32), axis=0)
-    for bit in reversed(halves(reps)):
+    for bit in reversed(halves(reps)[1:]):
         fetched = across(held, bit)
         upper = (me >> bit) & 1 == 1
         held = jnp.concatenate(
-            [jnp.where(upper, fetched, held), jnp.where(upper, held, fetched)],
-            axis=0 if bit > 0 else 1,
+            [jnp.where(upper, fetched, held), jnp.where(upper, held, fetched)], axis=0
         )
-    return held
+    return held, across(held, 0)
 
 
 def ring_of(owners):
@@ -530,15 +588,6 @@
                 source = 2 * ring[at - turn]
                 table[2 * here + side, 2 * turn : 2 * turn + 2] = (source + side, source + 1 - side)
     return table
-
-
-def pad_rows(array, multiple):
-    short = -array.shape[0] % multiple
-    return jnp.pad(array, ((0, short), (0, 0)))
-
-
-def unstack(pieces, rows, width):
-    return pieces.reshape(width // H, rows, H).transpose(1, 0, 2).reshape(rows, width)
 
 
 def local(
@@ -609,21 +658,17 @@
     source = pieces[:, 3] * 32.0 + pieces[:, 4]
 
     basis_rows = jnp.pad(basis_weight.T.astype(BF16), ((0, 0), (0, NB_ROWS - NB)))
-    weight_rows = pad_rows(
-        jnp.concatenate(
-            [
-                attention_weight.T.astype(BF16),
-                basis_rows.reshape(3 * wb, H),
-                gateup_weight.T.astype(BF16),
-                down_weight.T.astype(BF16).reshape(wd * (FF // H), H),
-                output_weight.T.astype(BF16),
-            ],
-            axis=0,
-        ),
-        8 * lax.axis_size("rep"),
-    )
-    weight_rows, meta = lax.optimization_barrier((weight_rows, meta))
-    weight_rows = gather_rows(weight_rows)
+    weight_rows = jnp.concatenate(
+        [
+            attention_weight.T.astype(BF16),
+            basis_rows.reshape(3 * wb, H),
+            gateup_weight.T.astype(BF16),
+            down_weight.T.astype(BF16).reshape(wd * (FF // H), H),
+            output_weight.T.astype(BF16),
+        ],
+        axis=0,
+    )
+    weight_rows = lax.all_gather(weight_rows, "edge", axis=0)
     at = 0
     fulls = []
     for width, rows in ((H, wa), (NB_ROWS, wb), (H, wg), (FF, wd), (H, wo)):
@@ -646,16 +691,23 @@
     order = jnp.asarray(table)[me]
     place = jnp.asarray(np.argsort(table, axis=1).astype(np.int32))[me]
     turns = owners // 2
-    mine, before = features, ()
-    for turn in range(turns):
-        if turn > 0:
-            mine = ring_step(mine)
-        before = (
-            run_edges_forward(
-                turn, order, mine, pair_swap(mine), small, dist_cols, src_cols, before
-            ),
-        )
-    (kept,) = before
+    arrivals = [features]
+    if turns > 1:
+        arrivals.append(ring_step(features))
+    swapped = [pair_swap(array) for array in arrivals]
+    ahead = ring_step(arrivals[1]) if turns > 2 else None
+    kept = run_edges_forward(0, order, [features], small, dist_cols, src_cols, ())
+    kept = run_edges_forward(1, order, [swapped[0]], small, dist_cols, src_cols, (kept,))
+    if turns > 1:
+        sources = [arrivals[1], swapped[1]]
+        if turns > 2:
+            ahead, kept = lax.optimization_barrier((ahead, kept))
+        kept = run_edges_forward(2, order, sources, small, dist_cols, src_cols, (kept,))
+    for turn in range(2, turns):
+        sources = [ahead, pair_swap(ahead)]
+        if turn < turns - 1:
+            ahead, kept = lax.optimization_barrier((ring_step(ahead), kept))
+        kept = run_edges_forward(2 * turn, order, sources, small, dist_cols, src_cols, (kept,))
 
     slot_ids = slot_index[0]
     slot_owner = slot_ids // sent
@@ -680,16 +732,44 @@
         gateup_rows,
         down_rows,
     )
-    shard = reduce_rows(grads_mine, grads_theirs)
-
-    running = None
-    for turn in [*range(1, turns), 0]:
-        part, part_other = run_edges_backward(turn, order, d_rows, src_rows, atoms)
-        total = part.astype(F32) + pair_swap(part_other).astype(F32)
-        if running is not None:
-            total = total + ring_step(running).astype(F32)
+    turns_back = [*range(1, turns), 0]
+    bits = halves(lax.axis_size("rep"))[1:]
+    fetched = across(grads_theirs, 0)
+    parts, after, running = [], (), None
+
+    def add_pair(number, latest):
+        part, other = parts[number]
+        if running is None:
+            return part.astype(F32) + behind(other, latest).astype(F32)
+        moved = behind(ring_step(running), latest)
+        return part.astype(F32) + other.astype(F32) + moved.astype(F32)
+
+    for number, turn in enumerate(turns_back):
+        part, part_other = run_edges_backward(turn, order, d_rows, src_rows, atoms, after)
+        parts.append((part, pair_swap(part_other)))
+        after = ()
+        if number == 1:
+            totals = grads_mine.astype(F32) + behind(fetched, part).astype(F32)
+            totals, sent_rows = halve(totals.reshape(owners, -1, LANES), bits[0])
+            fetched = across(sent_rows, bits[0])
+            after = (sent_rows,)
+        elif 1 < number < turns - 1:
+            running = add_pair(number - 2, part).astype(BF16)
+            after = (running,)
+    totals = totals + behind(fetched, part).astype(F32)
+    for bit in bits[1:]:
+        totals, sent_rows = halve(totals, bit)
+        totals = totals + across(sent_rows, bit).astype(F32)
+    totals = totals.astype(BF16)
+    pieces = lax.all_to_all(totals, "edge", 0, 0, tiled=True)
+    latest = totals
+    for number in range(turns - 3, turns):
+        if number == turns - 1:
+            latest = held = jnp.sum(pieces.astype(F32), axis=0)
+        total = add_pair(number, latest)
         running = total.astype(BF16)
     d_from_edges = total
+    held, fetched = gather_back(held)
 
     features = features.astype(F32)
     inv_one = inverse_rms(features)
@@ -701,61 +781,31 @@
         - features * inv_one**3 * jnp.mean(scaled * features, axis=-1, keepdims=True)
     )
 
-    cuts = np.cumsum([wa, 3 * wb, wg, wd * (FF // H), wo])
-    thin_shard = lax.dynamic_slice_in_dim(shard[cuts[4] : cuts[4] + 3], me * wr, wr, 1)
-    gradients = (
-        shard[: cuts[0]].T,
-        shard[cuts[3] : cuts[4]].T,
-        shard[cuts[1] : cuts[2]].T,
-        unstack(shard[cuts[2] : cuts[3]], wd, FF).T,
-        unstack(shard[cuts[0] : cuts[1]], wb, NB_ROWS)[:, :NB].T,
-        thin_shard[2],
-        thin_shard[:2],
-    )
-    step_rates = (
-        H ** (-0.5),
-        (H // 16) ** (-0.5),
-        H ** (-0.5),
-        FF ** (-0.5),
-        0.5,
-        H ** (-0.5),
-        0.2,
-    )
-    masters = (
-        attention_weight,
-        output_weight,
-        gateup_weight,
-        down_weight,
-        basis_weight,
-        readout_weight,
-        norm_gains,
-    )
-    firsts = (
-        attention_first,
-        output_first,
-        gateup_first,
-        down_first,
-        basis_first,
-        readout_first,
-        gains_first,
-    )
-    seconds = (
-        attention_second,
-        output_second,
-        gateup_second,
-        down_second,
-        basis_second,
-        readout_second,
-        gains_second,
-    )
-    updated = [
-        adamw_step(
-            masters[number], firsts[number], seconds[number], gradients[number], step_rates[number]
-        )
-        for number in range(7)
+    where = jnp.stack([core[0], me.astype(jnp.int32)])
+    states = (
+        (attention_weight, attention_first, attention_second),
+        (output_weight, output_first, output_second),
+        (gateup_weight, gateup_first, gateup_second),
+        (down_weight, down_first, down_second),
+        (basis_weight, basis_first, basis_second),
+        (readout_weight, readout_first, readout_second),
+        (norm_gains, gains_first, gains_second),
+    )
+
+    def turn_over(number, array):
+        return array.T if number in (0, 1, 3, 4) else array[None] if number == 5 else array
+
+    updated = run_adamw(
+        where,
+        held,
+        fetched,
+        [[turn_over(number, array) for array in triple] for number, triple in enumerate(states)],
+    )
+    flat = [
+        array[0] if at // 3 == 5 else turn_over(at // 3, array)
+        for at, array in enumerate(updated[:21])
     ]
-    flat = [array for triple in updated for array in triple]
-    lows = [updated[number][2].astype(BF16) for number in range(5)]
+    lows = [turn_over(number, array) for number, array in enumerate(updated[21:])]
     return (block_out[None], energy[:, 0][None], input_grad[None], *flat, *lows)
 
 

time: 360 us -> 369 us (1.025)
  blocking collectives: 21.5 us -> 0 us
  waiting for transfers between devices: 37.2 us -> 55.5 us
  between operations: 1.49 us -> 14.7 us
  other arithmetic: 33 us -> 26.7 us
  Pallas kernels: 197 us -> 203 us
    all_to_all x1 -> x0, blocking collectives: 21.5 us -> none  [gather_rows(): lax.all_to_all(jnp.broadcast_to(part[None], (owners, share, H)), 'edge',...]
    ppermute x6, waiting for transfers between devices: 26.8 us -> 40.3 us  [ring_step(): return lax.ppermute(array, 'edge', moves)]
    pallas_call x4 -> x6, Pallas kernels: 33.8 us -> 40 us  [the longest x5 36.5 us: run_edges_forward(): pl.pallas_call(functools.partial(edges_forward, count), grid_spec=pltpu.P...]
    unnamed x95 -> x65, local copies, waits for them, and re-layouts: 11.9 us -> 7.57 us
  transfers between devices with their start and end apart: 22 -> 21, of which waited for: 7 -> 7; matrix products, arithmetic and copies ran while one was open for 11% -> 9% of each run, Pallas kernels for 16% -> 16%
where the time goes in v2:
time: 369 us; the launch traced here: 367 us
  Pallas kernels  203 us (55%)
  waiting for transfers between devices  55.5 us (15%)
  starting transfers between devices  40.2 us (11%)
  local copies, waits for them, and re-layouts  26.7 us (7%)
  other arithmetic  26.7 us (7%)
  between operations  14.7 us (4%)
    pallas_call x1, Pallas kernels, run_atoms(): pl.pallas_call(functools.partial(atoms_kernel, ins, blocks, outs, owners)...  141 us
    ppermute x6, waiting for transfers between devices, ring_step(): return lax.ppermute(array, 'edge', moves)  40.3 us
    pallas_call x5, Pallas kernels, run_edges_forward(): pl.pallas_call(functools.partial(edges_forward, count), grid_spec=pltpu.P...  36.5 us
    pallas_call x4, Pallas kernels, run_edges_backward(): pl.pallas_call(edges_backward, grid_spec=pltpu.PrefetchScalarGridSpec(num...  22.4 us
    ppermute x6, starting transfers between devices, ring_step(): return lax.ppermute(array, 'edge', moves)  12.9 us
    ppermute x8, starting transfers between devices, pair_swap(): return lax.ppermute(array, 'edge', [(e, e ^ 1) for e in range(owners)])  11.2 us
    all_to_all x1, waiting for transfers between devices, local(): meta = lax.all_to_all(meta, 'edge', 0, 0, tiled=True)  9.4 us
    unnamed x65, local copies, waits for them, and re-layouts  7.57 us
  transfers between devices with their start and end apart: 21, of which 7 were waited for; matrix products, arithmetic and copies ran while one was open for 9% of the time, Pallas kernels for 16%

profile of v2, /device:TPU:0, one launch (start us, length us, event | category | flops | bytes accessed | tf_op | source)
XLA Modules:
  0.0 366.6 jit_solution(3983751501293208764)
XLA Ops:
  15.7 7.3 %all-to-all-start = ((bf16[8,48,256]{2,1,0:T(8,128)(2,1)}), bf16[8,48,256]{2,1,0:T(8,128)(2,1)S(1)}, u32[]{:S(2)}, u32[]{:S(2)}) async-start(bf16[8,48,256]{2,1,0:T(8,128)(2,1)} %pad_maximum_fusion.2), calls=%async_computation | async-start | bytes 393216 | tf_op jit(solution)/shard_map/all_to_all | solution.py:652
  22.9 2.9 collective-permute-start
  28.5 9.4 %all-to-all-done = bf16[8,48,256]{2,1,0:T(8,128)(2,1)S(1)} async-done(((bf16[8,48,256]{2,1,0:T(8,128)(2,1)}), bf16[8,48,256]{2,1,0:T(8,128)(2,1)S(1)}, u32[]{:S(2)}, u32[]{:S(2)}) %all-to-all-start) | async-done | bytes 196640 | tf_op jit(solution)/shard_map/all_to_all | solution.py:652
  38.1 12.5 %collective-permute-done.rest_0_ = bf16[1024,256]{1,0:T(8,128)(2,1)S(1)} collective-permute-done((bf16[1024,256]{1,0:T(8,128)(2,1)S(1)}, bf16[1024,256]{1,0:T(8,128)(2,1)S(1)}, u32[]{:S(2)}, u32[]{:S(2)}) %collective-permute-start) | collective-permute-done | bytes 524320 | tf_op jit(solution)/shard_map/ppermute | solution.py:574
  50.5 1.9 collective-permute-start.1
  56.1 1.7 collective-permute-start.4
  57.9 5.6 %shard_map.509.rest_1_ = bf16[16384,896]{1,0:T(8,128)(2,1)} custom-call(s32[8]{0:T(128)} %fusion.15.order_ref, f32[8,256]{1,0:T(8,128)} %pad.13.small_ref, f32[8,2,128,8]{3,2,1,0:T(8,128)} %bitcast.111, f32[8,2,128,8]{3,2,1,0:T(8,128)} %bitcast.106, bf16[1024,256]{1,0:T(8,128)(2,1)} %bitcast.118), custom_call_target="tpu_custom_call" | custom-call | flops 1073741824 | bytes 4194304 | tf_op jit(solution)/shard_map/pallas_call | solution.py:403
  64.2 5.6 %shard_map.510.rest_2_ = bf16[16384,896]{1,0:T(8,128)(2,1)} custom-call(s32[8]{0:T(128)} %fusion.15.order_ref, f32[8,256]{1,0:T(8,128)} %pad.13.small_ref, f32[8,2,128,8]{3,2,1,0:T(8,128)} %bitcast.112, f32[8,2,128,8]{3,2,1,0:T(8,128)} %bitcast.107, bf16[1024,256]{1,0:T(8,128)(2,1)} %copy-done.13, ...), custom_call_target="tpu_custom_call", output_to_operand_aliasing={{}: (5, {})} | custom-call | flops 1073741824 | bytes 4194304 | tf_op jit(solution)/shard_map/pallas_call | solution.py:403
  69.8 5.1 %collective-permute-done.1.rest_0_ = bf16[1024,256]{1,0:T(8,128)(2,1)S(1)} collective-permute-done((bf16[1024,256]{1,0:T(8,128)(2,1)S(1)}, bf16[1024,256]{1,0:T(8,128)(2,1)S(1)}, u32[]{:S(2)}, u32[]{:S(2)}) %collective-permute-start.1) | collective-permute-done | bytes 524320 | tf_op jit(solution)/shard_map/ppermute | solution.py:574
  76.9 4.9 %collective-permute-done.4.rest_1_ = bf16[1024,256]{1,0:T(8,128)(2,1)S(1)} collective-permute-done((bf16[1024,256]{1,0:T(8,128)(2,1)S(1)}, bf16[1024,256]{1,0:T(8,128)(2,1)S(1)}, u32[]{:S(2)}, u32[]{:S(2)}) %collective-permute-start.4) | collective-permute-done | bytes 524320 | tf_op jit(solution)/shard_map/ppermute | solution.py:579
  82.7 8.5 %shard_map.511.rest_2_ = bf16[16384,896]{1,0:T(8,128)(2,1)} custom-call(s32[8]{0:T(128)} %fusion.15.order_ref, f32[8,256]{1,0:T(8,128)} %pad.13.small_ref, f32[8,2,128,8]{3,2,1,0:T(8,128)} %bitcast.113, f32[8,2,128,8]{3,2,1,0:T(8,128)} %bitcast.108, bf16[1024,256]{1,0:T(8,128)(2,1)} %copy-done.11, ...), custom_call_target="tpu_custom_call", output_to_operand_aliasing={{}: (6, {})} | custom-call | flops 2147483648 | bytes 8388608 | tf_op jit(solution)/shard_map/pallas_call | solution.py:403
  93.4 5.3 %fusion.10 = s32[8,16,128]{2,0,1:T(8,128)S(1)} fusion(s32[2,8,8,128]{3,2,1,0:T(8,128)S(1)} %copy.100, s32[]{:T(128)} %bitcast.7, s32[]{:T(128)} %bitcast.6, s32[]{:T(128)} %bitcast.5, s32[]{:T(128)} %bitcast.4, s32[]{:T(128)} %bitcast.3, s32[]{:T(128)} %bitcast.2, s32[]{:T(128)} %bitcast.1, s32[]{:T(128)} %bitcast), kind=kLoop, calls=%fused_computation.39 | loop fusion | flops 737280 | bytes 131104 | tf_op jit(solution)/shard_map/mul | solution.py:716
  102.3 8.4 %shard_map.512.rest_2_ = bf16[16384,896]{1,0:T(8,128)(2,1)} custom-call(s32[8]{0:T(128)} %fusion.15.order_ref, f32[8,256]{1,0:T(8,128)} %pad.13.small_ref, f32[8,2,128,8]{3,2,1,0:T(8,128)} %bitcast.114, f32[8,2,128,8]{3,2,1,0:T(8,128)} %bitcast.109, bf16[1024,256]{1,0:T(8,128)(2,1)} %copy-done.10, ...), custom_call_target="tpu_custom_call", output_to_operand_aliasing={{}: (6, {})} | custom-call | flops 2147483648 | bytes 8388608 | tf_op jit(solution)/shard_map/pallas_call | solution.py:403
  111.5 8.4 %shard_map.513.kept_ref = bf16[16384,896]{1,0:T(8,128)(2,1)} custom-call(s32[8]{0:T(128)} %fusion.15.order_ref, f32[8,256]{1,0:T(8,128)} %pad.13.small_ref, f32[8,2,128,8]{3,2,1,0:T(8,128)} %bitcast.115, f32[8,2,128,8]{3,2,1,0:T(8,128)} %bitcast.110, bf16[1024,256]{1,0:T(8,128)(2,1)} %copy-done.12, ...), custom_call_target="tpu_custom_call", output_to_operand_aliasing={{}: (6, {})} | custom-call | flops 2147483648 | bytes 8388608 | tf_op jit(solution)/shard_map/pallas_call | solution.py:403
  127.3 140.5 %shard_map.514 = (bf16[1024,256]{1,0:T(8,128)(2,1)}, f32[1024,128]{1,0:T(8,128)}, f32[1024,256]{1,0:T(8,128)}, f32[1024,256]{1,0:T(8,128)}, bf16[16384,256]{1,0:...) custom-call(s32[16384]{0:T(1024)} %bitcast.146, s32[1]{0:T(128)} %bitcast.10.core_ref, ...), custom_call_target="tpu_custom_call" | custom-call | flops 52076478464 | bytes 71827456 | tf_op jit(solution)/shard_map/pallas_call | solution.py:447
  267.9 5.6 %shard_map.515 = (bf16[1024,256]{1,0:T(8,128)(2,1)}, bf16[1024,256]{1,0:T(8,128)(2,1)}) custom-call(s32[8]{0:T(128)} %fusion.15.order_ref, bf16[16384,256]{1,0:T(8,128)(2,1)} %get-tuple-element.88.rows_ref, f32[8,1,2048]{2,1,0:T(1,128)} %copy-done.5), custom_call_target="tpu_custom_call" | custom-call | flops 2147483648 | bytes 3145728 | tf_op jit(solution)/shard_map/pallas_call | solution.py:507
  273.9 5.6 %shard_map.516 = (bf16[1024,256]{1,0:T(8,128)(2,1)}, bf16[1024,256]{1,0:T(8,128)(2,1)}) custom-call(s32[8]{0:T(128)} %fusion.15.order_ref, bf16[16384,256]{1,0:T(8,128)(2,1)} %get-tuple-element.88.rows_ref, f32[8,1,2048]{2,1,0:T(1,128)} %copy-done.5), custom_call_target="tpu_custom_call" | custom-call | flops 2147483648 | bytes 3145728 | tf_op jit(solution)/shard_map/pallas_call | solution.py:507
  279.6 2.1 convert_add_fusion
  285.2 5.6 %shard_map.517 = (bf16[1024,256]{1,0:T(8,128)(2,1)}, bf16[1024,256]{1,0:T(8,128)(2,1)}) custom-call(s32[8]{0:T(128)} %fusion.15.order_ref, bf16[16384,256]{1,0:T(8,128)(2,1)} %get-tuple-element.88.rows_ref, f32[8,1,2048]{2,1,0:T(1,128)} %copy-done.5, bf16[8,356,128]{2,1,0:T(8,128)(2,1)} %copy-done), custom_call_target="tpu_custom_call" | custom-call | flops 2147483648 | bytes 3145728 | tf_op jit(solution)/shard_map/pallas_call | solution.py:507
  292.8 1.7 collective-permute-start.12
  296.0 5.6 %shard_map.518 = (bf16[1024,256]{1,0:T(8,128)(2,1)}, bf16[1024,256]{1,0:T(8,128)(2,1)}) custom-call(s32[8]{0:T(128)} %fusion.15.order_ref, bf16[16384,256]{1,0:T(8,128)(2,1)} %get-tuple-element.88.rows_ref, f32[8,1,2048]{2,1,0:T(1,128)} %copy-done.5, bf16[1024,256]{1,0:T(8,128)(2,1)} %copy-done.6), custom_call_target="tpu_custom_call" | custom-call | flops 2147483648 | bytes 3145728 | tf_op jit(solution)/shard_map/pallas_call | solution.py:507
  302.4 2.2 add_convert_fusion
  304.6 5.4 %all-to-all-start.1 = ((bf16[8,356,128]{2,1,0:T(8,128)(2,1)}), bf16[8,356,128]{2,1,0:T(8,128)(2,1)S(1)}, u32[]{:S(2)}, u32[]{:S(2)}) async-start(bf16[8,356,128]{2,1,0:T(8,128)(2,1)} %add_convert_fusion), calls=%async_computation.1 | async-start | bytes 1474560 | tf_op jit(solution)/shard_map/all_to_all | solution.py:764
  311.8 3.0 collective-permute-start.14
  316.2 16.7 %collective-permute-done.14 = bf16[1024,256]{1,0:T(8,128)(2,1)S(1)} collective-permute-done((bf16[1024,256]{1,0:T(8,128)(2,1)S(1)}, bf16[1024,256]{1,0:T(8,128)(2,1)S(1)}, u32[]{:S(2)}, u32[]{:S(2)}) %collective-permute-start.14) | collective-permute-done | bytes 524320 | tf_op jit(solution)/shard_map/ppermute | solution.py:574
  332.9 2.1 add_convert_fusion.1
  335.0 3.4 collective-permute-start.15
  338.4 1.7 collective-permute-start.9
  341.6 1.8 slice_reduce_fusion
  345.1 6.0 %collective-permute-done.15 = bf16[1024,256]{1,0:T(8,128)(2,1)S(1)} collective-permute-done((bf16[1024,256]{1,0:T(8,128)(2,1)}, bf16[1024,256]{1,0:T(8,128)(2,1)S(1)}, u32[]{:S(2)}, u32[]{:S(2)}) %collective-permute-start.15) | collective-permute-done | bytes 524320 | tf_op jit(solution)/shard_map/ppermute | solution.py:574
  352.9 2.6 fusion.3
  356.3 3.5 shard_map.519
  (158 shorter events, 49.3 us)
Async XLA Ops:
  7.2 15.7 %copy-start.1 = (bf16[1,1024,256]{2,1,0:T(8,128)(2,1)S(1)}, bf16[1,1024,256]{2,1,0:T(8,128)(2,1)}, u32[]{:S(2)}) copy-start(bf16[1,1024,256]{2,1,0:T(8,128)(2,1)} %param.30) | copy-start | bytes 1572868
  7.2 112.7 %all-gather.3.cloned.1.call-start = ((), (), s32[]{:S(2)}) async-start(), calls=%async_computation.2 | async-start | bytes 3244032 | tf_op jit(solution)/shard_map/all_gather | solution.py:671
  15.7 22.3 %all-to-all-start = ((bf16[8,48,256]{2,1,0:T(8,128)(2,1)}), bf16[8,48,256]{2,1,0:T(8,128)(2,1)S(1)}, u32[]{:S(2)}, u32[]{:S(2)}) async-start(bf16[8,48,256]{2,1,0:T(8,128)(2,1)} %pad_maximum_fusion.2), calls=%async_computation | async-start | bytes 393216 | tf_op jit(solution)/shard_map/all_to_all | solution.py:652
  22.9 27.6 %collective-permute-start = (bf16[1024,256]{1,0:T(8,128)(2,1)S(1)}, bf16[1024,256]{1,0:T(8,128)(2,1)S(1)}, u32[]{:S(2)}, u32[]{:S(2)}) collective-permute-start(bf16[1024,256]{1,0:T(8,128)(2,1)S(1)} %bitcast.120), channel_id=1, source_target_pairs={{0,16},{4,20},{16,24},{20,28},{24,8},{28,12},{8,0},{12,4},{1,17},{... | collective-permute-start | bytes 1572872 | tf_op jit(solution)/shard_map/ppermute | solution.py:574
  25.9 37.6 %collective-permute-start.2 = (bf16[1024,256]{1,0:T(8,128)(2,1)S(1)}, bf16[1024,256]{1,0:T(8,128)(2,1)S(1)}, u32[]{:S(2)}, u32[]{:S(2)}) collective-permute-start(bf16[1024,256]{1,0:T(8,128)(2,1)S(1)} %bitcast.121), channel_id=1, source_target_pairs={{0,4},{4,0},{8,12},{12,8},{16,20},{20,16},{24,28},{28,24},{1,5},{5... | collective-permute-start | bytes 1572872 | tf_op jit(solution)/shard_map/ppermute | solution.py:579
  50.5 12.9 %copy-start.11 = (bf16[1024,256]{1,0:T(8,128)(2,1)}, bf16[1024,256]{1,0:T(8,128)(2,1)S(1)}, u32[]{:S(2)}) copy-start(bf16[1024,256]{1,0:T(8,128)(2,1)S(1)} %collective-permute-done.rest_0_) | copy-start | bytes 1572868
  50.5 24.4 %collective-permute-start.1 = (bf16[1024,256]{1,0:T(8,128)(2,1)S(1)}, bf16[1024,256]{1,0:T(8,128)(2,1)S(1)}, u32[]{:S(2)}, u32[]{:S(2)}) collective-permute-start(bf16[1024,256]{1,0:T(8,128)(2,1)S(1)} %collective-permute-done.rest_0_), channel_id=1, source_target_pairs={{0,16},{4,20},{16,24},{20,28},{24,8},{28,12},{8,0},{12,4},{1,17},{... | collective-permute-start | bytes 1572872 | tf_op jit(solution)/shard_map/ppermute | solution.py:574
  52.7 10.7 %copy-start.5 = (f32[8,1,2048]{2,1,0:T(1,128)}, f32[8,1,2048]{2,1,0:T(1,128)S(1)}, u32[]{:S(2)}) copy-start(f32[8,1,2048]{2,1,0:T(1,128)S(1)} %get-tuple-element.138.src_ref) | copy-start | bytes 196612
  56.1 25.7 %collective-permute-start.4 = (bf16[1024,256]{1,0:T(8,128)(2,1)S(1)}, bf16[1024,256]{1,0:T(8,128)(2,1)S(1)}, u32[]{:S(2)}, u32[]{:S(2)}) collective-permute-start(bf16[1024,256]{1,0:T(8,128)(2,1)S(1)} %collective-permute-done.rest_0_), channel_id=1, source_target_pairs={{0,4},{4,0},{8,12},{12,8},{16,20},{20,16},{24,28},{28,24},{1,5},{5... | collective-permute-start | bytes 1572872 | tf_op jit(solution)/shard_map/ppermute | solution.py:579
  63.4 11.5 %copy-start.23 = (s32[1,1024,16]{1,2,0:T(8,128)S(1)}, s32[1,1024,16]{1,2,0:T(8,128)}, u32[]{:S(2)}) copy-start(s32[1,1024,16]{1,2,0:T(8,128)} %param.33) | copy-start | bytes 196612
  74.9 16.2 %copy-start.10 = (bf16[1024,256]{1,0:T(8,128)(2,1)}, bf16[1024,256]{1,0:T(8,128)(2,1)S(1)}, u32[]{:S(2)}) copy-start(bf16[1024,256]{1,0:T(8,128)(2,1)S(1)} %collective-permute-done.1.rest_0_) | copy-start | bytes 1572868
  74.9 16.2 %collective-permute-start.3 = (bf16[1024,256]{1,0:T(8,128)(2,1)S(1)}, bf16[1024,256]{1,0:T(8,128)(2,1)S(1)}, u32[]{:S(2)}, u32[]{:S(2)}) collective-permute-start(bf16[1024,256]{1,0:T(8,128)(2,1)S(1)} %collective-permute-done.1.rest_0_), channel_id=1, source_target_pairs={{0,16},{4,20},{16,24},{20,28},{24,8},{28,12},{8,0},{12,4},{1,17},{... | collective-permute-start | bytes 1572872 | tf_op jit(solution)/shard_map/ppermute | solution.py:574
  75.7 23.7 %copy-start.24 = (s32[1,1024,16]{1,2,0:T(8,128)S(1)}, s32[1,1024,16]{1,2,0:T(8,128)}, u32[]{:S(2)}) copy-start(s32[1,1024,16]{1,2,0:T(8,128)} %param.34) | copy-start | bytes 196612
  75.7 24.8 %copy-start.25 = (f32[1,1024]{1,0:T(1,128)S(1)}, f32[1,1024]{1,0:T(1,128)}, u32[]{:S(2)}) copy-start(f32[1,1024]{1,0:T(1,128)} %param.36) | copy-start | bytes 12292
  75.7 25.8 %collective-permute-start.6 = (bf16[1024,256]{1,0:T(8,128)(2,1)S(1)}, bf16[1024,256]{1,0:T(8,128)(2,1)S(1)}, u32[]{:S(2)}, u32[]{:S(2)}) collective-permute-start(bf16[1024,256]{1,0:T(8,128)(2,1)S(1)} %collective-permute-done.1.rest_0_), channel_id=1, source_target_pairs={{0,4},{4,0},{8,12},{12,8},{16,20},{20,16},{24,28},{28,24},{1,5},{5... | collective-permute-start | bytes 1572872 | tf_op jit(solution)/shard_map/ppermute | solution.py:579
  91.1 19.6 %copy-start.12 = (bf16[1024,256]{1,0:T(8,128)(2,1)}, bf16[1024,256]{1,0:T(8,128)(2,1)S(1)}, u32[]{:S(2)}) copy-start(bf16[1024,256]{1,0:T(8,128)(2,1)S(1)} %collective-permute-done.3.rest_0_) | copy-start | bytes 1572868
  91.1 19.6 %collective-permute-start.5 = (bf16[1024,256]{1,0:T(8,128)(2,1)S(1)}, bf16[1024,256]{1,0:T(8,128)(2,1)S(1)}, u32[]{:S(2)}, u32[]{:S(2)}) collective-permute-start(bf16[1024,256]{1,0:T(8,128)(2,1)S(1)} %collective-permute-done.3.rest_0_), channel_id=1, source_target_pairs={{0,4},{4,0},{8,12},{12,8},{16,20},{20,16},{24,28},{28,24},{1,5},{5... | collective-permute-start | bytes 1572872 | tf_op jit(solution)/shard_map/ppermute | solution.py:579
  267.9 11.7 %collective-permute-start.8 = (bf16[5696,128]{1,0:T(8,128)(2,1)}, bf16[5696,128]{1,0:T(8,128)(2,1)}, u32[]{:S(2)}, u32[]{:S(2)}) collective-permute-start(bf16[5696,128]{1,0:T(8,128)(2,1)} %get-tuple-element.92), channel_id=1, source_target_pairs={{0,1},{1,0},{2,3},{3,2},{4,5},{5,4},{6,7},{7,6},{8,9},{9,8},{10,11... | collective-permute-start | bytes 4374536 | tf_op jit(solution)/shard_map/ppermute | solution.py:535
  273.5 17.2 %collective-permute-start.7 = (bf16[1024,256]{1,0:T(8,128)(2,1)}, bf16[1024,256]{1,0:T(8,128)(2,1)S(1)}, u32[]{:S(2)}, u32[]{:S(2)}) collective-permute-start(bf16[1024,256]{1,0:T(8,128)(2,1)} %get-tuple-element.90), channel_id=1, source_target_pairs={{0,4},{4,0},{8,12},{12,8},{16,20},{20,16},{24,28},{28,24},{1,5},{5... | collective-permute-start | bytes 1572872 | tf_op jit(solution)/shard_map/ppermute | solution.py:579
  283.7 18.8 %collective-permute-start.13 = (bf16[8,356,128]{2,0,1:T(8,128)(2,1)}, bf16[8,356,128]{2,0,1:T(8,128)(2,1)}, u32[]{:S(2)}, u32[]{:S(2)}) collective-permute-start(bf16[8,356,128]{2,0,1:T(8,128)(2,1)} %copy.98), channel_id=1, source_target_pairs={{0,2},{1,3},{2,0},{3,1},{4,6},{5,7},{6,4},{7,5},{8,10},{9,11},{10,... | collective-permute-start | bytes 2187272 | tf_op jit(solution)/shard_map/ppermute | solution.py:535
  292.8 17.3 %collective-permute-start.12 = (bf16[1024,256]{1,0:T(8,128)(2,1)S(1)}, bf16[1024,256]{1,0:T(8,128)(2,1)}, u32[]{:S(2)}, u32[]{:S(2)}) collective-permute-start(bf16[1024,256]{1,0:T(8,128)(2,1)S(1)} %add_convert_fusion.3.rest_0_), channel_id=1, source_target_pairs={{0,16},{4,20},{16,24},{20,28},{24,8},{28,12},{8,0},{12,4},{1,17},{... | collective-permute-start | bytes 1572872 | tf_op jit(solution)/shard_map/ppermute | solution.py:574
  294.5 15.6 %collective-permute-start.11 = (bf16[1024,256]{1,0:T(8,128)(2,1)}, bf16[1024,256]{1,0:T(8,128)(2,1)}, u32[]{:S(2)}, u32[]{:S(2)}) collective-permute-start(bf16[1024,256]{1,0:T(8,128)(2,1)} %get-tuple-element.100), channel_id=1, source_target_pairs={{0,4},{4,0},{8,12},{12,8},{16,20},{20,16},{24,28},{28,24},{1,5},{5... | collective-permute-start | bytes 1572872 | tf_op jit(solution)/shard_map/ppermute | solution.py:579
  304.6 38.8 %all-to-all-start.1 = ((bf16[8,356,128]{2,1,0:T(8,128)(2,1)}), bf16[8,356,128]{2,1,0:T(8,128)(2,1)S(1)}, u32[]{:S(2)}, u32[]{:S(2)}) async-start(bf16[8,356,128]{2,1,0:T(8,128)(2,1)} %add_convert_fusion), calls=%async_computation.1 | async-start | bytes 1474560 | tf_op jit(solution)/shard_map/all_to_all | solution.py:764
  310.0 41.1 %copy-start.2 = (bf16[1,1024,256]{2,1,0:T(8,128)(2,1)S(1)}, bf16[1,1024,256]{2,1,0:T(8,128)(2,1)}, u32[]{:S(2)}) copy-start(bf16[1,1024,256]{2,1,0:T(8,128)(2,1)} %param.30) | copy-start | bytes 1572868
  310.0 41.1 %copy-start.3 = (f32[1024,256]{1,0:T(8,128)S(1)}, f32[1024,256]{1,0:T(8,128)}, u32[]{:S(2)}) copy-start(f32[1024,256]{1,0:T(8,128)} %get-tuple-element.87) | copy-start | bytes 3145732
  310.0 41.1 %copy-start.7 = (bf16[1024,256]{1,0:T(8,128)(2,1)S(1)}, bf16[1024,256]{1,0:T(8,128)(2,1)}, u32[]{:S(2)}) copy-start(bf16[1024,256]{1,0:T(8,128)(2,1)} %get-tuple-element.97) | copy-start | bytes 1572868
  311.8 21.1 %collective-permute-start.14 = (bf16[1024,256]{1,0:T(8,128)(2,1)S(1)}, bf16[1024,256]{1,0:T(8,128)(2,1)S(1)}, u32[]{:S(2)}, u32[]{:S(2)}) collective-permute-start(bf16[1024,256]{1,0:T(8,128)(2,1)S(1)} %add_convert_fusion.2), channel_id=1, source_target_pairs={{0,16},{4,20},{16,24},{20,28},{24,8},{28,12},{8,0},{12,4},{1,17},{... | collective-permute-start | bytes 1572872 | tf_op jit(solution)/shard_map/ppermute | solution.py:574
  314.7 18.2 %collective-permute-start.10 = (bf16[1024,256]{1,0:T(8,128)(2,1)}, bf16[1024,256]{1,0:T(8,128)(2,1)S(1)}, u32[]{:S(2)}, u32[]{:S(2)}) collective-permute-start(bf16[1024,256]{1,0:T(8,128)(2,1)} %get-tuple-element.99), channel_id=1, source_target_pairs={{0,4},{4,0},{8,12},{12,8},{16,20},{20,16},{24,28},{28,24},{1,5},{5... | collective-permute-start | bytes 1572872 | tf_op jit(solution)/shard_map/ppermute | solution.py:579
  335.0 16.2 %collective-permute-start.15 = (bf16[1024,256]{1,0:T(8,128)(2,1)}, bf16[1024,256]{1,0:T(8,128)(2,1)S(1)}, u32[]{:S(2)}, u32[]{:S(2)}) collective-permute-start(bf16[1024,256]{1,0:T(8,128)(2,1)} %add_convert_fusion.1), channel_id=1, source_target_pairs={{0,16},{4,20},{16,24},{20,28},{24,8},{28,12},{8,0},{12,4},{1,17},{... | collective-permute-start | bytes 1572872 | tf_op jit(solution)/shard_map/ppermute | solution.py:574
  338.4 12.8 %collective-permute-start.9 = (bf16[1024,256]{1,0:T(8,128)(2,1)}, bf16[1024,256]{1,0:T(8,128)(2,1)}, u32[]{:S(2)}, u32[]{:S(2)}) collective-permute-start(bf16[1024,256]{1,0:T(8,128)(2,1)} %get-tuple-element.98), channel_id=1, source_target_pairs={{0,4},{4,0},{8,12},{12,8},{16,20},{20,16},{24,28},{28,24},{1,5},{5... | collective-permute-start | bytes 1572872 | tf_op jit(solution)/shard_map/ppermute | solution.py:579
  343.5 9.2 %collective-permute-start.16 = (f32[356,128]{1,0:T(8,128)S(1)}, f32[356,128]{1,0:T(8,128)S(1)}, u32[]{:S(2)}, u32[]{:S(2)}) collective-permute-start(f32[356,128]{1,0:T(8,128)S(1)} %convert_reduce_fusion), channel_id=1, source_target_pairs={{0,2},{1,3},{2,0},{3,1},{4,6},{5,7},{6,4},{7,5},{8,10},{9,11},{10,... | collective-permute-start | bytes 546824 | tf_op jit(solution)/shard_map/ppermute | solution.py:535
  352.8 2.7 collective-permute-start.17
  (17 other events, 64.3 us)
Sparse Core Ops, SparseCore 0:
  13.0 88.7 all-gather.2

commit v3 on v2

--- a/solution.py
+++ b/solution.py
@@ -31,6 +31,7 @@
 BLOCK = 128
 GROUP = 1024
 UNROLL = 16
+STRIDE = 5
 VMEM_BYTES = 60 * 1024 * 1024
 
 F32 = jnp.float32
@@ -87,7 +88,7 @@
 ):
     step = pl.program_id(0)
     scaling = HEAD_DIM ** (-0.5)
-    slots = stage.shape[0] // (4 * BLOCK)
+    slots = stage.shape[0] // (STRIDE * BLOCK)
     pairs = slots * HEADS
 
     @pl.when(step == 0)
@@ -120,21 +121,21 @@
             for inner in range(UNROLL):
                 row = turn * UNROLL + inner
                 at = pl.multiple_of(idx_ref[base + row], 4)
-                stage[pl.ds(pl.multiple_of(row * 4, 4), 4), :] = rows[pl.ds(at, 4), :]
+                stage[pl.ds(row * STRIDE, 4), :] = rows[pl.ds(at, 4), :]
             return carry
 
         lax.fori_loop(0, total // UNROLL, fetch, 0)
 
         def staged(slot, part):
-            first = slot * (4 * BLOCK) + 2 * part
+            first = slot * (STRIDE * BLOCK) + 2 * part
             return jnp.concatenate(
-                [stage[pl.ds(first + half, BLOCK, stride=4), :] for half in (0, 1)], axis=1
+                [stage[pl.ds(first + half, BLOCK, stride=STRIDE), :] for half in (0, 1)], axis=1
             )
 
         def put(slot, part, value):
-            first = slot * (4 * BLOCK) + 2 * part
+            first = slot * (STRIDE * BLOCK) + 2 * part
             for half in (0, 1):
-                stage[pl.ds(first + half, BLOCK, stride=4), :] = value[
+                stage[pl.ds(first + half, BLOCK, stride=STRIDE), :] = value[
                     :, half * LANES : (half + 1) * LANES
                 ]
 
@@ -235,7 +236,7 @@
             for inner in range(UNROLL):
                 row = turn * UNROLL + inner
                 at = pl.multiple_of(idx_ref[base + row], 4)
-                rows[pl.ds(at, 4), :] = stage[pl.ds(pl.multiple_of(row * 4, 4), 4), :]
+                rows[pl.ds(at, 4), :] = stage[pl.ds(row * STRIDE, 4), :]
             return carry
 
         lax.fori_loop(0, total // UNROLL, spill, 0)
@@ -482,7 +483,7 @@
         ],
         scratch_shapes=[
             pltpu.VMEM((edges * 4 + 8, LANES), F32),
-            pltpu.VMEM((slots * BLOCK * 4 + 8, LANES), F32),
+            pltpu.VMEM((slots * BLOCK * STRIDE + 8, LANES), F32),
             pltpu.VMEM((BLOCK, slots * H), BF16),
             pltpu.VMEM((slots * HEADS, slots * H), BF16),
             pltpu.VMEM((slots * H, slots * HEADS), BF16),
@@ -535,6 +536,28 @@
     return lax.ppermute(array, "rep", [(r, r ^ (1 << bit)) for r in range(size)])
 
 
+def first_exchange(held):
+    bit = halves(lax.axis_size("rep"))[-1]
+    return {0: held, 1 << bit: across(held, bit)}
+
+
+def share_rows(shares):
+    reps = lax.axis_size("rep")
+    me = lax.axis_index("rep")
+    held = shares[0]
+    for bit in reversed(halves(reps)[:-1]):
+        shares = shares | {
+            number | (1 << bit): across(array, bit) for number, array in shares.items()
+        }
+    ordered = []
+    for batch in range(reps):
+        share = held
+        for number in range(1, reps):
+            share = jnp.where(me ^ batch == number, shares[number], share)
+        ordered.append(share)
+    return jnp.concatenate(ordered, axis=1)
+
+
 def behind(array, other):
     return lax.optimization_barrier((array, other))[0]
 
@@ -544,6 +567,15 @@
     upper = (lax.axis_index("rep") >> bit) & 1
     sent = lax.dynamic_slice_in_dim(totals, (1 - upper) * half, half, 1)
     return lax.dynamic_slice_in_dim(totals, upper * half, half, 1), sent.astype(BF16)
+
+
+def ring_rows(totals, order, turns, running):
+    for turn in turns:
+        total = lax.dynamic_index_in_dim(totals, order[2 * turn] >> 1, 0, keepdims=False)
+        if running is not None:
+            total = total + ring_step(running.astype(BF16)).astype(F32)
+        running = total
+    return running
 
 
 def gather_back(held):
@@ -648,15 +680,6 @@
     thin = jnp.broadcast_to(
         jnp.pad(thin, ((0, 0), (0, 7), (0, H - thin.shape[2]))), (owners, 8, H)
     )
-    meta = jnp.concatenate([meta.reshape(owners, meta_rows, H), thin], axis=1)
-    meta = lax.all_to_all(meta, "edge", 0, 0, tiled=True)
-    small = meta[:, meta_rows, : 3 * wr].reshape(owners, 3, wr)
-    small = small.transpose(1, 0, 2).reshape(3, H)
-    small = jnp.pad(small.astype(F32), ((0, 5), (0, 0)))
-    pieces = meta[:, :meta_rows].reshape(owners, 5, sent).astype(F32)
-    dist = pieces[:, 0] + pieces[:, 1] + pieces[:, 2]
-    source = pieces[:, 3] * 32.0 + pieces[:, 4]
-
     basis_rows = jnp.pad(basis_weight.T.astype(BF16), ((0, 0), (0, NB_ROWS - NB)))
     weight_rows = jnp.concatenate(
         [
@@ -668,7 +691,50 @@
         ],
         axis=0,
     )
-    weight_rows = lax.all_gather(weight_rows, "edge", axis=0)
+    short = -weight_rows.shape[0] % (8 * lax.axis_size("rep"))
+    weight_rows = jnp.pad(weight_rows, ((0, short), (0, 0)))
+
+    reps = lax.axis_size("rep")
+    share = weight_rows.shape[0] // reps
+    share = lax.dynamic_slice_in_dim(weight_rows, lax.axis_index("rep") * share, share, 0)
+    share = jnp.broadcast_to(share[None], (owners, *share.shape))
+    meta = jnp.concatenate([meta.reshape(owners, meta_rows, H), thin, share], axis=1)
+    meta = lax.all_to_all(meta, "edge", 0, 0, tiled=True)
+    share = meta[:, meta_rows + 8 :]
+    small = meta[:, meta_rows, : 3 * wr].reshape(owners, 3, wr)
+    small = small.transpose(1, 0, 2).reshape(3, H)
+    small = jnp.pad(small.astype(F32), ((0, 5), (0, 0)))
+    pieces = meta[:, :meta_rows].reshape(owners, 5, sent).astype(F32)
+    dist = pieces[:, 0] + pieces[:, 1] + pieces[:, 2]
+    source = pieces[:, 3] * 32.0 + pieces[:, 4]
+
+    size = min(GROUP, sent)
+    dist_cols, src_cols = (
+        values.reshape(owners, sent // size, size // LANES, LANES).transpose(0, 1, 3, 2)
+        for values in (dist, source)
+    )
+    src_rows = source[:, None]
+
+    table = arrival_order(owners)
+    me = lax.axis_index("edge")
+    order = jnp.asarray(table)[me]
+    place = jnp.asarray(np.argsort(table, axis=1).astype(np.int32))[me]
+    turns = owners // 2
+    kept, shares = (), first_exchange(share)
+    pair = (features, pair_swap(features))
+    for turn in range(turns):
+        coming = None
+        if turn < turns - 1:
+            ahead = ring_step(pair[0])
+            *pair, ahead, order, kept = lax.optimization_barrier((*pair, ahead, order, kept))
+            coming = (ahead, pair_swap(ahead))
+        kept = (run_edges_forward(2 * turn, order, pair, small, dist_cols, src_cols, kept),)
+        if turn == 1:
+            *kept, shares = lax.optimization_barrier((*kept, shares))
+            weight_rows = share_rows(shares)
+        pair = coming
+    (kept,) = kept
+
     at = 0
     fulls = []
     for width, rows in ((H, wa), (NB_ROWS, wb), (H, wg), (FF, wd), (H, wo)):
@@ -678,36 +744,6 @@
     attention_rows, basis_rows, gateup_rows, down_rows, output_rows = fulls
     query_rows, kv_rows = attention_rows[:H], attention_rows[H:]
     wide = jnp.concatenate([kv_rows, basis_rows[:, :NB_PAD]], axis=1)
-
-    size = min(GROUP, sent)
-    dist_cols, src_cols = (
-        values.reshape(owners, sent // size, size // LANES, LANES).transpose(0, 1, 3, 2)
-        for values in (dist, source)
-    )
-    src_rows = source[:, None]
-
-    table = arrival_order(owners)
-    me = lax.axis_index("edge")
-    order = jnp.asarray(table)[me]
-    place = jnp.asarray(np.argsort(table, axis=1).astype(np.int32))[me]
-    turns = owners // 2
-    arrivals = [features]
-    if turns > 1:
-        arrivals.append(ring_step(features))
-    swapped = [pair_swap(array) for array in arrivals]
-    ahead = ring_step(arrivals[1]) if turns > 2 else None
-    kept = run_edges_forward(0, order, [features], small, dist_cols, src_cols, ())
-    kept = run_edges_forward(1, order, [swapped[0]], small, dist_cols, src_cols, (kept,))
-    if turns > 1:
-        sources = [arrivals[1], swapped[1]]
-        if turns > 2:
-            ahead, kept = lax.optimization_barrier((ahead, kept))
-        kept = run_edges_forward(2, order, sources, small, dist_cols, src_cols, (kept,))
-    for turn in range(2, turns):
-        sources = [ahead, pair_swap(ahead)]
-        if turn < turns - 1:
-            ahead, kept = lax.optimization_barrier((ring_step(ahead), kept))
-        kept = run_edges_forward(2 * turn, order, sources, small, dist_cols, src_cols, (kept,))
 
     slot_ids = slot_index[0]
     slot_owner = slot_ids // sent
@@ -760,14 +796,22 @@
     for bit in bits[1:]:
         totals, sent_rows = halve(totals, bit)
         totals = totals + across(sent_rows, bit).astype(F32)
-    totals = totals.astype(BF16)
-    pieces = lax.all_to_all(totals, "edge", 0, 0, tiled=True)
-    latest = totals
+    side = me & 1
+    totals = totals.reshape(turns, 2, *totals.shape[1:])
+    sent_rows = lax.dynamic_index_in_dim(totals, 1 - side, 1, keepdims=False).astype(BF16)
+    totals = lax.dynamic_index_in_dim(totals, side, 1, keepdims=False)
+    fetched = pair_swap(sent_rows)
+    latest, held = sent_rows, None
     for number in range(turns - 3, turns):
-        if number == turns - 1:
-            latest = held = jnp.sum(pieces.astype(F32), axis=0)
         total = add_pair(number, latest)
         running = total.astype(BF16)
+        if number == turns - 3:
+            totals = totals + behind(fetched, running).astype(F32)
+            held = ring_rows(totals, order, turns_back[:1], None)
+        elif number == turns - 2:
+            held = ring_rows(totals, order, turns_back[1:-1], behind(held, running))
+        latest = held
+    held = ring_rows(totals, order, turns_back[-1:], held)
     d_from_edges = total
     held, fetched = gather_back(held)
 

time: 369 us -> 365 us (0.989)
  between operations: 14.7 us -> 4.16 us
  waiting for transfers between devices: 55.5 us -> 64.5 us
  other arithmetic: 26.7 us -> 31.6 us
    ppermute x6 -> x9, waiting for transfers between devices: 40.3 us -> 15 us  [ring_step(): return lax.ppermute(array, 'edge', moves)]
    ppermute x8 -> x9, waiting for transfers between devices: 4.95 us -> 29 us  [pair_swap(): return lax.ppermute(array, 'edge', [(e, e ^ 1) for e in range(owners)])]
    ppermute x4 -> x7, waiting for transfers between devices: 0.84 us -> 6.29 us  [across(): return lax.ppermute(array, 'rep', [(r, r ^ 1 << bit) for r in range(size)])]
    all_to_all x1 -> x0, starting transfers between devices: 5.42 us -> none  [local(): pieces = lax.all_to_all(totals, 'edge', 0, 0, tiled=True)]
    all_to_all x1, waiting for transfers between devices: 9.4 us -> 14.1 us  [local(): meta = lax.all_to_all(meta, 'edge', 0, 0, tiled=True)]
    pallas_call x5 -> x4, Pallas kernels: 36.5 us -> 34 us  [run_edges_forward(): pl.pallas_call(functools.partial(edges_forward, count), grid_spec=pltpu.P...]
    ppermute x6 -> x9, starting transfers between devices: 12.9 us -> 15.1 us  [ring_step(): return lax.ppermute(array, 'edge', moves)]
    unnamed x65 -> x71, local copies, waits for them, and re-layouts: 7.57 us -> 6.38 us
  transfers between devices with their start and end apart: 21 -> 26, of which waited for: 7 -> 14; matrix products, arithmetic and copies ran while one was open for 9% -> 9% of each run, Pallas kernels for 16% -> 16%
where the time goes in v3:
time: 365 us; the launch traced here: 363 us
  Pallas kernels  200 us (55%)
  waiting for transfers between devices  64.5 us (18%)
  starting transfers between devices  37.3 us (10%)
  other arithmetic  31.6 us (9%)
  local copies, waits for them, and re-layouts  25.4 us (7%)
  between operations  4.16 us (1%)
    pallas_call x1, Pallas kernels, run_atoms(): pl.pallas_call(functools.partial(atoms_kernel, ins, blocks, outs, owners)...  140 us
    pallas_call x4, Pallas kernels, run_edges_forward(): pl.pallas_call(functools.partial(edges_forward, count), grid_spec=pltpu.P...  34 us
    ppermute x9, waiting for transfers between devices, pair_swap(): return lax.ppermute(array, 'edge', [(e, e ^ 1) for e in range(owners)])  29 us
    pallas_call x4, Pallas kernels, run_edges_backward(): pl.pallas_call(edges_backward, grid_spec=pltpu.PrefetchScalarGridSpec(num...  22.4 us
    ppermute x9, starting transfers between devices, ring_step(): return lax.ppermute(array, 'edge', moves)  15.1 us
    ppermute x9, waiting for transfers between devices, ring_step(): return lax.ppermute(array, 'edge', moves)  15 us
    all_to_all x1, waiting for transfers between devices, local(): meta = lax.all_to_all(meta, 'edge', 0, 0, tiled=True)  14.1 us
    ppermute x9, starting transfers between devices, pair_swap(): return lax.ppermute(array, 'edge', [(e, e ^ 1) for e in range(owners)])  11.5 us
  transfers between devices with their start and end apart: 26, of which 14 were waited for; matrix products, arithmetic and copies ran while one was open for 9% of the time, Pallas kernels for 16%

profile of v3, /device:TPU:0, one launch (start us, length us, event | category | flops | bytes accessed | tf_op | source)
XLA Modules:
  0.0 363.2 jit_solution(8858462491096124529)
XLA Ops:
  7.9 7.3 %all-to-all-start = ((bf16[8,224,256]{2,1,0:T(8,128)(2,1)}), bf16[8,224,256]{2,1,0:T(8,128)(2,1)S(1)}, u32[]{:S(2)}, u32[]{:S(2)}) async-start(bf16[8,224,256]{2,1,0:T(8,128)(2,1)} %pad_maximum_fusion.2), calls=%async_computation | async-start | bytes 1835008 | tf_op jit(solution)/shard_map/all_to_all | solution.py:702
  15.2 2.0 collective-permute-start
  17.3 2.4 collective-permute-start.1
  20.8 17.8 %collective-permute-done.rest_1_ = bf16[1024,256]{1,0:T(8,128)(2,1)S(1)} collective-permute-done((bf16[1024,256]{1,0:T(8,128)(2,1)S(1)}, bf16[1024,256]{1,0:T(8,128)(2,1)S(1)}, u32[]{:S(2)}, u32[]{:S(2)}) %collective-permute-start) | collective-permute-done | bytes 524320 | tf_op jit(solution)/shard_map/ppermute | solution.py:611
  38.6 2.7 collective-permute-done.1.rest_0_
  43.2 3.5 collective-permute-start.3
  46.6 14.1 %all-to-all-done = bf16[8,224,256]{2,1,0:T(8,128)(2,1)S(1)} async-done(((bf16[8,224,256]{2,1,0:T(8,128)(2,1)}), bf16[8,224,256]{2,1,0:T(8,128)(2,1)S(1)}, u32[]{:S(2)}, u32[]{:S(2)}) %all-to-all-start) | async-done | bytes 917536 | tf_op jit(solution)/shard_map/all_to_all | solution.py:702
  66.8 8.5 %shard_map.509.rest_2_ = bf16[16384,896]{1,0:T(8,128)(2,1)} custom-call(s32[8]{0:T(128)} %fusion.17.order_ref, f32[8,256]{1,0:T(8,128)} %pad.14.small_ref, f32[8,2,128,8]{3,2,1,0:T(8,128)} %bitcast.128, f32[8,2,128,8]{3,2,1,0:T(8,128)} %bitcast.132, bf16[1024,256]{1,0:T(8,128)(2,1)} %bitcast.138, bf16[1024,256]{1,0:T(8,128)(2,1)} %copy-done.17), custom_call_target="tpu_custom_call" | custom-call | flops 2147483648 | bytes 8388608 | tf_op jit(solution)/shard_map/pallas_call | solution.py:404
  77.4 8.6 %shard_map.510.rest_2_ = bf16[16384,896]{1,0:T(8,128)(2,1)} custom-call(s32[8]{0:T(128)} %fusion.17.order_ref, f32[8,256]{1,0:T(8,128)} %pad.14.small_ref, f32[8,2,128,8]{3,2,1,0:T(8,128)} %bitcast.129, f32[8,2,128,8]{3,2,1,0:T(8,128)} %bitcast.133, bf16[1024,256]{1,0:T(8,128)(2,1)} %collective-permute-done.1.rest_0_, ...), custom_call_target="tpu_custom_call", output_to_operand_aliasing={{}: (6, {})} | custom-call | flops 2147483648 | bytes 8388608 | tf_op jit(solution)/shard_map/pallas_call | solution.py:404
  91.2 5.3 %fusion.12 = s32[8,16,128]{2,0,1:T(8,128)S(1)} fusion(s32[2,8,8,128]{3,2,1,0:T(8,128)S(1)} %copy.112, s32[]{:T(128)} %bitcast.7, s32[]{:T(128)} %bitcast.6, s32[]{:T(128)} %bitcast.5, s32[]{:T(128)} %bitcast.4, s32[]{:T(128)} %bitcast.3, s32[]{:T(128)} %bitcast.2, s32[]{:T(128)} %bitcast.1, s32[]{:T(128)} %bitcast), kind=kLoop, calls=%fused_computation.53 | loop fusion | flops 737280 | bytes 131104 | tf_op jit(solution)/shard_map/mul | solution.py:752
  99.2 8.4 %shard_map.511.rest_2_ = bf16[16384,896]{1,0:T(8,128)(2,1)} custom-call(s32[8]{0:T(128)} %fusion.17.order_ref, f32[8,256]{1,0:T(8,128)} %pad.14.small_ref, f32[8,2,128,8]{3,2,1,0:T(8,128)} %bitcast.130, f32[8,2,128,8]{3,2,1,0:T(8,128)} %bitcast.134, bf16[1024,256]{1,0:T(8,128)(2,1)} %copy-done.14, ...), custom_call_target="tpu_custom_call", output_to_operand_aliasing={{}: (6, {})} | custom-call | flops 2147483648 | bytes 8388608 | tf_op jit(solution)/shard_map/pallas_call | solution.py:404
  108.5 8.5 %shard_map.512.kept_ref = bf16[16384,896]{1,0:T(8,128)(2,1)} custom-call(s32[8]{0:T(128)} %fusion.17.order_ref, f32[8,256]{1,0:T(8,128)} %pad.14.small_ref, f32[8,2,128,8]{3,2,1,0:T(8,128)} %bitcast.131, f32[8,2,128,8]{3,2,1,0:T(8,128)} %bitcast.135, bf16[1024,256]{1,0:T(8,128)(2,1)} %copy-done.15, ...), custom_call_target="tpu_custom_call", output_to_operand_aliasing={{}: (6, {})} | custom-call | flops 2147483648 | bytes 8388608 | tf_op jit(solution)/shard_map/pallas_call | solution.py:404
  125.3 2.0 pad_maximum_fusion.3.wide_ref
  127.3 140.4 %shard_map.513 = (bf16[1024,256]{1,0:T(8,128)(2,1)}, f32[1024,128]{1,0:T(8,128)}, f32[1024,256]{1,0:T(8,128)}, f32[1024,256]{1,0:T(8,128)}, bf16[16384,256]{1,0:...) custom-call(s32[16384]{0:T(1024)} %bitcast.163, s32[1]{0:T(128)} %bitcast.10.core_ref, ...), custom_call_target="tpu_custom_call" | custom-call | flops 52076478464 | bytes 71827456 | tf_op jit(solution)/shard_map/pallas_call | solution.py:448
  267.7 5.7 %shard_map.514 = (bf16[1024,256]{1,0:T(8,128)(2,1)}, bf16[1024,256]{1,0:T(8,128)(2,1)}) custom-call(s32[8]{0:T(128)} %fusion.17.order_ref, bf16[16384,256]{1,0:T(8,128)(2,1)} %get-tuple-element.116.rows_ref, f32[8,1,2048]{2,1,0:T(1,128)} %copy-done.6), custom_call_target="tpu_custom_call" | custom-call | flops 2147483648 | bytes 3145728 | tf_op jit(solution)/shard_map/pallas_call | solution.py:508
  274.3 5.6 %shard_map.515 = (bf16[1024,256]{1,0:T(8,128)(2,1)}, bf16[1024,256]{1,0:T(8,128)(2,1)}) custom-call(s32[8]{0:T(128)} %fusion.17.order_ref, bf16[16384,256]{1,0:T(8,128)(2,1)} %get-tuple-element.116.rows_ref, f32[8,1,2048]{2,1,0:T(1,128)} %copy-done.6), custom_call_target="tpu_custom_call" | custom-call | flops 2147483648 | bytes 3145728 | tf_op jit(solution)/shard_map/pallas_call | solution.py:508
  281.1 2.1 convert_add_fusion
  286.9 5.5 %shard_map.516 = (bf16[1024,256]{1,0:T(8,128)(2,1)}, bf16[1024,256]{1,0:T(8,128)(2,1)}) custom-call(s32[8]{0:T(128)} %fusion.17.order_ref, bf16[16384,256]{1,0:T(8,128)(2,1)} %get-tuple-element.116.rows_ref, f32[8,1,2048]{2,1,0:T(1,128)} %copy-done.6, bf16[8,356,128]{2,1,0:T(8,128)(2,1)} %copy-done), custom_call_target="tpu_custom_call" | custom-call | flops 2147483648 | bytes 3145728 | tf_op jit(solution)/shard_map/pallas_call | solution.py:508
  294.4 5.6 %shard_map.517 = (bf16[1024,256]{1,0:T(8,128)(2,1)}, bf16[1024,256]{1,0:T(8,128)(2,1)}) custom-call(s32[8]{0:T(128)} %fusion.17.order_ref, bf16[16384,256]{1,0:T(8,128)(2,1)} %get-tuple-element.116.rows_ref, f32[8,1,2048]{2,1,0:T(1,128)} %copy-done.6, bf16[1024,256]{1,0:T(8,128)(2,1)} %copy-done.7), custom_call_target="tpu_custom_call" | custom-call | flops 2147483648 | bytes 3145728 | tf_op jit(solution)/shard_map/pallas_call | solution.py:508
  300.0 3.9 %collective-permute-done.16 = bf16[8,356,128]{2,0,1:T(8,128)(2,1)} collective-permute-done((bf16[8,356,128]{2,0,1:T(8,128)(2,1)}, bf16[8,356,128]{2,0,1:T(8,128)(2,1)}, u32[]{:S(2)}, u32[]{:S(2)}) %collective-permute-start.16) | collective-permute-done | bytes 729120 | tf_op jit(solution)/shard_map/ppermute | solution.py:536
  307.7 2.1 add_convert_fusion.1
  313.5 4.7 %collective-permute-done.18 = bf16[4,356,128]{2,1,0:T(8,128)(2,1)} collective-permute-done((bf16[4,356,128]{2,1,0:T(8,128)(2,1)S(1)}, bf16[4,356,128]{2,1,0:T(8,128)(2,1)}, u32[]{:S(2)}, u32[]{:S(2)}) %collective-permute-start.18) | collective-permute-done | bytes 364576 | tf_op jit(solution)/shard_map/ppermute | solution.py:611
  319.3 3.6 collective-permute-done.17
  322.9 4.9 %collective-permute-done.13 = bf16[1024,256]{1,0:T(8,128)(2,1)} collective-permute-done((bf16[1024,256]{1,0:T(8,128)(2,1)}, bf16[1024,256]{1,0:T(8,128)(2,1)}, u32[]{:S(2)}, u32[]{:S(2)}) %collective-permute-start.13) | collective-permute-done | bytes 524320 | tf_op jit(solution)/shard_map/ppermute | solution.py:611
  327.8 2.0 add_convert_fusion
  331.7 2.7 collective-permute-done.20
  334.4 2.2 collective-permute-start.21
  337.2 2.0 collective-permute-done.21
  339.2 3.2 collective-permute-start.22
  350.3 2.3 collective-permute-done.23
  356.3 2.5 fusion.3
  359.5 3.5 shard_map.518
  (190 shorter events, 63.5 us)
Async XLA Ops:
  7.9 52.8 %all-to-all-start = ((bf16[8,224,256]{2,1,0:T(8,128)(2,1)}), bf16[8,224,256]{2,1,0:T(8,128)(2,1)S(1)}, u32[]{:S(2)}, u32[]{:S(2)}) async-start(bf16[8,224,256]{2,1,0:T(8,128)(2,1)} %pad_maximum_fusion.2), calls=%async_computation | async-start | bytes 1835008 | tf_op jit(solution)/shard_map/all_to_all | solution.py:702
  15.2 23.4 %collective-permute-start = (bf16[1024,256]{1,0:T(8,128)(2,1)S(1)}, bf16[1024,256]{1,0:T(8,128)(2,1)S(1)}, u32[]{:S(2)}, u32[]{:S(2)}) collective-permute-start(bf16[1024,256]{1,0:T(8,128)(2,1)S(1)} %bitcast.140), channel_id=1, source_target_pairs={{0,4},{4,0},{8,12},{12,8},{16,20},{20,16},{24,28},{28,24},{1,5},{5... | collective-permute-start | bytes 1572872 | tf_op jit(solution)/shard_map/ppermute | solution.py:611
  17.3 24.1 %collective-permute-start.1 = (bf16[1024,256]{1,0:T(8,128)(2,1)S(1)}, bf16[1024,256]{1,0:T(8,128)(2,1)}, u32[]{:S(2)}, u32[]{:S(2)}) collective-permute-start(bf16[1024,256]{1,0:T(8,128)(2,1)S(1)} %bitcast.141), channel_id=1, source_target_pairs={{0,16},{4,20},{16,24},{20,28},{24,8},{28,12},{8,0},{12,4},{1,17},{... | collective-permute-start | bytes 1572872 | tf_op jit(solution)/shard_map/ppermute | solution.py:606
  38.6 22.9 %copy-start.17 = (bf16[1024,256]{1,0:T(8,128)(2,1)}, bf16[1024,256]{1,0:T(8,128)(2,1)S(1)}, u32[]{:S(2)}) copy-start(bf16[1024,256]{1,0:T(8,128)(2,1)S(1)} %collective-permute-done.rest_1_) | copy-start | bytes 1572868
  41.4 33.9 %collective-permute-start.2 = (bf16[1024,256]{1,0:T(8,128)(2,1)}, bf16[1024,256]{1,0:T(8,128)(2,1)}, u32[]{:S(2)}, u32[]{:S(2)}) collective-permute-start(bf16[1024,256]{1,0:T(8,128)(2,1)} %collective-permute-done.1.rest_0_), channel_id=1, source_target_pairs={{0,4},{4,0},{8,12},{12,8},{16,20},{20,16},{24,28},{28,24},{1,5},{5... | collective-permute-start | bytes 1572872 | tf_op jit(solution)/shard_map/ppermute | solution.py:611
  43.2 32.1 %collective-permute-start.3 = (bf16[1024,256]{1,0:T(8,128)(2,1)}, bf16[1024,256]{1,0:T(8,128)(2,1)S(1)}, u32[]{:S(2)}, u32[]{:S(2)}) collective-permute-start(bf16[1024,256]{1,0:T(8,128)(2,1)} %collective-permute-done.1.rest_0_), channel_id=1, source_target_pairs={{0,16},{4,20},{16,24},{20,28},{24,8},{28,12},{8,0},{12,4},{1,17},{... | collective-permute-start | bytes 1572872 | tf_op jit(solution)/shard_map/ppermute | solution.py:606
  64.6 21.4 %collective-permute-start.6 = (bf16[8,176,256]{2,1,0:T(8,128)(2,1)S(1)}, bf16[8,176,256]{2,1,0:T(8,128)(2,1)S(1)}, u32[]{:S(2)}, u32[]{:S(2)}) collective-permute-start(bf16[8,176,256]{2,1,0:T(8,128)(2,1)S(1)} %slice.139), channel_id=1, source_target_pairs={{0,2},{1,3},{2,0},{3,1},{4,6},{5,7},{6,4},{7,5},{8,10},{9,11},{10,... | collective-permute-start | bytes 2162696 | tf_op jit(solution)/shard_map/ppermute | solution.py:536
  75.3 12.2 %collective-permute-start.4 = (bf16[1024,256]{1,0:T(8,128)(2,1)S(1)}, bf16[1024,256]{1,0:T(8,128)(2,1)S(1)}, u32[]{:S(2)}, u32[]{:S(2)}) collective-permute-start(bf16[1024,256]{1,0:T(8,128)(2,1)S(1)} %collective-permute-done.3.rest_0_), channel_id=1, source_target_pairs={{0,4},{4,0},{8,12},{12,8},{16,20},{20,16},{24,28},{28,24},{1,5},{5... | collective-permute-start | bytes 1572872 | tf_op jit(solution)/shard_map/ppermute | solution.py:611
  76.7 12.3 %collective-permute-start.5 = (bf16[1024,256]{1,0:T(8,128)(2,1)S(1)}, bf16[1024,256]{1,0:T(8,128)(2,1)S(1)}, u32[]{:S(2)}, u32[]{:S(2)}) collective-permute-start(bf16[1024,256]{1,0:T(8,128)(2,1)S(1)} %collective-permute-done.3.rest_0_), channel_id=1, source_target_pairs={{0,16},{4,20},{16,24},{20,28},{24,8},{28,12},{8,0},{12,4},{1,17},{... | collective-permute-start | bytes 1572872 | tf_op jit(solution)/shard_map/ppermute | solution.py:606
  86.0 21.7 %copy-start.12 = (bf16[8,176,256]{2,1,0:T(8,128)(2,1)}, bf16[8,176,256]{2,1,0:T(8,128)(2,1)S(1)}, u32[]{:S(2)}) copy-start(bf16[8,176,256]{2,1,0:T(8,128)(2,1)S(1)} %collective-permute-done.6) | copy-start | bytes 2162692
  89.0 18.7 %collective-permute-start.7 = (bf16[1024,256]{1,0:T(8,128)(2,1)S(1)}, bf16[1024,256]{1,0:T(8,128)(2,1)S(1)}, u32[]{:S(2)}, u32[]{:S(2)}) collective-permute-start(bf16[1024,256]{1,0:T(8,128)(2,1)S(1)} %collective-permute-done.5.rest_0_), channel_id=1, source_target_pairs={{0,4},{4,0},{8,12},{12,8},{16,20},{20,16},{24,28},{28,24},{1,5},{5... | collective-permute-start | bytes 1572872 | tf_op jit(solution)/shard_map/ppermute | solution.py:611
  90.1 26.8 %collective-permute-start.8 = (bf16[8,176,256]{2,1,0:T(8,128)(2,1)S(1)}, bf16[8,176,256]{2,1,0:T(8,128)(2,1)S(1)}, u32[]{:S(2)}, u32[]{:S(2)}) collective-permute-start(bf16[8,176,256]{2,1,0:T(8,128)(2,1)S(1)} %collective-permute-done.6), channel_id=1, source_target_pairs={{0,1},{1,0},{2,3},{3,2},{4,5},{5,4},{6,7},{7,6},{8,9},{9,8},{10,11... | collective-permute-start | bytes 2162696 | tf_op jit(solution)/shard_map/ppermute | solution.py:536
  90.1 27.7 %collective-permute-start.9 = (bf16[8,176,256]{2,1,0:T(8,128)(2,1)S(1)}, bf16[8,176,256]{2,1,0:T(8,128)(2,1)}, u32[]{:S(2)}, u32[]{:S(2)}) collective-permute-start(bf16[8,176,256]{2,1,0:T(8,128)(2,1)S(1)} %slice.139), channel_id=1, source_target_pairs={{0,1},{1,0},{2,3},{3,2},{4,5},{5,4},{6,7},{7,6},{8,9},{9,8},{10,11... | collective-permute-start | bytes 2162696 | tf_op jit(solution)/shard_map/ppermute | solution.py:536
  267.6 12.3 %collective-permute-start.11 = (bf16[5696,128]{1,0:T(8,128)(2,1)}, bf16[5696,128]{1,0:T(8,128)(2,1)S(1)}, u32[]{:S(2)}, u32[]{:S(2)}) collective-permute-start(bf16[5696,128]{1,0:T(8,128)(2,1)} %get-tuple-element.120), channel_id=1, source_target_pairs={{0,1},{1,0},{2,3},{3,2},{4,5},{5,4},{6,7},{7,6},{8,9},{9,8},{10,11... | collective-permute-start | bytes 4374536 | tf_op jit(solution)/shard_map/ppermute | solution.py:536
  273.4 19.0 %collective-permute-start.10 = (bf16[1024,256]{1,0:T(8,128)(2,1)}, bf16[1024,256]{1,0:T(8,128)(2,1)}, u32[]{:S(2)}, u32[]{:S(2)}) collective-permute-start(bf16[1024,256]{1,0:T(8,128)(2,1)} %get-tuple-element.118), channel_id=1, source_target_pairs={{0,4},{4,0},{8,12},{12,8},{16,20},{20,16},{24,28},{28,24},{1,5},{5... | collective-permute-start | bytes 1572872 | tf_op jit(solution)/shard_map/ppermute | solution.py:611
  285.2 18.7 %collective-permute-start.16 = (bf16[8,356,128]{2,0,1:T(8,128)(2,1)}, bf16[8,356,128]{2,0,1:T(8,128)(2,1)}, u32[]{:S(2)}, u32[]{:S(2)}) collective-permute-start(bf16[8,356,128]{2,0,1:T(8,128)(2,1)} %copy.108), channel_id=1, source_target_pairs={{0,2},{1,3},{2,0},{3,1},{4,6},{5,7},{6,4},{7,5},{8,10},{9,11},{10,... | collective-permute-start | bytes 2187272 | tf_op jit(solution)/shard_map/ppermute | solution.py:536
  285.8 21.9 %collective-permute-start.14 = (bf16[1024,256]{1,0:T(8,128)(2,1)}, bf16[1024,256]{1,0:T(8,128)(2,1)}, u32[]{:S(2)}, u32[]{:S(2)}) collective-permute-start(bf16[1024,256]{1,0:T(8,128)(2,1)} %get-tuple-element.128), channel_id=1, source_target_pairs={{0,4},{4,0},{8,12},{12,8},{16,20},{20,16},{24,28},{28,24},{1,5},{5... | collective-permute-start | bytes 1572872 | tf_op jit(solution)/shard_map/ppermute | solution.py:611
  293.6 14.1 %collective-permute-start.15 = (bf16[1024,256]{1,0:T(8,128)(2,1)S(1)}, bf16[1024,256]{1,0:T(8,128)(2,1)S(1)}, u32[]{:S(2)}, u32[]{:S(2)}) collective-permute-start(bf16[1024,256]{1,0:T(8,128)(2,1)S(1)} %add_convert_fusion.2.rest_0_), channel_id=1, source_target_pairs={{0,16},{4,20},{16,24},{20,28},{24,8},{28,12},{8,0},{12,4},{1,17},{... | collective-permute-start | bytes 1572872 | tf_op jit(solution)/shard_map/ppermute | solution.py:606
  306.5 21.3 %copy-start.20 = (bf16[1024,256]{1,0:T(8,128)(2,1)S(1)}, bf16[1024,256]{1,0:T(8,128)(2,1)}, u32[]{:S(2)}) copy-start(bf16[1024,256]{1,0:T(8,128)(2,1)} %get-tuple-element.123) | copy-start | bytes 1572868
  306.5 11.7 %collective-permute-start.18 = (bf16[4,356,128]{2,1,0:T(8,128)(2,1)S(1)}, bf16[4,356,128]{2,1,0:T(8,128)(2,1)}, u32[]{:S(2)}, u32[]{:S(2)}) collective-permute-start(bf16[4,356,128]{2,1,0:T(8,128)(2,1)S(1)} %fusion.5), channel_id=1, source_target_pairs={{0,4},{4,0},{8,12},{12,8},{16,20},{20,16},{24,28},{28,24},{1,5},{5... | collective-permute-start | bytes 1093640 | tf_op jit(solution)/shard_map/ppermute | solution.py:611
  309.8 13.1 %collective-permute-start.17 = (bf16[1024,256]{1,0:T(8,128)(2,1)}, bf16[1024,256]{1,0:T(8,128)(2,1)S(1)}, u32[]{:S(2)}, u32[]{:S(2)}) collective-permute-start(bf16[1024,256]{1,0:T(8,128)(2,1)} %add_convert_fusion.1), channel_id=1, source_target_pairs={{0,16},{4,20},{16,24},{20,28},{24,8},{28,12},{8,0},{12,4},{1,17},{... | collective-permute-start | bytes 1572872 | tf_op jit(solution)/shard_map/ppermute | solution.py:606
  310.7 17.1 %collective-permute-start.13 = (bf16[1024,256]{1,0:T(8,128)(2,1)}, bf16[1024,256]{1,0:T(8,128)(2,1)}, u32[]{:S(2)}, u32[]{:S(2)}) collective-permute-start(bf16[1024,256]{1,0:T(8,128)(2,1)} %get-tuple-element.127), channel_id=1, source_target_pairs={{0,4},{4,0},{8,12},{12,8},{16,20},{20,16},{24,28},{28,24},{1,5},{5... | collective-permute-start | bytes 1572872 | tf_op jit(solution)/shard_map/ppermute | solution.py:611
  329.8 24.9 %copy-start.2 = (bf16[1,1024,256]{2,1,0:T(8,128)(2,1)S(1)}, bf16[1,1024,256]{2,1,0:T(8,128)(2,1)}, u32[]{:S(2)}) copy-start(bf16[1,1024,256]{2,1,0:T(8,128)(2,1)} %param.30) | copy-start | bytes 1572868
  329.8 24.9 %copy-start.5 = (f32[1024,256]{1,0:T(8,128)S(1)}, f32[1024,256]{1,0:T(8,128)}, u32[]{:S(2)}) copy-start(f32[1024,256]{1,0:T(8,128)} %get-tuple-element.115) | copy-start | bytes 3145732
  329.8 24.9 %copy-start.8 = (bf16[1024,256]{1,0:T(8,128)(2,1)S(1)}, bf16[1024,256]{1,0:T(8,128)(2,1)}, u32[]{:S(2)}) copy-start(bf16[1024,256]{1,0:T(8,128)(2,1)} %get-tuple-element.125) | copy-start | bytes 1572868
  329.8 4.6 %collective-permute-start.20 = (bf16[356,128]{1,0:T(8,128)(2,1)S(1)}, bf16[356,128]{1,0:T(8,128)(2,1)S(1)}, u32[]{:S(2)}, u32[]{:S(2)}) collective-permute-start(bf16[356,128]{1,0:T(8,128)(2,1)S(1)} %dynamic-slice_bitcast_fusion), channel_id=1, source_target_pairs={{0,16},{4,20},{16,24},{20,28},{24,8},{28,12},{8,0},{12,4},{1,17},{... | collective-permute-start | bytes 273416 | tf_op jit(solution)/shard_map/ppermute | solution.py:606
  334.4 4.8 %collective-permute-start.21 = (bf16[356,128]{1,0:T(8,128)(2,1)S(1)}, bf16[356,128]{1,0:T(8,128)(2,1)S(1)}, u32[]{:S(2)}, u32[]{:S(2)}) collective-permute-start(bf16[356,128]{1,0:T(8,128)(2,1)S(1)} %fusion.6), channel_id=1, source_target_pairs={{0,16},{4,20},{16,24},{20,28},{24,8},{28,12},{8,0},{12,4},{1,17},{... | collective-permute-start | bytes 273416 | tf_op jit(solution)/shard_map/ppermute | solution.py:606
  339.2 7.0 %collective-permute-start.22 = (bf16[356,128]{1,0:T(8,128)(2,1)S(1)}, bf16[356,128]{1,0:T(8,128)(2,1)}, u32[]{:S(2)}, u32[]{:S(2)}) collective-permute-start(bf16[356,128]{1,0:T(8,128)(2,1)S(1)} %bitcast_add_fusion.3), channel_id=1, source_target_pairs={{0,16},{4,20},{16,24},{20,28},{24,8},{28,12},{8,0},{12,4},{1,17},{... | collective-permute-start | bytes 273416 | tf_op jit(solution)/shard_map/ppermute | solution.py:606
  343.7 11.0 %collective-permute-start.12 = (bf16[1024,256]{1,0:T(8,128)(2,1)}, bf16[1024,256]{1,0:T(8,128)(2,1)S(1)}, u32[]{:S(2)}, u32[]{:S(2)}) collective-permute-start(bf16[1024,256]{1,0:T(8,128)(2,1)} %get-tuple-element.126), channel_id=1, source_target_pairs={{0,4},{4,0},{8,12},{12,8},{16,20},{20,16},{24,28},{28,24},{1,5},{5... | collective-permute-start | bytes 1572872 | tf_op jit(solution)/shard_map/ppermute | solution.py:611
  344.3 10.4 %collective-permute-start.19 = (bf16[1024,256]{1,0:T(8,128)(2,1)}, bf16[1024,256]{1,0:T(8,128)(2,1)}, u32[]{:S(2)}, u32[]{:S(2)}) collective-permute-start(bf16[1024,256]{1,0:T(8,128)(2,1)} %add_convert_fusion), channel_id=1, source_target_pairs={{0,16},{4,20},{16,24},{20,28},{24,8},{28,12},{8,0},{12,4},{1,17},{... | collective-permute-start | bytes 1572872 | tf_op jit(solution)/shard_map/ppermute | solution.py:606
  347.1 5.6 %collective-permute-start.23 = (f32[356,128]{1,0:T(8,128)S(1)}, f32[356,128]{1,0:T(8,128)S(1)}, u32[]{:S(2)}, u32[]{:S(2)}) collective-permute-start(f32[356,128]{1,0:T(8,128)S(1)} %bitcast_add_fusion.1), channel_id=1, source_target_pairs={{0,2},{1,3},{2,0},{3,1},{4,6},{5,7},{6,4},{7,5},{8,10},{9,11},{10,... | collective-permute-start | bytes 546824 | tf_op jit(solution)/shard_map/ppermute | solution.py:536
  352.8 6.0 %collective-permute-start.24 = (f32[712,128]{1,0:T(8,128)S(1)}, f32[712,128]{1,0:T(8,128)S(1)}, u32[]{:S(2)}, u32[]{:S(2)}) collective-permute-start(f32[712,128]{1,0:T(8,128)S(1)} %pad_maximum_fusion.5.held_ref), channel_id=1, source_target_pairs={{0,1},{1,0},{2,3},{3,2},{4,5},{5,4},{6,7},{7,6},{8,9},{9,8},{10,11... | collective-permute-start | bytes 1093640 | tf_op jit(solution)/shard_map/ppermute | solution.py:536
  (28 other events, 163.9 us)

commit v4 on v3

--- a/solution.py
+++ b/solution.py
@@ -31,7 +31,6 @@
 BLOCK = 128
 GROUP = 1024
 UNROLL = 16
-STRIDE = 5
 VMEM_BYTES = 60 * 1024 * 1024
 
 F32 = jnp.float32
@@ -88,7 +87,7 @@
 ):
     step = pl.program_id(0)
     scaling = HEAD_DIM ** (-0.5)
-    slots = stage.shape[0] // (STRIDE * BLOCK)
+    slots = stage.shape[0] // (4 * BLOCK)
     pairs = slots * HEADS
 
     @pl.when(step == 0)
@@ -121,21 +120,21 @@
             for inner in range(UNROLL):
                 row = turn * UNROLL + inner
                 at = pl.multiple_of(idx_ref[base + row], 4)
-                stage[pl.ds(row * STRIDE, 4), :] = rows[pl.ds(at, 4), :]
+                stage[pl.ds(pl.multiple_of(row * 4, 4), 4), :] = rows[pl.ds(at, 4), :]
             return carry
 
         lax.fori_loop(0, total // UNROLL, fetch, 0)
 
         def staged(slot, part):
-            first = slot * (STRIDE * BLOCK) + 2 * part
+            first = slot * (4 * BLOCK) + 2 * part
             return jnp.concatenate(
-                [stage[pl.ds(first + half, BLOCK, stride=STRIDE), :] for half in (0, 1)], axis=1
+                [stage[pl.ds(first + half, BLOCK, stride=4), :] for half in (0, 1)], axis=1
             )
 
         def put(slot, part, value):
-            first = slot * (STRIDE * BLOCK) + 2 * part
+            first = slot * (4 * BLOCK) + 2 * part
             for half in (0, 1):
-                stage[pl.ds(first + half, BLOCK, stride=STRIDE), :] = value[
+                stage[pl.ds(first + half, BLOCK, stride=4), :] = value[
                     :, half * LANES : (half + 1) * LANES
                 ]
 
@@ -236,7 +235,7 @@
             for inner in range(UNROLL):
                 row = turn * UNROLL + inner
                 at = pl.multiple_of(idx_ref[base + row], 4)
-                rows[pl.ds(at, 4), :] = stage[pl.ds(row * STRIDE, 4), :]
+                rows[pl.ds(at, 4), :] = stage[pl.ds(pl.multiple_of(row * 4, 4), 4), :]
             return carry
 
         lax.fori_loop(0, total // UNROLL, spill, 0)
@@ -483,7 +482,7 @@
         ],
         scratch_shapes=[
             pltpu.VMEM((edges * 4 + 8, LANES), F32),
-            pltpu.VMEM((slots * BLOCK * STRIDE + 8, LANES), F32),
+            pltpu.VMEM((slots * BLOCK * 4 + 8, LANES), F32),
             pltpu.VMEM((BLOCK, slots * H), BF16),
             pltpu.VMEM((slots * HEADS, slots * H), BF16),
             pltpu.VMEM((slots * H, slots * HEADS), BF16),
@@ -667,6 +666,21 @@
         readout_weight.shape[0],
     )
 
+    table = arrival_order(owners)
+    me = lax.axis_index("edge")
+    order = jnp.asarray(table)[me]
+    place = jnp.asarray(np.argsort(table, axis=1).astype(np.int32))[me]
+    turns = owners // 2
+    slot_ids = slot_index[0]
+    slot_owner = slot_ids // sent
+    arrived = sum(jnp.where(slot_owner == s, place[s], 0) for s in range(owners))
+    arrived = arrived * sent + slot_ids % sent
+    idx = arrived.reshape(atoms // BLOCK, BLOCK, slots).transpose(0, 2, 1).reshape(-1) * 4
+    live_count = jnp.sum(live_mask[0], axis=1, keepdims=True).astype(F32)
+    energy_rows = energy_cot[0][:, None]
+    pair = (features, pair_swap(features))
+    ahead = ring_step(features)
+
     dist = distances[0]
     high = lax.reduce_precision(dist, 8, 7)
     middle = lax.reduce_precision(dist - high, 8, 7)
@@ -699,6 +713,7 @@
     share = lax.dynamic_slice_in_dim(weight_rows, lax.axis_index("rep") * share, share, 0)
     share = jnp.broadcast_to(share[None], (owners, *share.shape))
     meta = jnp.concatenate([meta.reshape(owners, meta_rows, H), thin, share], axis=1)
+    meta, *pair, ahead = lax.optimization_barrier((meta, *pair, ahead))
     meta = lax.all_to_all(meta, "edge", 0, 0, tiled=True)
     share = meta[:, meta_rows + 8 :]
     small = meta[:, meta_rows, : 3 * wr].reshape(owners, 3, wr)
@@ -715,17 +730,15 @@
     )
     src_rows = source[:, None]
 
-    table = arrival_order(owners)
-    me = lax.axis_index("edge")
-    order = jnp.asarray(table)[me]
-    place = jnp.asarray(np.argsort(table, axis=1).astype(np.int32))[me]
-    turns = owners // 2
     kept, shares = (), first_exchange(share)
-    pair = (features, pair_swap(features))
+    order, idx, live_count, energy_rows = lax.optimization_barrier(
+        (order, idx, live_count, energy_rows)
+    )
     for turn in range(turns):
         coming = None
         if turn < turns - 1:
-            ahead = ring_step(pair[0])
+            if turn > 0:
+                ahead = ring_step(pair[0])
             *pair, ahead, order, kept = lax.optimization_barrier((*pair, ahead, order, kept))
             coming = (ahead, pair_swap(ahead))
         kept = (run_edges_forward(2 * turn, order, pair, small, dist_cols, src_cols, kept),)
@@ -745,12 +758,6 @@
     query_rows, kv_rows = attention_rows[:H], attention_rows[H:]
     wide = jnp.concatenate([kv_rows, basis_rows[:, :NB_PAD]], axis=1)
 
-    slot_ids = slot_index[0]
-    slot_owner = slot_ids // sent
-    arrived = sum(jnp.where(slot_owner == s, place[s], 0) for s in range(owners))
-    arrived = arrived * sent + slot_ids % sent
-    idx = arrived.reshape(atoms // BLOCK, BLOCK, slots).transpose(0, 2, 1).reshape(-1) * 4
-    count = jnp.sum(live_mask[0], axis=1, keepdims=True).astype(F32)
     core = (lax.axis_index("rep") & 1).astype(jnp.int32)[None]
     block_out, energy, d_after, d_normed_own, d_rows, grads_mine, grads_theirs = run_atoms(
         owners,
@@ -759,8 +766,8 @@
         kept,
         features,
         output_cot[0],
-        energy_cot[0][:, None],
-        count,
+        energy_rows,
+        live_count,
         small,
         wide,
         query_rows,

time: 365 us -> 353 us (0.967)
  waiting for transfers between devices: 64.5 us -> 55.7 us
    ppermute x9, waiting for transfers between devices: 29 us -> 13.7 us  [pair_swap(): return lax.ppermute(array, 'edge', [(e, e ^ 1) for e in range(owners)])]
    all_to_all x1, waiting for transfers between devices: 14.1 us -> 20.4 us  [local(): meta = lax.all_to_all(meta, 'edge', 0, 0, tiled=True)]
  transfers between devices with their start and end apart: 26 -> 26, of which waited for: 14 -> 15; matrix products, arithmetic and copies ran while one was open for 9% -> 11% of each run, Pallas kernels for 16% -> 16%
where the time goes in v4:
time: 353 us; the launch traced here: 351 us
  Pallas kernels  200 us (57%)
  waiting for transfers between devices  55.7 us (16%)
  starting transfers between devices  35.2 us (10%)
  other arithmetic  30.6 us (9%)
  local copies, waits for them, and re-layouts  25.5 us (7%)
  between operations  4.17 us (1%)
    pallas_call x1, Pallas kernels, run_atoms(): pl.pallas_call(functools.partial(atoms_kernel, ins, blocks, outs, owners)...  140 us
    pallas_call x4, Pallas kernels, run_edges_forward(): pl.pallas_call(functools.partial(edges_forward, count), grid_spec=pltpu.P...  33.7 us
    pallas_call x4, Pallas kernels, run_edges_backward(): pl.pallas_call(edges_backward, grid_spec=pltpu.PrefetchScalarGridSpec(num...  22.3 us
    all_to_all x1, waiting for transfers between devices, local(): meta = lax.all_to_all(meta, 'edge', 0, 0, tiled=True)  20.4 us
    ppermute x9, waiting for transfers between devices, ring_step(): return lax.ppermute(array, 'edge', moves)  15.9 us
    ppermute x9, starting transfers between devices, ring_step(): return lax.ppermute(array, 'edge', moves)  15.6 us
    ppermute x9, waiting for transfers between devices, pair_swap(): return lax.ppermute(array, 'edge', [(e, e ^ 1) for e in range(owners)])  13.7 us
    ppermute x9, starting transfers between devices, pair_swap(): return lax.ppermute(array, 'edge', [(e, e ^ 1) for e in range(owners)])  11.6 us
  transfers between devices with their start and end apart: 26, of which 15 were waited for; matrix products, arithmetic and copies ran while one was open for 11% of the time, Pallas kernels for 16%

profile of v4, /device:TPU:0, one launch (start us, length us, event | category | flops | bytes accessed | tf_op | source)
XLA Modules:
  0.0 351.2 jit_solution(6886576374794098757)
XLA Ops:
  0.7 3.0 collective-permute-start
  3.8 2.6 collective-permute-start.1
  13.5 2.4 collective-permute-done.rest_1_
  17.6 4.7 %all-to-all-start = ((bf16[8,224,256]{2,1,0:T(8,128)(2,1)}), bf16[8,224,256]{2,1,0:T(8,128)(2,1)S(1)}, u32[]{:S(2)}, u32[]{:S(2)}) async-start(bf16[8,224,256]{2,1,0:T(8,128)(2,1)} %pad_maximum_fusion.2), calls=%async_computation | async-start | bytes 1835008 | tf_op jit(solution)/shard_map/all_to_all | solution.py:717
  23.6 5.3 %fusion.12 = s32[8,16,128]{2,0,1:T(8,128)S(1)} fusion(s32[2,8,8,128]{3,2,1,0:T(8,128)S(1)} %copy.112, s32[]{:T(128)} %bitcast.8, s32[]{:T(128)} %bitcast.7, s32[]{:T(128)} %bitcast.6, s32[]{:T(128)} %bitcast.5, s32[]{:T(128)} %bitcast.4, s32[]{:T(128)} %bitcast.3, s32[]{:T(128)} %bitcast.2, s32[]{:T(128)} %bitcast.1), kind=kLoop, calls=%fused_computation.53 | loop fusion | flops 737280 | bytes 131104 | tf_op jit(solution)/shard_map/mul | solution.py:678
  32.8 2.4 collective-permute-start.3
  35.1 20.4 %all-to-all-done = bf16[8,224,256]{2,1,0:T(8,128)(2,1)S(1)} async-done(((bf16[8,224,256]{2,1,0:T(8,128)(2,1)}), bf16[8,224,256]{2,1,0:T(8,128)(2,1)S(1)}, u32[]{:S(2)}, u32[]{:S(2)}) %all-to-all-start) | async-done | bytes 917536 | tf_op jit(solution)/shard_map/all_to_all | solution.py:717
  61.4 8.4 %shard_map.509.rest_2_ = bf16[16384,896]{1,0:T(8,128)(2,1)} custom-call(s32[8]{0:T(128)} %fusion.17.order_ref, f32[8,256]{1,0:T(8,128)} %pad.14.small_ref, f32[8,2,128,8]{3,2,1,0:T(8,128)} %bitcast.128, f32[8,2,128,8]{3,2,1,0:T(8,128)} %bitcast.132, bf16[1024,256]{1,0:T(8,128)(2,1)} %bitcast.140, bf16[1024,256]{1,0:T(8,128)(2,1)} %copy-done.14), custom_call_target="tpu_custom_call" | custom-call | flops 2147483648 | bytes 8388608 | tf_op jit(solution)/shard_map/pallas_call | solution.py:403
  71.1 8.5 %shard_map.510.rest_2_ = bf16[16384,896]{1,0:T(8,128)(2,1)} custom-call(s32[8]{0:T(128)} %fusion.17.order_ref, f32[8,256]{1,0:T(8,128)} %pad.14.small_ref, f32[8,2,128,8]{3,2,1,0:T(8,128)} %bitcast.129, f32[8,2,128,8]{3,2,1,0:T(8,128)} %bitcast.133, bf16[1024,256]{1,0:T(8,128)(2,1)} %copy-done.13, ...), custom_call_target="tpu_custom_call", output_to_operand_aliasing={{}: (6, {})} | custom-call | flops 2147483648 | bytes 8388608 | tf_op jit(solution)/shard_map/pallas_call | solution.py:403
  79.6 2.3 collective-permute-done.4.rest_1_
  86.4 8.4 %shard_map.511.rest_2_ = bf16[16384,896]{1,0:T(8,128)(2,1)} custom-call(s32[8]{0:T(128)} %fusion.17.order_ref, f32[8,256]{1,0:T(8,128)} %pad.14.small_ref, f32[8,2,128,8]{3,2,1,0:T(8,128)} %bitcast.130, f32[8,2,128,8]{3,2,1,0:T(8,128)} %bitcast.134, bf16[1024,256]{1,0:T(8,128)(2,1)} %collective-permute-done.3.rest_0_, ...), custom_call_target="tpu_custom_call", output_to_operand_aliasing={{}: (6, {})} | custom-call | flops 2147483648 | bytes 8388608 | tf_op jit(solution)/shard_map/pallas_call | solution.py:403
  94.8 8.5 %shard_map.512.kept_ref = bf16[16384,896]{1,0:T(8,128)(2,1)} custom-call(s32[8]{0:T(128)} %fusion.17.order_ref, f32[8,256]{1,0:T(8,128)} %pad.14.small_ref, f32[8,2,128,8]{3,2,1,0:T(8,128)} %bitcast.131, f32[8,2,128,8]{3,2,1,0:T(8,128)} %bitcast.135, bf16[1024,256]{1,0:T(8,128)(2,1)} %copy-done.15, ...), custom_call_target="tpu_custom_call", output_to_operand_aliasing={{}: (6, {})} | custom-call | flops 2147483648 | bytes 8388608 | tf_op jit(solution)/shard_map/pallas_call | solution.py:403
  110.6 2.2 reshape.192.down_ref
  113.8 140.5 %shard_map.513 = (bf16[1024,256]{1,0:T(8,128)(2,1)}, f32[1024,128]{1,0:T(8,128)}, f32[1024,256]{1,0:T(8,128)}, f32[1024,256]{1,0:T(8,128)}, bf16[16384,256]{1,0:...) custom-call(s32[16384]{0:T(1024)} %bitcast.163, s32[1]{0:T(128)} %bitcast.13.core_ref, ...), custom_call_target="tpu_custom_call" | custom-call | flops 52076478464 | bytes 71827456 | tf_op jit(solution)/shard_map/pallas_call | solution.py:447
  254.4 5.6 %shard_map.514 = (bf16[1024,256]{1,0:T(8,128)(2,1)}, bf16[1024,256]{1,0:T(8,128)(2,1)}) custom-call(s32[8]{0:T(128)} %fusion.17.order_ref, bf16[16384,256]{1,0:T(8,128)(2,1)} %get-tuple-element.132.rows_ref, f32[8,1,2048]{2,1,0:T(1,128)} %copy-done.5), custom_call_target="tpu_custom_call" | custom-call | flops 2147483648 | bytes 3145728 | tf_op jit(solution)/shard_map/pallas_call | solution.py:507
  261.5 5.6 %shard_map.515 = (bf16[1024,256]{1,0:T(8,128)(2,1)}, bf16[1024,256]{1,0:T(8,128)(2,1)}) custom-call(s32[8]{0:T(128)} %fusion.17.order_ref, bf16[16384,256]{1,0:T(8,128)(2,1)} %get-tuple-element.132.rows_ref, f32[8,1,2048]{2,1,0:T(1,128)} %copy-done.5), custom_call_target="tpu_custom_call" | custom-call | flops 2147483648 | bytes 3145728 | tf_op jit(solution)/shard_map/pallas_call | solution.py:507
  268.3 2.1 convert_add_fusion
  273.4 5.5 %shard_map.516 = (bf16[1024,256]{1,0:T(8,128)(2,1)}, bf16[1024,256]{1,0:T(8,128)(2,1)}) custom-call(s32[8]{0:T(128)} %fusion.17.order_ref, bf16[16384,256]{1,0:T(8,128)(2,1)} %get-tuple-element.132.rows_ref, f32[8,1,2048]{2,1,0:T(1,128)} %copy-done.5, bf16[8,356,128]{2,1,0:T(8,128)(2,1)} %copy-done), custom_call_target="tpu_custom_call" | custom-call | flops 2147483648 | bytes 3145728 | tf_op jit(solution)/shard_map/pallas_call | solution.py:507
  282.2 5.6 %shard_map.517 = (bf16[1024,256]{1,0:T(8,128)(2,1)}, bf16[1024,256]{1,0:T(8,128)(2,1)}) custom-call(s32[8]{0:T(128)} %fusion.17.order_ref, bf16[16384,256]{1,0:T(8,128)(2,1)} %get-tuple-element.132.rows_ref, f32[8,1,2048]{2,1,0:T(1,128)} %copy-done.5, bf16[1024,256]{1,0:T(8,128)(2,1)} %copy-done.6), custom_call_target="tpu_custom_call" | custom-call | flops 2147483648 | bytes 3145728 | tf_op jit(solution)/shard_map/pallas_call | solution.py:507
  287.8 3.4 collective-permute-done.16
  294.9 2.1 add_convert_fusion.1
  300.7 4.7 %collective-permute-done.18 = bf16[4,356,128]{2,1,0:T(8,128)(2,1)} collective-permute-done((bf16[4,356,128]{2,1,0:T(8,128)(2,1)S(1)}, bf16[4,356,128]{2,1,0:T(8,128)(2,1)}, u32[]{:S(2)}, u32[]{:S(2)}) %collective-permute-start.18) | collective-permute-done | bytes 364576 | tf_op jit(solution)/shard_map/ppermute | solution.py:610
  306.5 4.2 %collective-permute-done.17 = bf16[1024,256]{1,0:T(8,128)(2,1)S(1)} collective-permute-done((bf16[1024,256]{1,0:T(8,128)(2,1)}, bf16[1024,256]{1,0:T(8,128)(2,1)S(1)}, u32[]{:S(2)}, u32[]{:S(2)}) %collective-permute-start.17) | collective-permute-done | bytes 524320 | tf_op jit(solution)/shard_map/ppermute | solution.py:605
  310.7 4.3 %collective-permute-done.13 = bf16[1024,256]{1,0:T(8,128)(2,1)} collective-permute-done((bf16[1024,256]{1,0:T(8,128)(2,1)}, bf16[1024,256]{1,0:T(8,128)(2,1)}, u32[]{:S(2)}, u32[]{:S(2)}) %collective-permute-start.13) | collective-permute-done | bytes 524320 | tf_op jit(solution)/shard_map/ppermute | solution.py:610
  318.8 2.8 collective-permute-done.20
  321.6 2.1 collective-permute-start.21
  324.4 2.4 collective-permute-done.21
  326.8 2.7 collective-permute-start.22
  337.9 2.3 collective-permute-done.23
  340.4 2.3 collective-permute-done.19
  344.2 2.5 fusion.3
  347.5 3.5 shard_map.518
  (186 shorter events, 64.0 us)
Async XLA Ops:
  0.7 15.2 %collective-permute-start = (bf16[1024,256]{1,0:T(8,128)(2,1)}, bf16[1024,256]{1,0:T(8,128)(2,1)S(1)}, u32[]{:S(2)}, u32[]{:S(2)}) collective-permute-start(bf16[1024,256]{1,0:T(8,128)(2,1)} %bitcast.138), channel_id=1, source_target_pairs={{0,4},{4,0},{8,12},{12,8},{16,20},{20,16},{24,28},{28,24},{1,5},{5... | collective-permute-start | bytes 1572872 | tf_op jit(solution)/shard_map/ppermute | solution.py:610
  3.8 13.8 %collective-permute-start.1 = (bf16[1024,256]{1,0:T(8,128)(2,1)}, bf16[1024,256]{1,0:T(8,128)(2,1)S(1)}, u32[]{:S(2)}, u32[]{:S(2)}) collective-permute-start(bf16[1024,256]{1,0:T(8,128)(2,1)} %bitcast.139), channel_id=1, source_target_pairs={{0,16},{4,20},{16,24},{20,28},{24,8},{28,12},{8,0},{12,4},{1,17},{... | collective-permute-start | bytes 1572872 | tf_op jit(solution)/shard_map/ppermute | solution.py:605
  15.9 40.4 %copy-start.14 = (bf16[1024,256]{1,0:T(8,128)(2,1)}, bf16[1024,256]{1,0:T(8,128)(2,1)S(1)}, u32[]{:S(2)}) copy-start(bf16[1024,256]{1,0:T(8,128)(2,1)S(1)} %collective-permute-done.rest_1_) | copy-start | bytes 1572868
  17.6 38.8 %copy-start.13 = (bf16[1024,256]{1,0:T(8,128)(2,1)}, bf16[1024,256]{1,0:T(8,128)(2,1)S(1)}, u32[]{:S(2)}) copy-start(bf16[1024,256]{1,0:T(8,128)(2,1)S(1)} %collective-permute-done.1.rest_0_) | copy-start | bytes 1572868
  17.6 37.9 %all-to-all-start = ((bf16[8,224,256]{2,1,0:T(8,128)(2,1)}), bf16[8,224,256]{2,1,0:T(8,128)(2,1)S(1)}, u32[]{:S(2)}, u32[]{:S(2)}) async-start(bf16[8,224,256]{2,1,0:T(8,128)(2,1)} %pad_maximum_fusion.2), calls=%async_computation | async-start | bytes 1835008 | tf_op jit(solution)/shard_map/all_to_all | solution.py:717
  30.7 39.1 %collective-permute-start.2 = (bf16[1024,256]{1,0:T(8,128)(2,1)S(1)}, bf16[1024,256]{1,0:T(8,128)(2,1)}, u32[]{:S(2)}, u32[]{:S(2)}) collective-permute-start(bf16[1024,256]{1,0:T(8,128)(2,1)S(1)} %collective-permute-done.1.rest_0_), channel_id=1, source_target_pairs={{0,4},{4,0},{8,12},{12,8},{16,20},{20,16},{24,28},{28,24},{1,5},{5... | collective-permute-start | bytes 1572872 | tf_op jit(solution)/shard_map/ppermute | solution.py:610
  32.8 37.1 %collective-permute-start.3 = (bf16[1024,256]{1,0:T(8,128)(2,1)S(1)}, bf16[1024,256]{1,0:T(8,128)(2,1)}, u32[]{:S(2)}, u32[]{:S(2)}) collective-permute-start(bf16[1024,256]{1,0:T(8,128)(2,1)S(1)} %collective-permute-done.1.rest_0_), channel_id=1, source_target_pairs={{0,16},{4,20},{16,24},{20,28},{24,8},{28,12},{8,0},{12,4},{1,17},{... | collective-permute-start | bytes 1572872 | tf_op jit(solution)/shard_map/ppermute | solution.py:605
  59.3 20.3 %collective-permute-start.6 = (bf16[8,176,256]{2,1,0:T(8,128)(2,1)S(1)}, bf16[8,176,256]{2,1,0:T(8,128)(2,1)S(1)}, u32[]{:S(2)}, u32[]{:S(2)}) collective-permute-start(bf16[8,176,256]{2,1,0:T(8,128)(2,1)S(1)} %slice.139), channel_id=1, source_target_pairs={{0,2},{1,3},{2,0},{3,1},{4,6},{5,7},{6,4},{7,5},{8,10},{9,11},{10,... | collective-permute-start | bytes 2162696 | tf_op jit(solution)/shard_map/ppermute | solution.py:535
  69.8 12.0 %collective-permute-start.4 = (bf16[1024,256]{1,0:T(8,128)(2,1)}, bf16[1024,256]{1,0:T(8,128)(2,1)S(1)}, u32[]{:S(2)}, u32[]{:S(2)}) collective-permute-start(bf16[1024,256]{1,0:T(8,128)(2,1)} %collective-permute-done.3.rest_0_), channel_id=1, source_target_pairs={{0,4},{4,0},{8,12},{12,8},{16,20},{20,16},{24,28},{28,24},{1,5},{5... | collective-permute-start | bytes 1572872 | tf_op jit(solution)/shard_map/ppermute | solution.py:610
  71.1 12.2 %collective-permute-start.5 = (bf16[1024,256]{1,0:T(8,128)(2,1)}, bf16[1024,256]{1,0:T(8,128)(2,1)S(1)}, u32[]{:S(2)}, u32[]{:S(2)}) collective-permute-start(bf16[1024,256]{1,0:T(8,128)(2,1)} %collective-permute-done.3.rest_0_), channel_id=1, source_target_pairs={{0,16},{4,20},{16,24},{20,28},{24,8},{28,12},{8,0},{12,4},{1,17},{... | collective-permute-start | bytes 1572872 | tf_op jit(solution)/shard_map/ppermute | solution.py:605
  83.3 11.5 %collective-permute-start.7 = (bf16[1024,256]{1,0:T(8,128)(2,1)S(1)}, bf16[1024,256]{1,0:T(8,128)(2,1)}, u32[]{:S(2)}, u32[]{:S(2)}) collective-permute-start(bf16[1024,256]{1,0:T(8,128)(2,1)S(1)} %collective-permute-done.5.rest_0_), channel_id=1, source_target_pairs={{0,4},{4,0},{8,12},{12,8},{16,20},{20,16},{24,28},{28,24},{1,5},{5... | collective-permute-start | bytes 1572872 | tf_op jit(solution)/shard_map/ppermute | solution.py:610
  83.8 19.5 %collective-permute-start.8 = (bf16[8,176,256]{2,1,0:T(8,128)(2,1)S(1)}, bf16[8,176,256]{2,1,0:T(8,128)(2,1)S(1)}, u32[]{:S(2)}, u32[]{:S(2)}) collective-permute-start(bf16[8,176,256]{2,1,0:T(8,128)(2,1)S(1)} %collective-permute-done.6), channel_id=1, source_target_pairs={{0,1},{1,0},{2,3},{3,2},{4,5},{5,4},{6,7},{7,6},{8,9},{9,8},{10,11... | collective-permute-start | bytes 2162696 | tf_op jit(solution)/shard_map/ppermute | solution.py:535
  83.8 20.3 %collective-permute-start.9 = (bf16[8,176,256]{2,1,0:T(8,128)(2,1)S(1)}, bf16[8,176,256]{2,1,0:T(8,128)(2,1)}, u32[]{:S(2)}, u32[]{:S(2)}) collective-permute-start(bf16[8,176,256]{2,1,0:T(8,128)(2,1)S(1)} %slice.139), channel_id=1, source_target_pairs={{0,1},{1,0},{2,3},{3,2},{4,5},{5,4},{6,7},{7,6},{8,9},{9,8},{10,11... | collective-permute-start | bytes 2162696 | tf_op jit(solution)/shard_map/ppermute | solution.py:535
  254.3 12.8 %collective-permute-start.11 = (bf16[5696,128]{1,0:T(8,128)(2,1)}, bf16[5696,128]{1,0:T(8,128)(2,1)S(1)}, u32[]{:S(2)}, u32[]{:S(2)}) collective-permute-start(bf16[5696,128]{1,0:T(8,128)(2,1)} %get-tuple-element.136), channel_id=1, source_target_pairs={{0,1},{1,0},{2,3},{3,2},{4,5},{5,4},{6,7},{7,6},{8,9},{9,8},{10,11... | collective-permute-start | bytes 4374536 | tf_op jit(solution)/shard_map/ppermute | solution.py:535
  260.0 18.9 %collective-permute-start.10 = (bf16[1024,256]{1,0:T(8,128)(2,1)}, bf16[1024,256]{1,0:T(8,128)(2,1)}, u32[]{:S(2)}, u32[]{:S(2)}) collective-permute-start(bf16[1024,256]{1,0:T(8,128)(2,1)} %get-tuple-element.134), channel_id=1, source_target_pairs={{0,4},{4,0},{8,12},{12,8},{16,20},{20,16},{24,28},{28,24},{1,5},{5... | collective-permute-start | bytes 1572872 | tf_op jit(solution)/shard_map/ppermute | solution.py:610
  272.4 18.8 %collective-permute-start.16 = (bf16[8,356,128]{2,0,1:T(8,128)(2,1)}, bf16[8,356,128]{2,0,1:T(8,128)(2,1)}, u32[]{:S(2)}, u32[]{:S(2)}) collective-permute-start(bf16[8,356,128]{2,0,1:T(8,128)(2,1)} %copy.108), channel_id=1, source_target_pairs={{0,2},{1,3},{2,0},{3,1},{4,6},{5,7},{6,4},{7,5},{8,10},{9,11},{10,... | collective-permute-start | bytes 2187272 | tf_op jit(solution)/shard_map/ppermute | solution.py:535
  272.9 22.0 %collective-permute-start.14 = (bf16[1024,256]{1,0:T(8,128)(2,1)}, bf16[1024,256]{1,0:T(8,128)(2,1)}, u32[]{:S(2)}, u32[]{:S(2)}) collective-permute-start(bf16[1024,256]{1,0:T(8,128)(2,1)} %get-tuple-element.144), channel_id=1, source_target_pairs={{0,4},{4,0},{8,12},{12,8},{16,20},{20,16},{24,28},{28,24},{1,5},{5... | collective-permute-start | bytes 1572872 | tf_op jit(solution)/shard_map/ppermute | solution.py:610
  280.2 14.7 %collective-permute-start.15 = (bf16[1024,256]{1,0:T(8,128)(2,1)S(1)}, bf16[1024,256]{1,0:T(8,128)(2,1)S(1)}, u32[]{:S(2)}, u32[]{:S(2)}) collective-permute-start(bf16[1024,256]{1,0:T(8,128)(2,1)S(1)} %add_convert_fusion.2.rest_0_), channel_id=1, source_target_pairs={{0,16},{4,20},{16,24},{20,28},{24,8},{28,12},{8,0},{12,4},{1,17},{... | collective-permute-start | bytes 1572872 | tf_op jit(solution)/shard_map/ppermute | solution.py:605
  293.7 21.3 %copy-start.18 = (bf16[1024,256]{1,0:T(8,128)(2,1)S(1)}, bf16[1024,256]{1,0:T(8,128)(2,1)}, u32[]{:S(2)}) copy-start(bf16[1024,256]{1,0:T(8,128)(2,1)} %get-tuple-element.139) | copy-start | bytes 1572868
  293.7 11.7 %collective-permute-start.18 = (bf16[4,356,128]{2,1,0:T(8,128)(2,1)S(1)}, bf16[4,356,128]{2,1,0:T(8,128)(2,1)}, u32[]{:S(2)}, u32[]{:S(2)}) collective-permute-start(bf16[4,356,128]{2,1,0:T(8,128)(2,1)S(1)} %fusion.5), channel_id=1, source_target_pairs={{0,4},{4,0},{8,12},{12,8},{16,20},{20,16},{24,28},{28,24},{1,5},{5... | collective-permute-start | bytes 1093640 | tf_op jit(solution)/shard_map/ppermute | solution.py:610
  297.0 13.7 %collective-permute-start.17 = (bf16[1024,256]{1,0:T(8,128)(2,1)}, bf16[1024,256]{1,0:T(8,128)(2,1)S(1)}, u32[]{:S(2)}, u32[]{:S(2)}) collective-permute-start(bf16[1024,256]{1,0:T(8,128)(2,1)} %add_convert_fusion.1), channel_id=1, source_target_pairs={{0,16},{4,20},{16,24},{20,28},{24,8},{28,12},{8,0},{12,4},{1,17},{... | collective-permute-start | bytes 1572872 | tf_op jit(solution)/shard_map/ppermute | solution.py:605
  298.6 16.4 %collective-permute-start.13 = (bf16[1024,256]{1,0:T(8,128)(2,1)}, bf16[1024,256]{1,0:T(8,128)(2,1)}, u32[]{:S(2)}, u32[]{:S(2)}) collective-permute-start(bf16[1024,256]{1,0:T(8,128)(2,1)} %get-tuple-element.143), channel_id=1, source_target_pairs={{0,4},{4,0},{8,12},{12,8},{16,20},{20,16},{24,28},{28,24},{1,5},{5... | collective-permute-start | bytes 1572872 | tf_op jit(solution)/shard_map/ppermute | solution.py:610
  317.0 25.6 %copy-start.1 = (bf16[1,1024,256]{2,1,0:T(8,128)(2,1)S(1)}, bf16[1,1024,256]{2,1,0:T(8,128)(2,1)}, u32[]{:S(2)}) copy-start(bf16[1,1024,256]{2,1,0:T(8,128)(2,1)} %param.30) | copy-start | bytes 1572868
  317.0 25.6 %copy-start.4 = (f32[1024,256]{1,0:T(8,128)S(1)}, f32[1024,256]{1,0:T(8,128)}, u32[]{:S(2)}) copy-start(f32[1024,256]{1,0:T(8,128)} %get-tuple-element.131) | copy-start | bytes 3145732
  317.1 25.6 %copy-start.7 = (bf16[1024,256]{1,0:T(8,128)(2,1)S(1)}, bf16[1024,256]{1,0:T(8,128)(2,1)}, u32[]{:S(2)}) copy-start(bf16[1024,256]{1,0:T(8,128)(2,1)} %get-tuple-element.141) | copy-start | bytes 1572868
  317.1 4.6 %collective-permute-start.20 = (bf16[356,128]{1,0:T(8,128)(2,1)S(1)}, bf16[356,128]{1,0:T(8,128)(2,1)S(1)}, u32[]{:S(2)}, u32[]{:S(2)}) collective-permute-start(bf16[356,128]{1,0:T(8,128)(2,1)S(1)} %dynamic-slice_bitcast_fusion), channel_id=1, source_target_pairs={{0,16},{4,20},{16,24},{20,28},{24,8},{28,12},{8,0},{12,4},{1,17},{... | collective-permute-start | bytes 273416 | tf_op jit(solution)/shard_map/ppermute | solution.py:605
  321.6 5.2 %collective-permute-start.21 = (bf16[356,128]{1,0:T(8,128)(2,1)S(1)}, bf16[356,128]{1,0:T(8,128)(2,1)S(1)}, u32[]{:S(2)}, u32[]{:S(2)}) collective-permute-start(bf16[356,128]{1,0:T(8,128)(2,1)S(1)} %fusion.6), channel_id=1, source_target_pairs={{0,16},{4,20},{16,24},{20,28},{24,8},{28,12},{8,0},{12,4},{1,17},{... | collective-permute-start | bytes 273416 | tf_op jit(solution)/shard_map/ppermute | solution.py:605
  326.8 6.9 %collective-permute-start.22 = (bf16[356,128]{1,0:T(8,128)(2,1)S(1)}, bf16[356,128]{1,0:T(8,128)(2,1)}, u32[]{:S(2)}, u32[]{:S(2)}) collective-permute-start(bf16[356,128]{1,0:T(8,128)(2,1)S(1)} %bitcast_add_fusion.3), channel_id=1, source_target_pairs={{0,16},{4,20},{16,24},{20,28},{24,8},{28,12},{8,0},{12,4},{1,17},{... | collective-permute-start | bytes 273416 | tf_op jit(solution)/shard_map/ppermute | solution.py:605
  330.8 11.8 %collective-permute-start.12 = (bf16[1024,256]{1,0:T(8,128)(2,1)}, bf16[1024,256]{1,0:T(8,128)(2,1)S(1)}, u32[]{:S(2)}, u32[]{:S(2)}) collective-permute-start(bf16[1024,256]{1,0:T(8,128)(2,1)} %get-tuple-element.142), channel_id=1, source_target_pairs={{0,4},{4,0},{8,12},{12,8},{16,20},{20,16},{24,28},{28,24},{1,5},{5... | collective-permute-start | bytes 1572872 | tf_op jit(solution)/shard_map/ppermute | solution.py:610
  332.2 10.5 %collective-permute-start.19 = (bf16[1024,256]{1,0:T(8,128)(2,1)}, bf16[1024,256]{1,0:T(8,128)(2,1)}, u32[]{:S(2)}, u32[]{:S(2)}) collective-permute-start(bf16[1024,256]{1,0:T(8,128)(2,1)} %add_convert_fusion), channel_id=1, source_target_pairs={{0,16},{4,20},{16,24},{20,28},{24,8},{28,12},{8,0},{12,4},{1,17},{... | collective-permute-start | bytes 1572872 | tf_op jit(solution)/shard_map/ppermute | solution.py:605
  334.6 5.6 %collective-permute-start.23 = (f32[356,128]{1,0:T(8,128)S(1)}, f32[356,128]{1,0:T(8,128)S(1)}, u32[]{:S(2)}, u32[]{:S(2)}) collective-permute-start(f32[356,128]{1,0:T(8,128)S(1)} %bitcast_add_fusion.1), channel_id=1, source_target_pairs={{0,2},{1,3},{2,0},{3,1},{4,6},{5,7},{6,4},{7,5},{8,10},{9,11},{10,... | collective-permute-start | bytes 546824 | tf_op jit(solution)/shard_map/ppermute | solution.py:535
  340.3 6.5 %collective-permute-start.24 = (f32[712,128]{1,0:T(8,128)S(1)}, f32[712,128]{1,0:T(8,128)S(1)}, u32[]{:S(2)}, u32[]{:S(2)}) collective-permute-start(f32[712,128]{1,0:T(8,128)S(1)} %pad_maximum_fusion.5.held_ref), channel_id=1, source_target_pairs={{0,1},{1,0},{2,3},{3,2},{4,5},{5,4},{6,7},{7,6},{8,9},{9,8},{10,11... | collective-permute-start | bytes 1093640 | tf_op jit(solution)/shard_map/ppermute | solution.py:535
  (26 other events, 175.6 us)
